TPU v7x, 256 devices: a whole 4x4x8 slice. The times are simulated.
256 devices in a mesh: leaf: 64 (over z, y, core), sub: 4 (over x).
Axes of the slice: x: 4, y: 4, z: 8, core: 2. Of those that a mesh axis runs over, the one named last changes fastest.
Arguments:
- probes: bfloat16 [32, 1024, 256], P(None, 'leaf', 'sub'), may hold values from -6 to 6
- near_blocks: bfloat16 [1024, 9, 256, 256], P('leaf', None, 'sub'), may hold values from -0.125 to 0.125
- leaf_cluster_basis: bfloat16 [1024, 64, 256], P('leaf', None, 'sub'), may hold values from -0.375 to 0.375
- transfer: bfloat16 [1024, 64, 64], P('leaf'), may hold values from -0.375 to 0.375
- couplings: bfloat16 [1024, 16, 64, 64], P('leaf'), may hold values from -0.1875 to 0.1875
- coarse_couplings: bfloat16 [256, 16, 64, 64], P('leaf'), may hold values from -0.1875 to 0.1875
- near_list: int32 [1024, 9], P('leaf'), may hold values from -1 to 1023, as said below
- distant_interaction_list: int32 [1024, 16], P('leaf'), may hold values from -1 to 1023, as said below
- coarse_list: int32 [256, 16], P('leaf'), may hold values from -1 to 255, as said below
Outputs:
- first_apply: bfloat16 [32, 1024, 256], P(None, 'leaf', 'sub')
- second_apply: bfloat16 [32, 1024, 256], P(None, 'leaf', 'sub')
Inputs may be any that keep to these rules, and one draw needn't show every extreme that they name: `near_list`: slot 0 of leaf i holds i; every other entry is -1 (an unused slot) or a leaf at most 4 positions from i in tree order. `distant_interaction_list`: entries are -1 (an unused slot) or leaves. The 16 leaves of one index of leaf name, over all their slots, at most 2 distinct leaves of any one index of leaf (itself included), and in every draw some index names exactly 2 leaves of another. `coarse_list`: entries are -1 (an unused slot) or parent clusters.
All inputs are finite; a program needn't handle non-finite values.
Results may differ from a plain program's by a relative error of at most 0.009.
Values may be sent and summed in bfloat16 or wider, within the bound.
No kernel may reach another device: no remote copies, remote signals or barrier semaphores. Data moves between devices by JAX's collectives and lax.ppermute only.
A program may use at most 64 MiB of HBM per device.

v0:
```python
import jax
import jax.numpy as jnp
from jax import lax
from jax.sharding import PartitionSpec as P

RANK = 64
BRANCH = 4
REACH = 4


def with_halo(block, sides, width):
    for axis, dim in sides:
        count = lax.axis_size(axis)
        forward = [(i, i + 1) for i in range(count - 1)]
        backward = [(target, source) for source, target in forward]
        low = lax.ppermute(
            lax.slice_in_dim(block, block.shape[dim] - width, None, axis=dim), axis, forward
        )
        high = lax.ppermute(lax.slice_in_dim(block, 0, width, axis=dim), axis, backward)
        block = jnp.concatenate([low, block, high], axis=dim)
    return block


def pick_mapped(shard_piece, global_rows, valid):
    row_count = shard_piece.shape[0]
    inside = valid & (global_rows >= 0) & (global_rows < row_count)
    chosen = jnp.take(shard_piece, jnp.clip(global_rows, 0, row_count - 1), axis=0)
    return jnp.where(inside[:, None], chosen, jnp.zeros_like(chosen))


def pick_rows(listing, shard_piece):
    flat_list = listing.reshape(-1)
    return pick_mapped(shard_piece, flat_list, flat_list >= 0)


def near_product(probe_vector_batch, near_blocks, near_list):
    probe_count, leaf_dev, shard_rows = probe_vector_batch.shape
    slot_count = near_list.shape[1]
    extended = with_halo(probe_vector_batch, (("leaf", 1),), REACH)
    first_leaf = lax.axis_index("leaf") * leaf_dev
    live_slots = near_list >= 0
    local_index = jnp.where(live_slots, near_list - first_leaf + REACH, 0).reshape(-1)
    shard_piece = lax.all_gather(extended, "sub", axis=2, tiled=True)
    row_count = shard_piece.shape[2]
    chosen = jnp.take(shard_piece, local_index, axis=1).reshape(
        probe_count, leaf_dev, slot_count, row_count
    )
    chosen = jnp.where(live_slots[None, :, :, None], chosen, jnp.zeros_like(chosen))
    return jnp.einsum("pikc,ikrc->pir", chosen, near_blocks, preferred_element_type=jnp.float32)


def local(
    probes,
    near_blocks,
    leaf_cluster_basis,
    transfer,
    couplings,
    coarse_couplings,
    near_list,
    distant_interaction_list,
    coarse_list,
):
    leaf_dev = probes.shape[1]
    parent_dev = leaf_dev // BRANCH
    transfer_wide = transfer.astype(jnp.float32)

    def apply_once(probe_vector_batch):
        probe_count = probe_vector_batch.shape[0]
        near_part = near_product(probe_vector_batch, near_blocks, near_list)
        leaf_level_sums = jnp.einsum(
            "dze,sde->dzs",
            leaf_cluster_basis,
            probe_vector_batch,
            preferred_element_type=jnp.float32,
        )
        parent_sums = jnp.einsum(
            "iab,iap->ibp", transfer_wide, leaf_level_sums, precision=lax.Precision.HIGHEST
        )
        parent_sums = parent_sums.reshape(parent_dev, BRANCH, RANK, probe_count).sum(axis=1)
        leaf_full, parent_full = (
            lax.psum_scatter(leaf_level_sums, "sub", scatter_dimension=1, tiled=True),
            lax.psum_scatter(parent_sums, "sub", scatter_dimension=1, tiled=True),
        )
        band_rows = RANK // lax.axis_size("sub")
        band_start = lax.axis_index("sub") * band_rows
        far_weights = lax.dynamic_slice_in_dim(couplings, band_start, band_rows, 3)
        coarse_weights = lax.dynamic_slice_in_dim(coarse_couplings, band_start, band_rows, 3)
        row_width = band_rows * probe_count
        leaf_coef = leaf_full.astype(jnp.bfloat16).reshape(leaf_dev, row_width)
        parent_coef = parent_full.astype(jnp.bfloat16).reshape(parent_dev, row_width)
        gathered_blocks = pick_rows(
            distant_interaction_list, lax.all_gather(leaf_coef, "leaf", axis=0, tiled=True)
        )
        coarse_fetched = pick_rows(
            coarse_list, lax.all_gather(parent_coef, "leaf", axis=0, tiled=True)
        )
        gathered_blocks = gathered_blocks.reshape(
            leaf_dev, distant_interaction_list.shape[1], band_rows, probe_count
        )
        coarse_fetched = coarse_fetched.reshape(
            parent_dev, coarse_list.shape[1], band_rows, probe_count
        )
        far_part = jnp.einsum(
            "ikab,ikbp->iap", far_weights, gathered_blocks, preferred_element_type=jnp.float32
        )
        coarse_part = jnp.einsum(
            "qkab,qkbp->qap", coarse_weights, coarse_fetched, preferred_element_type=jnp.float32
        )
        down_part = jnp.repeat(coarse_part, BRANCH, axis=0)
        far_field = far_part + jnp.einsum(
            "iab,ibp->iap", transfer_wide, down_part, precision=lax.Precision.HIGHEST
        )
        far_field = lax.psum(far_field, "sub")
        partial_field_output = far_field.astype(jnp.bfloat16)
        distant_block_rows = jnp.einsum(
            "zmc,zmb->bzc",
            leaf_cluster_basis,
            partial_field_output,
            preferred_element_type=jnp.float32,
        )
        return (near_part + distant_block_rows).astype(jnp.bfloat16)

    first_apply = apply_once(probes)
    second_apply = apply_once(first_apply)
    return (first_apply, second_apply)


def solution(mesh):
    return jax.shard_map(
        local,
        mesh=mesh,
        in_specs=(
            P(None, "leaf", "sub"),
            P("leaf", None, "sub", None),
            P("leaf", None, "sub"),
            P("leaf", None, None),
            P("leaf", None, None, None),
            P("leaf", None, None, None),
            P("leaf", None),
            P("leaf", None),
            P("leaf", None),
        ),
        out_specs=(P(None, "leaf", "sub"), P(None, "leaf", "sub")),
        check_vma=False,
    )
```

profile of v0, /device:TPU:96, one launch (start us, length us, event | category | flops | bytes accessed | tf_op | source)
XLA Modules:
  0.0 351.5 jit_solution(16656075611175461067)
XLA Ops:
  11.7 1.9 collective-permute-start
  13.6 5.8 %collective-permute-start.1 = (bf16[32,4,64]{0,1,2:T(4,128)(2,1)}, bf16[32,4,64]{0,1,2:T(4,128)(2,1)}, u32[]{:S(2)}, u32[]{:S(2)}) collective-permute-start(bf16[32,4,64]{0,1,2:T(4,128)(2,1)} %get-tuple-element.16), channel_id=1, source_target_pairs={{4,0},{8,4},{12,8},{16,12},{20,16},{24,20},{28,24},{32,28},{36,32}... | collective-permute-start | bytes 49160 | tf_op jit(solution)/shard_map/ppermute | solution.py:19
  20.6 18.4 %all-reduce = bf16[4,64,32]{2,0,1:T(4,128)(2,1)S(1)} all-reduce(f32[4,64,32]{2,0,1:T(4,128)S(1)} %copy.78), channel_id=3, replica_groups=mesh['leaf'=64,'sub'=4] {'sub'}, use_global_device_ids=true, to_apply=%region_2.5.clone | all-reduce | flops 8192 | bytes 49152
  41.3 45.4 %all-gather = bf16[64,4,512]{2,1,0:T(4,128)(2,1)S(1)} all-gather(bf16[1,4,512]{2,1,0:T(4,128)(2,1)S(1)} %reshape.179), channel_id=1, replica_groups=mesh['leaf'=64,'sub'=4] {'leaf'}, dimensions={0}, use_global_device_ids=true | all-gather | bytes 266240 | tf_op jit(solution)/shard_map/all_gather | solution.py:95
  94.6 17.4 %all_gather.18 = bf16[32,24,256]{0,1,2:T(8,128)(2,1)S(1)} all-gather(bf16[32,24,64]{0,1,2:T(8,128)(2,1)S(1)} %pad_maximum_fusion), channel_id=1, replica_groups=mesh['leaf'=64,'sub'=4] {'sub'}, dimensions={2}, use_global_device_ids=true | all-gather | bytes 491520 | tf_op jit(solution)/shard_map/all_gather | solution.py:43
  113.0 2.4 gather_fusion
  115.4 2.0 broadcast_select_fusion.1
  117.4 4.5 %fusion.20 = f32[16,32,64]{2,1,0:T(8,128)} fusion(bf16[16,9,64,256]{3,2,1,0:T(8,128)(2,1)} %param.16, bf16[32,16,9,256]{3,0,2,1:T(8,128)(2,1)S(1)} %bitcast.71, pred[16,9]{1,0:T(8,128)(4,1)S(1)} %copy-done.17), kind=kOutput, calls=%fused_computation.28 | convolution fusion | flops 152174592 | bytes 7209104 | tf_op jit(solution)/shard_map/pikc,ikrc->pir/dot_general | solution.py:49
  121.9 40.0 %all-gather.5.cloned.1.call-done = bf16[1024,512]{1,0:T(8,128)(2,1)} async-done(((bf16[16,512]{1,0:T(8,128)(2,1)}), bf16[1024,512]{1,0:T(8,128)(2,1)}) %all-gather.5.cloned.1.call-update) | async-done | bytes 1048592 | tf_op jit(solution)/shard_map/all_gather | solution.py:92
  161.8 2.6 gather_fusion.1
  165.2 4.2 %fusion.15 = f32[16,64,32]{1,2,0:T(8,128)S(1)} fusion(bf16[16,16,16,32]{3,2,1,0:T(8,128)(2,1)S(1)} %reshape.113, bf16[16,16,64,64]{3,2,1,0:T(8,128)(2,1)} %param.19, s32[]{:T(128)S(6)} %select_n.55), kind=kOutput, calls=%fused_computation.21 | convolution fusion | flops 16777216 | bytes 2490372 | tf_op jit(solution)/shard_map/ikab,ikbp->iap/dot_general | solution.py:103
  170.0 20.4 %all-reduce.4 = bf16[16,64,32]{1,2,0:T(8,128)(2,1)S(1)} all-reduce(f32[16,64,32]{1,2,0:T(8,128)S(1)} %fusion.19), channel_id=1, replica_groups=mesh['leaf'=64,'sub'=4] {'sub'}, use_global_device_ids=true, to_apply=%region_3.7 | all-reduce | flops 32768 | bytes 196608 | tf_op jit(solution)/shard_map/psum | solution.py:113
  193.0 21.6 %reduce-scatter.5.cloned.1.call-done = f32[16,16,32]{2,0,1:T(8,128)} async-done(((f32[16,64,32]{2,0,1:T(8,128)}), f32[16,16,32]{2,0,1:T(8,128)}) %reduce-scatter.5.cloned.1.call-update) | async-done | bytes 32784 | tf_op jit(solution)/shard_map/reduce_scatter | solution.py:81
  216.2 1.9 collective-permute-start.2
  218.2 5.8 %collective-permute-start.3 = (bf16[32,4,64]{2,0,1:T(8,128)(2,1)S(1)}, bf16[32,4,64]{2,0,1:T(8,128)(2,1)S(1)}, u32[]{:S(2)}, u32[]{:S(2)}) collective-permute-start(bf16[32,4,64]{2,0,1:T(8,128)(2,1)S(1)} %get-tuple-element.18), channel_id=1, source_target_pairs={{4,0},{8,4},{12,8},{16,12},{20,16},{24,20},{28,24},{32,28},{36,32}... | collective-permute-start | bytes 49160 | tf_op jit(solution)/shard_map/ppermute | solution.py:19
  224.4 16.3 %all-reduce.1 = bf16[4,64,32]{2,0,1:T(4,128)(2,1)S(1)} all-reduce(f32[4,64,32]{2,0,1:T(4,128)S(1)} %copy.85), channel_id=5, replica_groups=mesh['leaf'=64,'sub'=4] {'sub'}, use_global_device_ids=true, to_apply=%region_6.10.clone | all-reduce | flops 8192 | bytes 49152
  240.8 45.0 %all-gather.1 = bf16[64,4,512]{2,1,0:T(4,128)(2,1)S(1)} all-gather(bf16[1,4,512]{2,1,0:T(4,128)(2,1)S(1)} %reshape.181), channel_id=1, replica_groups=mesh['leaf'=64,'sub'=4] {'leaf'}, dimensions={0}, use_global_device_ids=true | all-gather | bytes 266240 | tf_op jit(solution)/shard_map/all_gather | solution.py:95
  288.9 17.5 %all_gather.21 = bf16[32,24,256]{0,1,2:T(8,128)(2,1)S(1)} all-gather(bf16[32,24,64]{0,1,2:T(8,128)(2,1)S(1)} %copy.81), channel_id=1, replica_groups=mesh['leaf'=64,'sub'=4] {'sub'}, dimensions={2}, use_global_device_ids=true | all-gather | bytes 491520 | tf_op jit(solution)/shard_map/all_gather | solution.py:43
  307.4 2.4 gather_fusion.3
  309.8 2.0 broadcast_select_fusion
  311.8 4.5 %fusion.23 = f32[16,32,64]{2,1,0:T(8,128)} fusion(bf16[16,9,64,256]{3,2,1,0:T(8,128)(2,1)} %param.16, bf16[32,16,9,256]{3,0,2,1:T(8,128)(2,1)S(1)} %bitcast.70, pred[16,9]{1,0:T(8,128)(4,1)S(1)} %copy-done.18), kind=kOutput, calls=%fused_computation.29 | convolution fusion | flops 152174592 | bytes 7209104 | tf_op jit(solution)/shard_map/pikc,ikrc->pir/dot_general | solution.py:49
  316.2 2.6 gather_fusion.4
  319.6 4.2 %fusion.12 = f32[16,64,32]{1,2,0:T(8,128)S(1)} fusion(bf16[16,16,16,32]{3,2,1,0:T(8,128)(2,1)S(1)} %reshape.120, bf16[16,16,64,64]{3,2,1,0:T(8,128)(2,1)} %param.19, s32[]{:T(128)S(6)} %select_n.55), kind=kOutput, calls=%fused_computation.20 | convolution fusion | flops 16777216 | bytes 2490372 | tf_op jit(solution)/shard_map/ikab,ikbp->iap/dot_general | solution.py:103
  324.4 18.8 %all-reduce.5 = bf16[16,64,32]{1,2,0:T(8,128)(2,1)S(1)} all-reduce(f32[16,64,32]{1,2,0:T(8,128)S(1)} %fusion.18), channel_id=1, replica_groups=mesh['leaf'=64,'sub'=4] {'sub'}, use_global_device_ids=true, to_apply=%region_7.11 | all-reduce | flops 32768 | bytes 196608 | tf_op jit(solution)/shard_map/psum | solution.py:113
  (131 shorter events, 29.1 us)
Async XLA Ops:
  7.2 33.8 %copy-start = (bf16[4,16,64,64]{3,2,1,0:T(8,128)(2,1)S(1)}, bf16[4,16,64,64]{3,2,1,0:T(8,128)(2,1)}, u32[]{:S(2)}) copy-start(bf16[4,16,64,64]{3,2,1,0:T(8,128)(2,1)} %param.20) | copy-start | bytes 1572868
  7.2 31.8 %copy-start.21 = (u32[256]{0:T(256)S(1)}, u32[256]{0:T(256)}, u32[]{:S(2)}) copy-start(u32[256]{0:T(256)} %constant.75) | copy-start | bytes 3076
  7.2 12.2 %copy-start.9 = (s32[4,16]{1,0:T(4,128)S(1)}, s32[4,16]{1,0:T(4,128)}, u32[]{:S(2)}) copy-start(s32[4,16]{1,0:T(4,128)} %param.23) | copy-start | bytes 772
  7.2 12.3 %copy-start.6 = (s32[16,16]{1,0:T(8,128)S(1)}, s32[16,16]{1,0:T(8,128)}, u32[]{:S(2)}) copy-start(s32[16,16]{1,0:T(8,128)} %param.22) | copy-start | bytes 3076
  7.2 12.9 %copy-start.2 = (bf16[16,64,64]{2,1,0:T(8,128)(2,1)S(1)}, bf16[16,64,64]{2,1,0:T(8,128)(2,1)}, u32[]{:S(2)}) copy-start(bf16[16,64,64]{2,1,0:T(8,128)(2,1)} %param.18) | copy-start | bytes 393220
  7.2 33.1 %copy-start.7 = (s32[16,9]{1,0:T(8,128)S(1)}, s32[16,9]{1,0:T(8,128)}, u32[]{:S(2)}) copy-start(s32[16,9]{1,0:T(8,128)} %param.21) | copy-start | bytes 1732
  7.2 80.5 %reduce-scatter.3.cloned.1.call-start = ((), (), s32[]{:S(2)}) async-start(), calls=%async_computation.2 | async-start | bytes 655360 | tf_op jit(solution)/shard_map/reduce_scatter | solution.py:81
  9.7 152.1 %all-gather.5.cloned.1.call-start = ((), (), s32[]{:S(2)}) async-start(), calls=%async_computation.3 | async-start | bytes 1064960 | tf_op jit(solution)/shard_map/all_gather | solution.py:92
  11.7 81.2 %collective-permute-start = (bf16[32,4,64]{0,1,2:T(4,128)(2,1)}, bf16[32,4,64]{0,1,2:T(4,128)(2,1)S(1)}, u32[]{:S(2)}, u32[]{:S(2)}) collective-permute-start(bf16[32,4,64]{0,1,2:T(4,128)(2,1)} %get-tuple-element.15), channel_id=1, source_target_pairs={{0,4},{4,8},{8,12},{12,16},{16,20},{20,24},{24,28},{28,32},{32,36}... | collective-permute-start | bytes 49160 | tf_op jit(solution)/shard_map/ppermute | solution.py:16
  13.6 80.0 %collective-permute-start.1 = (bf16[32,4,64]{0,1,2:T(4,128)(2,1)}, bf16[32,4,64]{0,1,2:T(4,128)(2,1)}, u32[]{:S(2)}, u32[]{:S(2)}) collective-permute-start(bf16[32,4,64]{0,1,2:T(4,128)(2,1)} %get-tuple-element.16), channel_id=1, source_target_pairs={{4,0},{8,4},{12,8},{16,12},{20,16},{24,20},{28,24},{32,28},{36,32}... | collective-permute-start | bytes 49160 | tf_op jit(solution)/shard_map/ppermute | solution.py:19
  19.5 68.2 %copy-start.12 = (pred[64]{0:T(512)(128)(4,1)}, pred[64]{0:T(512)(128)(4,1)S(1)}, u32[]{:S(2)}) copy-start(pred[64]{0:T(512)(128)(4,1)S(1)} %compare_and_fusion.1) | copy-start | bytes 196
  40.3 46.6 %copy-start.10 = (s32[1024]{0:T(1024)}, s32[1024]{0:T(1024)S(1)}, u32[]{:S(2)}) copy-start(s32[1024]{0:T(1024)S(1)} %pad_clamp_fusion) | copy-start | bytes 12292
  40.4 49.1 %copy-start.11 = (s32[144]{0:T(256)}, s32[144]{0:T(256)S(1)}, u32[]{:S(2)}) copy-start(s32[144]{0:T(256)S(1)} %reshape.110) | copy-start | bytes 1732
  89.4 125.2 %reduce-scatter.5.cloned.1.call-start = ((), (), s32[]{:S(2)}) async-start(), calls=%async_computation.4 | async-start | bytes 655360 | tf_op jit(solution)/shard_map/reduce_scatter | solution.py:81
  117.4 44.5 %copy-start.8 = (s32[1024]{0:T(1024)S(1)}, s32[1024]{0:T(1024)}, u32[]{:S(2)}) copy-start(s32[1024]{0:T(1024)} %pad_clamp_fusion.1) | copy-start | bytes 12292
  121.9 42.6 %copy-start.19 = (pred[256]{0:T(512)(128)(4,1)S(1)}, pred[256]{0:T(512)(128)(4,1)}, u32[]{:S(2)}) copy-start(pred[256]{0:T(512)(128)(4,1)} %compare_and_fusion.2) | copy-start | bytes 772
  165.2 4.3 %copy-start.4 = (f32[4,64,32]{1,2,0:T(8,128)S(1)}, f32[4,64,32]{1,2,0:T(8,128)}, u32[]{:S(2)}) copy-start(f32[4,64,32]{1,2,0:T(8,128)} %convolution_bitcast_fusion.3) | copy-start | bytes 98308
  165.2 25.3 %copy-start.1 = (bf16[16,64,64]{2,1,0:T(8,128)(2,1)S(1)}, bf16[16,64,64]{2,1,0:T(8,128)(2,1)}, u32[]{:S(2)}) copy-start(bf16[16,64,64]{2,1,0:T(8,128)(2,1)} %param.17) | copy-start | bytes 393220
  191.6 95.1 %copy-start.13 = (pred[64]{0:T(512)(128)(4,1)S(1)}, pred[64]{0:T(512)(128)(4,1)}, u32[]{:S(2)}) copy-start(pred[64]{0:T(512)(128)(4,1)} %copy-done.12) | copy-start | bytes 196
  191.6 95.1 %copy-start.16 = (pred[64]{0:T(512)(128)(4,1)S(1)}, pred[64]{0:T(512)(128)(4,1)}, u32[]{:S(2)}) copy-start(pred[64]{0:T(512)(128)(4,1)} %copy-done.15) | copy-start | bytes 196
  192.9 123.3 %all-gather.7.cloned.1.call-start = ((), (), s32[]{:S(2)}) async-start(), calls=%async_computation.5 | async-start | bytes 1064960 | tf_op jit(solution)/shard_map/all_gather | solution.py:92
  216.2 72.3 %collective-permute-start.2 = (bf16[32,4,64]{2,0,1:T(8,128)(2,1)S(1)}, bf16[32,4,64]{2,0,1:T(8,128)(2,1)S(1)}, u32[]{:S(2)}, u32[]{:S(2)}) collective-permute-start(bf16[32,4,64]{2,0,1:T(8,128)(2,1)S(1)} %get-tuple-element.17), channel_id=1, source_target_pairs={{0,4},{4,8},{8,12},{12,16},{16,20},{20,24},{24,28},{28,32},{32,36}... | collective-permute-start | bytes 49160 | tf_op jit(solution)/shard_map/ppermute | solution.py:16
  218.2 70.4 %collective-permute-start.3 = (bf16[32,4,64]{2,0,1:T(8,128)(2,1)S(1)}, bf16[32,4,64]{2,0,1:T(8,128)(2,1)S(1)}, u32[]{:S(2)}, u32[]{:S(2)}) collective-permute-start(bf16[32,4,64]{2,0,1:T(8,128)(2,1)S(1)} %get-tuple-element.18), channel_id=1, source_target_pairs={{4,0},{8,4},{12,8},{16,12},{20,16},{24,20},{28,24},{32,28},{36,32}... | collective-permute-start | bytes 49160 | tf_op jit(solution)/shard_map/ppermute | solution.py:19
  319.5 4.2 %copy-start.3 = (f32[4,64,32]{1,2,0:T(8,128)S(1)}, f32[4,64,32]{1,2,0:T(8,128)}, u32[]{:S(2)}) copy-start(f32[4,64,32]{1,2,0:T(8,128)} %convolution_bitcast_fusion.2) | copy-start | bytes 98308
  (6 other events, 12.2 us)
Sparse Core Ops, SparseCore 0:
  10.6 26.5 reduce-scatter.2
  89.5 72.2 all-gather.4
  193.1 21.4 reduce-scatter.4
  217.2 74.8 all-gather.6
where the time goes:
time: 353 us; the launch traced here: 352 us
  blocking collectives  199 us (56%)
  waiting for transfers between devices  61.6 us (17%)
  local copies, waits for them, and re-layouts  25.2 us (7%)
  matrix products  24.6 us (7%)
  starting transfers between devices  15.5 us (4%)
  between operations  15 us (4%)
  other arithmetic  10.3 us (3%)
    all_gather x2, blocking collectives, apply_once(): lax.all_gather(parent_coef, 'leaf', axis=0, tiled=True)  90.4 us
    all_gather x2, waiting for transfers between devices, apply_once(): lax.all_gather(leaf_coef, 'leaf', axis=0, tiled=True)  40 us
    psum x2, blocking collectives, apply_once(): far_field = lax.psum(far_field, 'sub')  39.2 us
    all_gather x2, blocking collectives, near_product(): shard_piece = lax.all_gather(extended, 'sub', axis=2, tiled=True)  35 us
    unnamed x2, blocking collectives  34.7 us
    reduce_scatter x2, waiting for transfers between devices, apply_once(): lax.psum_scatter(leaf_level_sums, 'sub', scatter_dimension=1, tiled=True)  21.6 us
    ppermute x2, starting transfers between devices, with_halo(): lax.ppermute(lax.slice_in_dim(block, 0, width, axis=dim), axis, backward)  11.5 us
    dot_general x2, matrix products, near_product(): jnp.einsum('pikc,ikrc->pir', chosen, near_blocks, preferred_element_type=...  8.91 us
  transfers between devices with their start and end apart: 8, of which 2 were waited for; matrix products, arithmetic and copies ran while one was open for 10% of the time, Pallas kernels for 0%

commit v1 on v0

v1 whole, which is shorter than its diff:
```python
import jax
import jax.numpy as jnp
from jax import lax
from jax.sharding import PartitionSpec as P

RANK = 64
BRANCH = 4
REACH = 4
CAP = 2


def from_sub(x):
    count = lax.axis_size("sub")
    return [
        lax.ppermute(x, "sub", [((i + k) % count, i) for i in range(count)]) for k in range(1, count)
    ]


def gather_sub(x):
    pieces = jnp.stack([x] + from_sub(x))
    return jnp.roll(pieces, lax.axis_index("sub"), axis=0)


def halo(x, width):
    count = lax.axis_size("leaf")
    low = lax.ppermute(x[-width:], "leaf", [(i, i + 1) for i in range(count - 1)])
    high = lax.ppermute(x[:width], "leaf", [(i + 1, i) for i in range(count - 1)])
    return jnp.concatenate([low, x, high], axis=0)


def local(
    probes,
    near_blocks,
    leaf_cluster_basis,
    transfer,
    couplings,
    coarse_couplings,
    near_list,
    distant_interaction_list,
    coarse_list,
):
    probe_count, leaf_dev, rows = probes.shape
    parent_dev = leaf_dev // BRANCH
    groups = lax.axis_size("leaf")
    subs = lax.axis_size("sub")
    sub = lax.axis_index("sub")
    first_leaf = lax.axis_index("leaf") * leaf_dev
    band = RANK // subs
    width = band * probe_count
    bf16, f32 = jnp.bfloat16, jnp.float32

    named = distant_interaction_list.reshape(-1)
    owner = jnp.where(named >= 0, named // leaf_dev, -1)
    place = named % leaf_dev
    of_peer = owner[None, :] == jnp.arange(groups)[:, None]
    least = jnp.min(jnp.where(of_peer, place[None, :], leaf_dev), axis=1)
    greatest = jnp.max(jnp.where(of_peer, place[None, :], -1), axis=1)
    asked = lax.all_to_all(jnp.stack([least, greatest], axis=1), "leaf", 0, 0, tiled=True)
    send_leaf = (asked.reshape(-1)[:, None] == jnp.arange(leaf_dev)[None, :]).astype(bf16)
    is_least = jnp.where(of_peer, place[None, :] == least[:, None], False)
    is_greatest = of_peer & ~is_least
    take_leaf = jnp.stack([is_least, is_greatest], axis=1).reshape(CAP * groups, -1).T.astype(bf16)
    take_parent = (
        coarse_list.reshape(-1)[:, None] == jnp.arange(groups * parent_dev)[None, :]
    ).astype(bf16)

    far_weights = lax.dynamic_slice_in_dim(couplings, sub * band, band, 3)
    coarse_weights = lax.dynamic_slice_in_dim(coarse_couplings, sub * band, band, 3)
    near_index = jnp.where(near_list >= 0, near_list - first_leaf + REACH, -1)
    near_take = (
        near_index.reshape(-1)[:, None] == jnp.arange(leaf_dev + 2 * REACH)[None, :]
    ).astype(bf16)

    basis_parts = gather_sub(leaf_cluster_basis.reshape(-1, 128))
    basis = basis_parts.reshape(subs, leaf_dev, RANK, rows).transpose(1, 2, 0, 3)
    basis = basis.reshape(leaf_dev, RANK, subs * rows)

    def whole(x):
        parts = gather_sub(x.reshape(-1, 128)).reshape(subs, leaf_dev, probe_count, rows)
        return parts.transpose(1, 2, 0, 3).reshape(leaf_dev, probe_count, subs * rows)

    def near(x):
        extended = halo(x.reshape(leaf_dev, -1), REACH)
        chosen = jnp.dot(near_take, extended, preferred_element_type=f32).astype(bf16)
        chosen = chosen.reshape(leaf_dev, near_list.shape[1], probe_count, subs * rows)
        return jnp.einsum("ikpc,ikrc->ipr", chosen, near_blocks, preferred_element_type=f32)

    def far(x):
        leaf_sums = jnp.einsum("iac,ipc->iap", basis, x, preferred_element_type=f32)
        leaf_coef = leaf_sums.astype(bf16)
        parent_sums = jnp.einsum("iab,iap->ibp", transfer, leaf_coef, preferred_element_type=f32)
        parent_coef = parent_sums.reshape(parent_dev, BRANCH, RANK, probe_count).sum(1).astype(bf16)
        leaf_band = lax.dynamic_slice_in_dim(leaf_coef, sub * band, band, 1).reshape(leaf_dev, width)
        parent_band = lax.dynamic_slice_in_dim(parent_coef, sub * band, band, 1)
        parent_band = parent_band.reshape(1, parent_dev, width)
        leaf_out = jnp.dot(send_leaf, leaf_band, preferred_element_type=f32).astype(bf16)
        out = jnp.concatenate(
            [
                leaf_out.reshape(groups, CAP, width),
                jnp.broadcast_to(parent_band, (groups, parent_dev, width)),
            ],
            axis=1,
        )
        got = lax.all_to_all(out, "leaf", 0, 0, tiled=True)
        got_leaf = got[:, :CAP].reshape(groups * CAP, width)
        got_parent = got[:, CAP:].reshape(groups * parent_dev, width)
        picked = jnp.dot(take_leaf, got_leaf, preferred_element_type=f32).astype(bf16)
        picked = picked.reshape(leaf_dev, -1, band, probe_count)
        coarse_picked = jnp.dot(take_parent, got_parent, preferred_element_type=f32).astype(bf16)
        coarse_picked = coarse_picked.reshape(parent_dev, -1, band, probe_count)
        far_part = jnp.einsum("ikab,ikbp->iap", far_weights, picked, preferred_element_type=f32)
        coarse_part = jnp.einsum(
            "qkab,qkbp->qap", coarse_weights, coarse_picked, preferred_element_type=f32
        )
        down = jnp.repeat(coarse_part.astype(bf16), BRANCH, axis=0)
        far_part = far_part + jnp.einsum("iab,ibp->iap", transfer, down, preferred_element_type=f32)
        flat = far_part.reshape(leaf_dev, -1)
        others = from_sub(flat.astype(bf16))
        total = flat + sum(piece.astype(f32) for piece in others)
        return total.astype(bf16).reshape(leaf_dev, RANK, probe_count)

    def spread(field, some_basis):
        return jnp.einsum("iar,iap->ipr", some_basis, field, preferred_element_type=f32)

    x0 = whole(probes.transpose(1, 0, 2))
    near1 = near(x0)
    near1_whole = whole(near1.astype(bf16))
    field1 = far(x0)
    first = (near1 + spread(field1, leaf_cluster_basis)).astype(bf16)
    x1 = (near1_whole.astype(f32) + spread(field1, basis)).astype(bf16)
    near2 = near(x1)
    field2 = far(x1)
    second = (near2 + spread(field2, leaf_cluster_basis)).astype(bf16)
    return (first.transpose(1, 0, 2), second.transpose(1, 0, 2))


def solution(mesh):
    return jax.shard_map(
        local,
        mesh=mesh,
        in_specs=(
            P(None, "leaf", "sub"),
            P("leaf", None, "sub", None),
            P("leaf", None, "sub"),
            P("leaf", None, None),
            P("leaf", None, None, None),
            P("leaf", None, None, None),
            P("leaf", None),
            P("leaf", None),
            P("leaf", None),
        ),
        out_specs=(P(None, "leaf", "sub"), P(None, "leaf", "sub")),
        check_vma=False,
    )
```

time: 353 us -> 179 us (0.51)
  the two profiles are of different devices: /device:TPU:96 before, /device:TPU:1 now
where the time goes in v1:
time: 179 us; the launch traced here: 178 us
  starting transfers between devices  67.5 us (38%)
  local copies, waits for them, and re-layouts  63.3 us (35%)
  matrix products  27.7 us (15%)
  waiting for transfers between devices  10.8 us (6%)
  other arithmetic  7.12 us (4%)
    all_to_all x2, starting transfers between devices, far(): got = lax.all_to_all(out, 'leaf', 0, 0, tiled=True)  22.9 us
    ppermute x15, starting transfers between devices, from_sub(): lax.ppermute(x, 'sub', [((i + k) % count, i) for i in range(count)])  19.3 us
    unnamed x45, local copies, waits for them, and re-layouts  14.3 us
    all_to_all x1, starting transfers between devices, local(): lax.all_to_all(jnp.stack([least, greatest], axis=1), 'leaf', 0, 0, tiled=...  13.7 us
    all_to_all x2, waiting for transfers between devices, far(): got = lax.all_to_all(out, 'leaf', 0, 0, tiled=True)  9.59 us
    dot_general x2, matrix products, near(): jnp.einsum('ikpc,ikrc->ipr', chosen, near_blocks, preferred_element_type=...  8.8 us
    ppermute x2, starting transfers between devices, halo(): lax.ppermute(x[-width:], 'leaf', [(i, i + 1) for i in range(count - 1)])  6.53 us
    dynamic_slice x1, local copies, waits for them, and re-layouts, local(): far_weights = lax.dynamic_slice_in_dim(couplings, sub * band, band, 3)  5.48 us
  transfers between devices with their start and end apart: 22, of which 3 were waited for; matrix products, arithmetic and copies ran while one was open for 40% of the time, Pallas kernels for 0%

profile of v1, /device:TPU:1, one launch (start us, length us, event | category | flops | bytes accessed | tf_op | source)
XLA Modules:
  0.0 177.7 jit_solution(12821695968752008650)
XLA Ops:
  1.8 3.4 %collective-permute-start = (bf16[256,128]{1,0:T(8,128)(2,1)S(1)}, bf16[256,128]{1,0:T(8,128)(2,1)S(1)}, u32[]{:S(2)}, u32[]{:S(2)}) collective-permute-start(bf16[256,128]{1,0:T(8,128)(2,1)S(1)} %reshape.298), channel_id=1, source_target_pairs={{1,0},{2,1},{3,2},{0,3},{5,4},{6,5},{7,6},{4,7},{9,8},{10,9},{11,1... | collective-permute-start | bytes 196616 | tf_op jit(solution)/shard_map/ppermute | solution.py:15
  7.4 2.1 %collective-permute-start.5 = (bf16[512,128]{1,0:T(8,128)(2,1)S(1)}, bf16[512,128]{1,0:T(8,128)(2,1)S(1)}, u32[]{:S(2)}, u32[]{:S(2)}) collective-permute-start(bf16[512,128]{1,0:T(8,128)(2,1)S(1)} %reshape.302), channel_id=1, source_target_pairs={{1,0},{2,1},{3,2},{0,3},{5,4},{6,5},{7,6},{4,7},{9,8},{10,9},{11,1... | collective-permute-start | bytes 393224 | tf_op jit(solution)/shard_map/ppermute | solution.py:15
  12.5 13.7 %all-to-all-start = ((s32[64,1,2]{2,1,0:T(1,128)}), s32[64,1,2]{2,1,0:T(1,128)S(1)}, u32[]{:S(2)}, u32[]{:S(2)}) async-start(s32[64,1,2]{2,1,0:T(1,128)} %copy.136), calls=%async_computation | async-start | bytes 65536 | tf_op jit(solution)/shard_map/all_to_all | solution.py:58
  28.2 5.5 %constant_dynamic-slice_fusion.4 = bf16[16,16,64,16]{3,2,1,0:T(8,128)(2,1)} fusion(bf16[16,16,64,64]{3,2,1,0:T(8,128)(2,1)} %param.15, s32[]{:T(128)S(6)} %select_n.82), kind=kLoop, calls=%fused_computation.119 | loop fusion | bytes 1048580 | tf_op jit(solution)/shard_map/dynamic_slice | solution.py:67
  38.9 2.6 %collective-permute-start.4 = (bf16[4,8192]{1,0:T(4,128)(2,1)}, bf16[4,8192]{1,0:T(4,128)(2,1)}, u32[]{:S(2)}, u32[]{:S(2)}) collective-permute-start(bf16[4,8192]{1,0:T(4,128)(2,1)} %slice.39), channel_id=1, source_target_pairs={{4,0},{8,4},{12,8},{16,12},{20,16},{24,20},{28,24},{32,28},{36,32}... | collective-permute-start | bytes 196616 | tf_op jit(solution)/shard_map/ppermute | solution.py:27
  42.4 3.1 %collective-permute-start.3 = (bf16[4,8192]{1,0:T(4,128)(2,1)}, bf16[4,8192]{1,0:T(4,128)(2,1)}, u32[]{:S(2)}, u32[]{:S(2)}) collective-permute-start(bf16[4,8192]{1,0:T(4,128)(2,1)} %slice.37), channel_id=1, source_target_pairs={{0,4},{4,8},{8,12},{12,16},{16,20},{20,24},{24,28},{28,32},{32,36}... | collective-permute-start | bytes 196616 | tf_op jit(solution)/shard_map/ppermute | solution.py:26
  54.7 2.1 %reshape.304 = bf16[16,64,256]{2,1,0:T(8,128)(2,1)S(1)} reshape(bf16[16,64,4,64]{3,2,1,0:T(4,128)(2,1)} %copy.137) | data formatting | bytes 1048576 | tf_op jit(solution)/shard_map/reshape | solution.py:76
  60.3 11.0 %all-to-all-start.1 = ((bf16[64,6,512]{2,1,0:T(8,128)(2,1)}), bf16[64,6,512]{2,1,0:T(8,128)(2,1)}, u32[]{:S(2)}, u32[]{:S(2)}) async-start(bf16[64,6,512]{2,1,0:T(8,128)(2,1)} %pad_maximum_fusion), calls=%async_computation.1 | async-start | bytes 1048576 | tf_op jit(solution)/shard_map/all_to_all | solution.py:104
  72.8 3.8 %copy.167 = bf16[16,16,64,16]{2,1,3,0:T(8,128)(2,1)S(1)} copy(bf16[16,16,64,16]{3,2,1,0:T(8,128)(2,1)} %constant_dynamic-slice_fusion.4) | data formatting | bytes 1048576
  76.6 2.7 %copy.169 = bf16[4,16,64,16]{2,1,3,0:T(8,128)(2,1)} copy(bf16[4,16,64,16]{3,2,1,0:T(8,128)(2,1)} %constant_dynamic-slice_fusion.1) | data formatting | bytes 262144
  83.1 4.4 %fusion.55 = (bf16[16,32,64]{2,1,0:T(8,128)(2,1)S(1)}, f32[16,32,64]{2,1,0:T(8,128)}) fusion(bf16[16,9,32,256]{3,2,1,0:T(8,128)(2,1)S(1)} %bitcast.122, bf16[16,9,64,256]{3,2,1,0:T(8,128)(2,1)} %param.12), kind=kOutput, calls=%fused_computation.134 | convolution fusion | flops 151027712 | bytes 7274496 | tf_op jit(solution)/shard_map/ikpc,ikrc->ipr/dot_general | solution.py:86
  89.0 2.6 %collective-permute-start.11 = (bf16[256,128]{1,0:T(8,128)(2,1)}, bf16[256,128]{1,0:T(8,128)(2,1)}, u32[]{:S(2)}, u32[]{:S(2)}) collective-permute-start(bf16[256,128]{1,0:T(8,128)(2,1)} %reshape.315), channel_id=1, source_target_pairs={{1,0},{2,1},{3,2},{0,3},{5,4},{6,5},{7,6},{4,7},{9,8},{10,9},{11,1... | collective-permute-start | bytes 196616 | tf_op jit(solution)/shard_map/ppermute | solution.py:15
  95.2 1.9 %slice.51 = bf16[64,4,512]{2,1,0:T(4,128)(2,1)} slice(bf16[64,6,512]{2,1,0:T(8,128)(2,1)} %all-to-all-done.1), slice={[0:64], [2:6], [0:512]} | slice | bytes 524288 | tf_op jit(solution)/shard_map/slice | solution.py:106
  103.5 2.1 %collective-permute-start.10 = (bf16[16,2048]{1,0:T(8,128)(2,1)}, bf16[16,2048]{1,0:T(8,128)(2,1)}, u32[]{:S(2)}, u32[]{:S(2)}) collective-permute-start(bf16[16,2048]{1,0:T(8,128)(2,1)} %convert_element_type.115), channel_id=1, source_target_pairs={{3,0},{0,1},{1,2},{2,3},{7,4},{4,5},{5,6},{6,7},{11,8},{8,9},{9,10... | collective-permute-start | bytes 196616 | tf_op jit(solution)/shard_map/ppermute | solution.py:15
  111.2 1.9 %reshape.327 = f32[16,32,256]{2,1,0:T(8,128)S(1)} reshape(f32[16,32,4,64]{3,2,1,0:T(4,128)} %bitcast.126) | data formatting | bytes 1048576 | tf_op jit(solution)/shard_map/convert_element_type | solution.py:130
  117.7 11.9 %all-to-all-start.2 = ((bf16[64,6,512]{2,1,0:T(8,128)(2,1)}), bf16[64,6,512]{2,1,0:T(8,128)(2,1)}, u32[]{:S(2)}, u32[]{:S(2)}) async-start(bf16[64,6,512]{2,1,0:T(8,128)(2,1)} %pad_maximum_fusion.1), calls=%async_computation.2 | async-start | bytes 1048576 | tf_op jit(solution)/shard_map/all_to_all | solution.py:104
  129.7 2.4 %collective-permute-start.15 = (bf16[4,8192]{1,0:T(4,128)(2,1)S(1)}, bf16[4,8192]{1,0:T(4,128)(2,1)S(1)}, u32[]{:S(2)}, u32[]{:S(2)}) collective-permute-start(bf16[4,8192]{1,0:T(4,128)(2,1)S(1)} %bitcast.137), channel_id=1, source_target_pairs={{4,0},{8,4},{12,8},{16,12},{20,16},{24,20},{28,24},{32,28},{36,32}... | collective-permute-start | bytes 196616 | tf_op jit(solution)/shard_map/ppermute | solution.py:27
  132.2 3.4 %collective-permute-start.14 = (bf16[4,8192]{1,0:T(4,128)(2,1)S(1)}, bf16[4,8192]{1,0:T(4,128)(2,1)S(1)}, u32[]{:S(2)}, u32[]{:S(2)}) collective-permute-start(bf16[4,8192]{1,0:T(4,128)(2,1)S(1)} %bitcast.138), channel_id=1, source_target_pairs={{0,4},{4,8},{8,12},{12,16},{16,20},{20,24},{24,28},{28,32},{32,36}... | collective-permute-start | bytes 196616 | tf_op jit(solution)/shard_map/ppermute | solution.py:26
  138.3 9.6 %all-to-all-done.2 = bf16[64,6,512]{2,1,0:T(8,128)(2,1)} async-done(((bf16[64,6,512]{2,1,0:T(8,128)(2,1)}), bf16[64,6,512]{2,1,0:T(8,128)(2,1)}, u32[]{:S(2)}, u32[]{:S(2)}) %all-to-all-start.2) | async-done | bytes 393248 | tf_op jit(solution)/shard_map/all_to_all | solution.py:104
  150.0 2.5 %reshape.321 = bf16[16,16,16,32]{3,2,1,0:T(8,128)(2,1)} reshape(bf16[256,512]{1,0:T(8,128)(2,1)} %fusion.2) | data formatting | bytes 524288 | tf_op jit(solution)/shard_map/reshape | solution.py:108
  152.5 2.7 %convolution_bitcast_fusion.6 = f32[16,64,32]{1,2,0:T(8,128)} fusion(bf16[16,16,64,16]{2,1,3,0:T(8,128)(2,1)} %copy-done.1, bf16[16,16,16,32]{3,2,1,0:T(8,128)(2,1)} %reshape.321), kind=kOutput, calls=%fused_computation.16 | convolution fusion | flops 16777216 | bytes 917504 | tf_op jit(solution)/shard_map/ikab,ikbp->iap/dot_general | solution.py:111
  162.1 2.0 %fusion.3 = f32[16,64,32]{1,2,0:T(8,128)} fusion(f32[16,64,32]{1,2,0:T(8,128)} %convolution_bitcast_fusion.6, bf16[16,64,32]{1,2,0:T(8,128)(2,1)S(1)} %bitcast.132, bf16[16,64,64]{2,1,0:T(8,128)(2,1)} %param.14), kind=kOutput, calls=%fused_computation.10 | convolution fusion | flops 4227072 | bytes 458752 | tf_op jit(solution)/shard_map/iab,ibp->iap/dot_general | solution.py:116
  164.1 2.0 %copy.154 = f32[16,64,32]{2,1,0:T(8,128)} copy(f32[16,64,32]{1,2,0:T(8,128)} %fusion.3) | data formatting | bytes 262144 | tf_op jit(solution)/shard_map/add | solution.py:116
  171.0 4.4 %convolution_bitcast_fusion.3 = f32[16,32,64]{2,1,0:T(8,128)} fusion(bf16[16,9,32,256]{3,2,1,0:T(8,128)(2,1)S(1)} %bitcast.121, bf16[16,9,64,256]{3,2,1,0:T(8,128)(2,1)} %param.12), kind=kOutput, calls=%fused_computation.11 | convolution fusion | flops 150994944 | bytes 7208960 | tf_op jit(solution)/shard_map/ikpc,ikrc->ipr/dot_general | solution.py:86
  (168 shorter events, 72.6 us)
Async XLA Ops:
  0.6 70.7 %copy-start = (bf16[4,16,64,64]{3,2,1,0:T(8,128)(2,1)S(1)}, bf16[4,16,64,64]{3,2,1,0:T(8,128)(2,1)}, u32[]{:S(2)}) copy-start(bf16[4,16,64,64]{3,2,1,0:T(8,128)(2,1)} %param.16) | copy-start | bytes 1572868
  1.8 35.1 %collective-permute-start = (bf16[256,128]{1,0:T(8,128)(2,1)S(1)}, bf16[256,128]{1,0:T(8,128)(2,1)S(1)}, u32[]{:S(2)}, u32[]{:S(2)}) collective-permute-start(bf16[256,128]{1,0:T(8,128)(2,1)S(1)} %reshape.298), channel_id=1, source_target_pairs={{1,0},{2,1},{3,2},{0,3},{5,4},{6,5},{7,6},{4,7},{9,8},{10,9},{11,1... | collective-permute-start | bytes 196616 | tf_op jit(solution)/shard_map/ppermute | solution.py:15
  5.2 31.8 %collective-permute-start.1 = (bf16[256,128]{1,0:T(8,128)(2,1)S(1)}, bf16[256,128]{1,0:T(8,128)(2,1)S(1)}, u32[]{:S(2)}, u32[]{:S(2)}) collective-permute-start(bf16[256,128]{1,0:T(8,128)(2,1)S(1)} %reshape.298), channel_id=1, source_target_pairs={{2,0},{3,1},{0,2},{1,3},{6,4},{7,5},{4,6},{5,7},{10,8},{11,9},{8,1... | collective-permute-start | bytes 196616 | tf_op jit(solution)/shard_map/ppermute | solution.py:15
  5.7 31.3 %collective-permute-start.2 = (bf16[256,128]{1,0:T(8,128)(2,1)S(1)}, bf16[256,128]{1,0:T(8,128)(2,1)S(1)}, u32[]{:S(2)}, u32[]{:S(2)}) collective-permute-start(bf16[256,128]{1,0:T(8,128)(2,1)S(1)} %reshape.298), channel_id=1, source_target_pairs={{3,0},{0,1},{1,2},{2,3},{7,4},{4,5},{5,6},{6,7},{11,8},{8,9},{9,10... | collective-permute-start | bytes 196616 | tf_op jit(solution)/shard_map/ppermute | solution.py:15
  7.4 39.2 %collective-permute-start.5 = (bf16[512,128]{1,0:T(8,128)(2,1)S(1)}, bf16[512,128]{1,0:T(8,128)(2,1)S(1)}, u32[]{:S(2)}, u32[]{:S(2)}) collective-permute-start(bf16[512,128]{1,0:T(8,128)(2,1)S(1)} %reshape.302), channel_id=1, source_target_pairs={{1,0},{2,1},{3,2},{0,3},{5,4},{6,5},{7,6},{4,7},{9,8},{10,9},{11,1... | collective-permute-start | bytes 393224 | tf_op jit(solution)/shard_map/ppermute | solution.py:15
  9.6 37.7 %collective-permute-start.6 = (bf16[512,128]{1,0:T(8,128)(2,1)S(1)}, bf16[512,128]{1,0:T(8,128)(2,1)S(1)}, u32[]{:S(2)}, u32[]{:S(2)}) collective-permute-start(bf16[512,128]{1,0:T(8,128)(2,1)S(1)} %reshape.302), channel_id=1, source_target_pairs={{2,0},{3,1},{0,2},{1,3},{6,4},{7,5},{4,6},{5,7},{10,8},{11,9},{8,1... | collective-permute-start | bytes 393224 | tf_op jit(solution)/shard_map/ppermute | solution.py:15
  12.5 23.0 %all-to-all-start = ((s32[64,1,2]{2,1,0:T(1,128)}), s32[64,1,2]{2,1,0:T(1,128)S(1)}, u32[]{:S(2)}, u32[]{:S(2)}) async-start(s32[64,1,2]{2,1,0:T(1,128)} %copy.136), calls=%async_computation | async-start | bytes 65536 | tf_op jit(solution)/shard_map/all_to_all | solution.py:58
  27.4 65.9 %copy-start.6 = (pred[64,1,256]{2,0,1:T(32,128)(4,1)}, pred[64,1,256]{2,0,1:T(32,128)(4,1)S(1)}, u32[]{:S(2)}) copy-start(pred[64,1,256]{2,0,1:T(32,128)(4,1)S(1)} %get-tuple-element.22) | copy-start | bytes 49156
  36.9 11.1 %collective-permute-start.7 = (bf16[512,128]{1,0:T(8,128)(2,1)S(1)}, bf16[512,128]{1,0:T(8,128)(2,1)S(1)}, u32[]{:S(2)}, u32[]{:S(2)}) collective-permute-start(bf16[512,128]{1,0:T(8,128)(2,1)S(1)} %reshape.302), channel_id=1, source_target_pairs={{3,0},{0,1},{1,2},{2,3},{7,4},{4,5},{5,6},{6,7},{11,8},{8,9},{9,10... | collective-permute-start | bytes 393224 | tf_op jit(solution)/shard_map/ppermute | solution.py:15
  38.9 41.7 %collective-permute-start.4 = (bf16[4,8192]{1,0:T(4,128)(2,1)}, bf16[4,8192]{1,0:T(4,128)(2,1)}, u32[]{:S(2)}, u32[]{:S(2)}) collective-permute-start(bf16[4,8192]{1,0:T(4,128)(2,1)} %slice.39), channel_id=1, source_target_pairs={{4,0},{8,4},{12,8},{16,12},{20,16},{24,20},{28,24},{32,28},{36,32}... | collective-permute-start | bytes 196616 | tf_op jit(solution)/shard_map/ppermute | solution.py:27
  42.4 38.2 %collective-permute-start.3 = (bf16[4,8192]{1,0:T(4,128)(2,1)}, bf16[4,8192]{1,0:T(4,128)(2,1)}, u32[]{:S(2)}, u32[]{:S(2)}) collective-permute-start(bf16[4,8192]{1,0:T(4,128)(2,1)} %slice.37), channel_id=1, source_target_pairs={{0,4},{4,8},{8,12},{12,16},{16,20},{20,24},{24,28},{28,32},{32,36}... | collective-permute-start | bytes 196616 | tf_op jit(solution)/shard_map/ppermute | solution.py:26
  60.3 31.9 %all-to-all-start.1 = ((bf16[64,6,512]{2,1,0:T(8,128)(2,1)}), bf16[64,6,512]{2,1,0:T(8,128)(2,1)}, u32[]{:S(2)}, u32[]{:S(2)}) async-start(bf16[64,6,512]{2,1,0:T(8,128)(2,1)} %pad_maximum_fusion), calls=%async_computation.1 | async-start | bytes 1048576 | tf_op jit(solution)/shard_map/all_to_all | solution.py:104
  89.0 18.2 %collective-permute-start.11 = (bf16[256,128]{1,0:T(8,128)(2,1)}, bf16[256,128]{1,0:T(8,128)(2,1)}, u32[]{:S(2)}, u32[]{:S(2)}) collective-permute-start(bf16[256,128]{1,0:T(8,128)(2,1)} %reshape.315), channel_id=1, source_target_pairs={{1,0},{2,1},{3,2},{0,3},{5,4},{6,5},{7,6},{4,7},{9,8},{10,9},{11,1... | collective-permute-start | bytes 196616 | tf_op jit(solution)/shard_map/ppermute | solution.py:15
  91.6 16.3 %collective-permute-start.12 = (bf16[256,128]{1,0:T(8,128)(2,1)}, bf16[256,128]{1,0:T(8,128)(2,1)}, u32[]{:S(2)}, u32[]{:S(2)}) collective-permute-start(bf16[256,128]{1,0:T(8,128)(2,1)} %reshape.315), channel_id=1, source_target_pairs={{2,0},{3,1},{0,2},{1,3},{6,4},{7,5},{4,6},{5,7},{10,8},{11,9},{8,1... | collective-permute-start | bytes 196616 | tf_op jit(solution)/shard_map/ppermute | solution.py:15
  92.1 15.8 %collective-permute-start.13 = (bf16[256,128]{1,0:T(8,128)(2,1)}, bf16[256,128]{1,0:T(8,128)(2,1)}, u32[]{:S(2)}, u32[]{:S(2)}) collective-permute-start(bf16[256,128]{1,0:T(8,128)(2,1)} %reshape.315), channel_id=1, source_target_pairs={{3,0},{0,1},{1,2},{2,3},{7,4},{4,5},{5,6},{6,7},{11,8},{8,9},{9,10... | collective-permute-start | bytes 196616 | tf_op jit(solution)/shard_map/ppermute | solution.py:15
  103.5 9.6 %collective-permute-start.10 = (bf16[16,2048]{1,0:T(8,128)(2,1)}, bf16[16,2048]{1,0:T(8,128)(2,1)}, u32[]{:S(2)}, u32[]{:S(2)}) collective-permute-start(bf16[16,2048]{1,0:T(8,128)(2,1)} %convert_element_type.115), channel_id=1, source_target_pairs={{3,0},{0,1},{1,2},{2,3},{7,4},{4,5},{5,6},{6,7},{11,8},{8,9},{9,10... | collective-permute-start | bytes 196616 | tf_op jit(solution)/shard_map/ppermute | solution.py:15
  105.5 7.6 %collective-permute-start.9 = (bf16[16,2048]{1,0:T(8,128)(2,1)}, bf16[16,2048]{1,0:T(8,128)(2,1)}, u32[]{:S(2)}, u32[]{:S(2)}) collective-permute-start(bf16[16,2048]{1,0:T(8,128)(2,1)} %convert_element_type.115), channel_id=1, source_target_pairs={{2,0},{3,1},{0,2},{1,3},{6,4},{7,5},{4,6},{5,7},{10,8},{11,9},{8,1... | collective-permute-start | bytes 196616 | tf_op jit(solution)/shard_map/ppermute | solution.py:15
  107.2 5.8 %collective-permute-start.8 = (bf16[16,2048]{1,0:T(8,128)(2,1)}, bf16[16,2048]{1,0:T(8,128)(2,1)}, u32[]{:S(2)}, u32[]{:S(2)}) collective-permute-start(bf16[16,2048]{1,0:T(8,128)(2,1)} %convert_element_type.115), channel_id=1, source_target_pairs={{1,0},{2,1},{3,2},{0,3},{5,4},{6,5},{7,6},{4,7},{9,8},{10,9},{11,1... | collective-permute-start | bytes 196616 | tf_op jit(solution)/shard_map/ppermute | solution.py:15
  117.7 30.2 %all-to-all-start.2 = ((bf16[64,6,512]{2,1,0:T(8,128)(2,1)}), bf16[64,6,512]{2,1,0:T(8,128)(2,1)}, u32[]{:S(2)}, u32[]{:S(2)}) async-start(bf16[64,6,512]{2,1,0:T(8,128)(2,1)} %pad_maximum_fusion.1), calls=%async_computation.2 | async-start | bytes 1048576 | tf_op jit(solution)/shard_map/all_to_all | solution.py:104
  129.7 7.0 %collective-permute-start.15 = (bf16[4,8192]{1,0:T(4,128)(2,1)S(1)}, bf16[4,8192]{1,0:T(4,128)(2,1)S(1)}, u32[]{:S(2)}, u32[]{:S(2)}) collective-permute-start(bf16[4,8192]{1,0:T(4,128)(2,1)S(1)} %bitcast.137), channel_id=1, source_target_pairs={{4,0},{8,4},{12,8},{16,12},{20,16},{24,20},{28,24},{32,28},{36,32}... | collective-permute-start | bytes 196616 | tf_op jit(solution)/shard_map/ppermute | solution.py:27
  132.2 4.6 %collective-permute-start.14 = (bf16[4,8192]{1,0:T(4,128)(2,1)S(1)}, bf16[4,8192]{1,0:T(4,128)(2,1)S(1)}, u32[]{:S(2)}, u32[]{:S(2)}) collective-permute-start(bf16[4,8192]{1,0:T(4,128)(2,1)S(1)} %bitcast.138), channel_id=1, source_target_pairs={{0,4},{4,8},{8,12},{12,16},{16,20},{20,24},{24,28},{28,32},{32,36}... | collective-permute-start | bytes 196616 | tf_op jit(solution)/shard_map/ppermute | solution.py:26
  167.4 8.1 %collective-permute-start.18 = (bf16[16,2048]{1,0:T(8,128)(2,1)S(1)}, bf16[16,2048]{1,0:T(8,128)(2,1)S(1)}, u32[]{:S(2)}, u32[]{:S(2)}) collective-permute-start(bf16[16,2048]{1,0:T(8,128)(2,1)S(1)} %convert_element_type.135), channel_id=1, source_target_pairs={{3,0},{0,1},{1,2},{2,3},{7,4},{4,5},{5,6},{6,7},{11,8},{8,9},{9,10... | collective-permute-start | bytes 196616 | tf_op jit(solution)/shard_map/ppermute | solution.py:15
  168.6 6.9 %collective-permute-start.17 = (bf16[16,2048]{1,0:T(8,128)(2,1)S(1)}, bf16[16,2048]{1,0:T(8,128)(2,1)S(1)}, u32[]{:S(2)}, u32[]{:S(2)}) collective-permute-start(bf16[16,2048]{1,0:T(8,128)(2,1)S(1)} %convert_element_type.135), channel_id=1, source_target_pairs={{2,0},{3,1},{0,2},{1,3},{6,4},{7,5},{4,6},{5,7},{10,8},{11,9},{8,1... | collective-permute-start | bytes 196616 | tf_op jit(solution)/shard_map/ppermute | solution.py:15
  169.8 5.7 %collective-permute-start.16 = (bf16[16,2048]{1,0:T(8,128)(2,1)S(1)}, bf16[16,2048]{1,0:T(8,128)(2,1)S(1)}, u32[]{:S(2)}, u32[]{:S(2)}) collective-permute-start(bf16[16,2048]{1,0:T(8,128)(2,1)S(1)} %convert_element_type.135), channel_id=1, source_target_pairs={{1,0},{2,1},{3,2},{0,3},{5,4},{6,5},{7,6},{4,7},{9,8},{10,9},{11,1... | collective-permute-start | bytes 196616 | tf_op jit(solution)/shard_map/ppermute | solution.py:15
  (12 other events, 208.1 us)

commit v2 on v0

v2 whole, which is shorter than its diff:
```python
import jax
import jax.numpy as jnp
from jax import lax
from jax.experimental import pallas as pl
from jax.experimental.pallas import tpu as pltpu
from jax.sharding import PartitionSpec as P

RANK = 64
BRANCH = 4
REACH = 4
CAP = 2
LEAVES = 16
PARENTS = 4
PROBES = 32
ROWS = 64
SUBS = 4
UNKNOWNS = SUBS * ROWS
BAND = RANK // SUBS
NEAR = 9
FAR = 16
PLANES = 8
PLANE = 8
TILES = (LEAVES + PARENTS) // 4
OUT_TILES = PLANES * CAP // 4 + PLANES
BF16, F32 = jnp.bfloat16, jnp.float32

NT = (((1,), (1,)), ((), ()))
VMEM_LIMIT = 24 * 1024 * 1024


def dot(x, y):
    return jnp.dot(x, y, preferred_element_type=F32)


def dot_nt(x, y):
    return lax.dot_general(x, y, NT, preferred_element_type=F32)


def call(kernel, name, outs, args, smem, scratch=()):
    in_specs = [pl.BlockSpec(memory_space=pltpu.SMEM)] * smem
    in_specs += [pl.BlockSpec(memory_space=pltpu.VMEM)] * (len(args) - smem)
    return pl.pallas_call(
        kernel,
        name=name,
        out_shape=[jax.ShapeDtypeStruct(s, d) for s, d in outs],
        in_specs=in_specs,
        out_specs=[pl.BlockSpec(memory_space=pltpu.VMEM)] * len(outs),
        scratch_shapes=list(scratch),
        compiler_params=pltpu.CompilerParams(vmem_limit_bytes=VMEM_LIMIT),
    )(*args)


def pack_kernel(x_ref, basis_ref, out_ref):
    x = jnp.transpose(x_ref[...].astype(F32), (1, 0, 2)).astype(BF16)
    for j in range(LEAVES // 2):
        pair = jnp.concatenate([x[2 * j], x[2 * j + 1]], axis=1)
        basis = jnp.concatenate([basis_ref[2 * j], basis_ref[2 * j + 1]], axis=1)
        for s in range(SUBS):
            out_ref[s, pl.ds(j * PROBES, PROBES), :] = pair
            out_ref[s, pl.ds(LEAVES // 2 * PROBES + j * RANK, RANK), :] = basis


def unpack(ref, i, start, rows):
    half = slice((i % 2) * ROWS, (i % 2 + 1) * ROWS)
    place = pl.ds(start + (i // 2) * rows, rows)
    return jnp.concatenate([ref[s, place, half] for s in range(SUBS)], axis=1)


def coefficients(sub_ref, leaf_x, leaf_basis, transfer_t_ref, out_ref, band_ref):
    band = pl.ds(pl.multiple_of(sub_ref[0] * BAND, BAND), BAND)
    parents = []
    for q in range(PARENTS):
        sums = [dot_nt(leaf_basis(i), leaf_x(i)) for i in range(4 * q, 4 * q + 4)]
        band_ref[q] = jnp.concatenate(sums, axis=1)
        tall = jnp.concatenate([s.astype(BF16) for s in sums], axis=0)
        parents.append(dot(transfer_t_ref[q], tall))
    band_ref[PARENTS] = jnp.concatenate(parents, axis=1)
    for t in range(TILES):
        tile = band_ref[t, band, :].astype(BF16)
        for z in range(PLANES):
            out_ref[z, t] = tile


def first_kernel(sub_ref, got_ref, transfer_t_ref, x_ref, basis_ref, low_ref, high_ref, out_ref, band_ref):
    for i in range(LEAVES):
        x = unpack(got_ref, i, 0, PROBES)
        x_ref[i] = x
        if i < REACH:
            low_ref[i] = x
        if i >= LEAVES - REACH:
            high_ref[i - (LEAVES - REACH)] = x
        basis_ref[i] = unpack(got_ref, i, LEAVES // 2 * PROBES, RANK)
    coefficients(
        sub_ref, lambda i: x_ref[i], lambda i: basis_ref[i], transfer_t_ref, out_ref, band_ref
    )


def field_of(got_ref, q):
    total = got_ref[0, q].astype(F32)
    for s in range(1, SUBS):
        total = total + got_ref[s, q].astype(F32)
    return jnp.transpose(total).astype(BF16)


def second_kernel(
    sub_ref, field_ref, near_ref, basis_ref, transfer_t_ref, x_ref, low_ref, high_ref, out_ref, band_ref
):
    for q in range(PARENTS):
        field = field_of(field_ref, q)
        for c in range(4):
            i = 4 * q + c
            far = dot(field[c * PROBES : (c + 1) * PROBES], basis_ref[i])
            x = (unpack(near_ref, i, 0, PROBES).astype(F32) + far).astype(BF16)
            x_ref[i] = x
            if i < REACH:
                low_ref[i] = x
            if i >= LEAVES - REACH:
                high_ref[i - (LEAVES - REACH)] = x
    coefficients(
        sub_ref, lambda i: x_ref[i], lambda i: basis_ref[i], transfer_t_ref, out_ref, band_ref
    )


def output_kernel(field_ref, near_ref, basis_ref, out_ref):
    outs = []
    for q in range(PARENTS):
        field = field_of(field_ref, q)
        for c in range(4):
            i = 4 * q + c
            outs.append(near_ref[i] + dot(field[c * PROBES : (c + 1) * PROBES], basis_ref[i]))
    out_ref[...] = jnp.transpose(jnp.stack(outs), (1, 0, 2)).astype(BF16)


def near_kernel(index_ref, x_ref, low_ref, high_ref, blocks_ref, out_ref, packed_ref, wide_ref):
    wide_ref[pl.ds(0, REACH)] = low_ref[...]
    wide_ref[pl.ds(REACH, LEAVES)] = x_ref[...]
    wide_ref[pl.ds(REACH + LEAVES, REACH)] = high_ref[...]
    wide_ref[2 * REACH + LEAVES] = jnp.zeros((PROBES, UNKNOWNS), BF16)
    for j in range(LEAVES // 2):
        pair = []
        for i in (2 * j, 2 * j + 1):
            total = jnp.zeros((PROBES, ROWS), F32)
            for k in range(NEAR):
                total = total + dot_nt(wide_ref[index_ref[i * NEAR + k]], blocks_ref[i, k])
            out_ref[i] = total
            pair.append(total.astype(BF16))
        both = jnp.concatenate(pair, axis=1)
        for s in range(SUBS):
            packed_ref[s, pl.ds(j * PROBES, PROBES), :] = both


def quarter_lanes():
    return lax.broadcasted_iota(jnp.int32, (BAND, 4 * PROBES), 1) // PROBES


def choose_kernel(asked_ref, got_ref, out_ref, rows_ref):
    for z in range(PLANES):
        for i in range(LEAVES):
            c = i % 4
            piece = got_ref[z, i // 4][:, c * PROBES : (c + 1) * PROBES]
            rows_ref[z * LEAVES + i] = jnp.concatenate([piece] * 4, axis=1)
    quarter = quarter_lanes()
    for m in range(PLANE):
        for t in range(PLANES * CAP // 4):
            tile = None
            for c in range(4):
                n = 4 * t + c
                row = rows_ref[n // CAP * LEAVES + asked_ref[m * PLANES * CAP + n]]
                tile = row if tile is None else jnp.where(quarter == c, row, tile)
            out_ref[m, t] = tile
        for z in range(PLANES):
            out_ref[m, PLANES * CAP // 4 + z] = got_ref[z, TILES - 1]


def fold(x):
    x = x + pltpu.roll(x, 2 * PROBES, 1)
    return x + pltpu.roll(x, PROBES, 1)


def far_kernel(far_ref, coarse_ref, got_ref, weights_ref, coarse_weights_ref, transfer_ref, out_ref):
    quarter = quarter_lanes()
    zero = jnp.zeros((BAND, 4 * PROBES), BF16)

    def picked(index_ref, first):
        tiles = []
        for k in range(FAR):
            index = index_ref[first + k]
            tiles.append(jnp.where(quarter == index % 8, got_ref[index // 8], zero))
        return jnp.concatenate(tiles, axis=0)

    wide_quarter = lax.broadcasted_iota(jnp.int32, (RANK, 4 * PROBES), 1) // PROBES
    for q in range(PARENTS):
        coarse = fold(dot(coarse_weights_ref[q], picked(coarse_ref, q * FAR))).astype(BF16)
        down = dot(transfer_ref[q], coarse)
        total = None
        for c in range(4):
            i = 4 * q + c
            part = fold(dot(weights_ref[i], picked(far_ref, i * FAR)))
            part = part + down[c * RANK : (c + 1) * RANK]
            total = part if total is None else jnp.where(wide_quarter == c, part, total)
        for s in range(SUBS):
            out_ref[s, q] = total.astype(BF16)


def weights_kernel(sub_ref, couplings_ref, coarse_ref, out_ref, coarse_out_ref, move_ref):
    source = lax.broadcasted_iota(jnp.int32, (RANK, FAR * BAND), 0) - sub_ref[0] * BAND
    target = lax.broadcasted_iota(jnp.int32, (RANK, FAR * BAND), 1)
    inside = (source >= 0) & (source < BAND)
    for k in range(FAR):
        hit = inside & (target == source + k * BAND)
        move_ref[k] = jnp.where(hit, 1.0, 0.0).astype(BF16)

    def reorder(from_ref, to_ref):
        def body(i, carry):
            total = dot(from_ref[i, 0], move_ref[0])
            for k in range(1, FAR):
                total = total + dot(from_ref[i, k], move_ref[k])
            to_ref[i] = total.astype(BF16)
            return carry

        lax.fori_loop(0, from_ref.shape[0], body, 0)

    reorder(couplings_ref, out_ref)
    reorder(coarse_ref, coarse_out_ref)


def local(
    probes,
    near_blocks,
    leaf_cluster_basis,
    transfer,
    couplings,
    coarse_couplings,
    near_list,
    distant_interaction_list,
    coarse_list,
):
    groups = PLANES * PLANE
    in_plane = [[z * PLANE + m for m in range(PLANE)] for z in range(PLANES)]
    along_z = [[z * PLANE + m for z in range(PLANES)] for m in range(PLANE)]
    sub = lax.axis_index("sub").reshape(1)
    first_leaf = lax.axis_index("leaf") * LEAVES

    named = distant_interaction_list.reshape(-1)
    owner = jnp.where(named >= 0, named // LEAVES, -1)
    place = named % LEAVES
    of_peer = owner[None, :] == jnp.arange(groups)[:, None]
    least = jnp.min(jnp.where(of_peer, place[None, :], LEAVES - 1), axis=1)
    greatest = jnp.max(jnp.where(of_peer, place[None, :], 0), axis=1)
    wanted = jnp.stack([least, greatest], axis=1).reshape(PLANES, PLANE, CAP)
    wanted = wanted.transpose(1, 0, 2).reshape(PLANE, PLANES * CAP)
    asked = lax.all_to_all(wanted, "leaf", 0, 0, axis_index_groups=in_plane, tiled=True)
    asked = asked.reshape(-1)

    def address(live, row, group):
        row = row + (group % PLANE) * OUT_TILES * 4
        return jnp.where(live, row // 4 * 8 + row % 4, 4)

    least_named = jnp.max(jnp.where(of_peer, least[:, None], 0), axis=0)
    second = (place != least_named).astype(jnp.int32)
    far_index = address(named >= 0, owner // PLANE * CAP + second, owner)
    coarse = coarse_list.reshape(-1)
    coarse_owner = coarse // PARENTS
    coarse_index = address(
        coarse >= 0,
        PLANES * CAP + coarse_owner // PLANE * PARENTS + coarse % PARENTS,
        coarse_owner,
    )
    near_index = near_list.reshape(-1)
    near_index = jnp.where(near_index >= 0, near_index - first_leaf + REACH, LEAVES + 2 * REACH)

    transfer_down = transfer.reshape(PARENTS, BRANCH * RANK, RANK)
    transfer_up = jnp.swapaxes(transfer_down, 1, 2)

    weights, coarse_weights = call(
        weights_kernel,
        "order_couplings",
        [((LEAVES, RANK, FAR * BAND), BF16), ((PARENTS, RANK, FAR * BAND), BF16)],
        [sub, couplings, coarse_couplings],
        1,
        [pltpu.VMEM((FAR, RANK, FAR * BAND), BF16)],
    )

    def over_sub(x):
        return lax.all_to_all(x, "sub", 0, 0, tiled=True)

    x_shape = (LEAVES, PROBES, UNKNOWNS)
    edge = (REACH, PROBES, UNKNOWNS)
    message = (PLANES, TILES, BAND, 4 * PROBES)
    packed_rows = LEAVES // 2 * PROBES
    band_scratch = [pltpu.VMEM((TILES, RANK, 4 * PROBES), F32)]

    def exchange(tiles):
        column = lax.all_to_all(tiles, "leaf", 0, 0, axis_index_groups=along_z, tiled=True)
        (chosen,) = call(
            choose_kernel,
            "choose_rows",
            [((PLANE, OUT_TILES, BAND, 4 * PROBES), BF16)],
            [asked, column],
            1,
            [pltpu.VMEM((PLANES * LEAVES, BAND, 4 * PROBES), BF16)],
        )
        got = lax.all_to_all(chosen, "leaf", 0, 0, axis_index_groups=in_plane, tiled=True)
        return got.reshape(PLANE * OUT_TILES, BAND, 4 * PROBES)

    def far(tiles):
        (part,) = call(
            far_kernel,
            "far_field",
            [((SUBS, PARENTS, RANK, 4 * PROBES), BF16)],
            [far_index, coarse_index, exchange(tiles), weights, coarse_weights, transfer_down],
            2,
        )
        return over_sub(part)

    def near(x, low, high):
        count = groups
        from_below = lax.ppermute(high, "leaf", [(i, i + 1) for i in range(count - 1)])
        from_above = lax.ppermute(low, "leaf", [(i + 1, i) for i in range(count - 1)])
        return call(
            near_kernel,
            "near_field",
            [((LEAVES, PROBES, ROWS), F32), ((SUBS, packed_rows, 2 * ROWS), BF16)],
            [near_index, x, from_below, from_above, near_blocks],
            1,
            [pltpu.VMEM((LEAVES + 2 * REACH + 1, PROBES, UNKNOWNS), BF16)],
        )

    def output(field, near_part):
        return call(
            output_kernel,
            "output",
            [((PROBES, LEAVES, ROWS), BF16)],
            [field, near_part, leaf_cluster_basis],
            0,
        )[0]

    (packed,) = call(
        pack_kernel,
        "pack",
        [((SUBS, packed_rows + LEAVES // 2 * RANK, 2 * ROWS), BF16)],
        [probes, leaf_cluster_basis],
        0,
    )
    x0, basis, low, high, tiles = call(
        first_kernel,
        "first_coefficients",
        [
            (x_shape, BF16),
            ((LEAVES, RANK, UNKNOWNS), BF16),
            (edge, BF16),
            (edge, BF16),
            (message, BF16),
        ],
        [sub, over_sub(packed), transfer_up],
        1,
        band_scratch,
    )
    near1, near1_packed = near(x0, low, high)
    near1_whole = over_sub(near1_packed)
    field1 = far(tiles)
    x1, low, high, tiles = call(
        second_kernel,
        "second_coefficients",
        [(x_shape, BF16), (edge, BF16), (edge, BF16), (message, BF16)],
        [sub, field1, near1_whole, basis, transfer_up],
        1,
        band_scratch,
    )
    first = output(field1, near1)
    near2, _ = near(x1, low, high)
    field2 = far(tiles)
    return (first, output(field2, near2))


def solution(mesh):
    return jax.shard_map(
        local,
        mesh=mesh,
        in_specs=(
            P(None, "leaf", "sub"),
            P("leaf", None, "sub", None),
            P("leaf", None, "sub"),
            P("leaf", None, None),
            P("leaf", None, None, None),
            P("leaf", None, None, None),
            P("leaf", None),
            P("leaf", None),
            P("leaf", None),
        ),
        out_specs=(P(None, "leaf", "sub"), P(None, "leaf", "sub")),
        check_vma=False,
    )
```

time: 353 us -> 142 us (0.40)
  the two profiles are of different devices: /device:TPU:96 before, /device:TPU:27 now
where the time goes in v2:
time: 142 us; the launch traced here: 141 us
  starting transfers between devices  46.5 us (33%)
  blocking collectives  34.7 us (24%)
  Pallas kernels  27.5 us (19%)
  waiting for transfers between devices  21 us (15%)
  local copies, waits for them, and re-layouts  9.9 us (7%)
    pallas_call x12, Pallas kernels, call(): pl.pallas_call(kernel, name=name, out_shape=[jax.ShapeDtypeStruct(s, d) f...  27.5 us
    all_to_all x1, blocking collectives, exchange(): lax.all_to_all(chosen, 'leaf', 0, 0, axis_index_groups=in_plane, tiled=True)  16.1 us
    all_to_all x3, starting transfers between devices, over_sub(): return lax.all_to_all(x, 'sub', 0, 0, tiled=True)  13.5 us
    all_to_all x1, blocking collectives, exchange(): lax.all_to_all(tiles, 'leaf', 0, 0, axis_index_groups=along_z, tiled=True)  10.7 us
    all_to_all x3, waiting for transfers between devices, over_sub(): return lax.all_to_all(x, 'sub', 0, 0, tiled=True)  9.2 us
    all_to_all x1, starting transfers between devices, exchange(): lax.all_to_all(tiles, 'leaf', 0, 0, axis_index_groups=along_z, tiled=True)  8.19 us
    all_to_all x1, blocking collectives, over_sub(): return lax.all_to_all(x, 'sub', 0, 0, tiled=True)  7.9 us
    all_to_all x1, starting transfers between devices, exchange(): lax.all_to_all(chosen, 'leaf', 0, 0, axis_index_groups=in_plane, tiled=True)  7.69 us
  transfers between devices with their start and end apart: 10, of which 5 were waited for; matrix products, arithmetic and copies ran while one was open for 3% of the time, Pallas kernels for 12%

profile of v2, /device:TPU:27, one launch (start us, length us, event | category | flops | bytes accessed | tf_op | source)
XLA Modules:
  0.0 141.4 jit_solution(17230274388040601378)
XLA Ops:
  3.6 4.3 %all-to-all-start.1 = ((bf16[4,768,128]{2,1,0:T(8,128)(2,1)}), bf16[4,768,128]{2,1,0:T(8,128)(2,1)S(1)}, u32[]{:S(2)}, u32[]{:S(2)}) async-start(bf16[4,768,128]{2,1,0:T(8,128)(2,1)} %pack.1), calls=%async_computation.1 | async-start | bytes 1572864 | tf_op jit(solution)/shard_map/all_to_all | solution.py:285
  9.6 8.4 %all-to-all-done.1.got_ref = bf16[4,768,128]{2,1,0:T(8,128)(2,1)S(1)} async-done(((bf16[4,768,128]{2,1,0:T(8,128)(2,1)}), bf16[4,768,128]{2,1,0:T(8,128)(2,1)S(1)}, u32[]{:S(2)}, u32[]{:S(2)}) %all-to-all-start.1) | async-done | bytes 786464 | tf_op jit(solution)/shard_map/all_to_all | solution.py:285
  18.0 6.2 %all-to-all-start = ((s32[8,1,16]{2,1,0:T(1,128)}), s32[8,1,16]{2,1,0:T(1,128)S(1)}, u32[]{:S(2)}, u32[]{:S(2)}) async-start(s32[8,1,16]{2,1,0:T(1,128)} %copy.20), calls=%async_computation | async-start | bytes 8192 | tf_op jit(solution)/shard_map/all_to_all | solution.py:252
  27.1 8.2 %all-to-all-start.2 = ((bf16[8,5,16,128]{3,2,1,0:T(8,128)(2,1)}), bf16[8,5,16,128]{3,2,1,0:T(8,128)(2,1)S(1)}, u32[]{:S(2)}, u32[]{:S(2)}) async-start(bf16[8,5,16,128]{3,2,1,0:T(8,128)(2,1)} %get-tuple-element.16), calls=%async_computation.2 | async-start | bytes 327680 | tf_op jit(solution)/shard_map/all_to_all | solution.py:294
  36.6 6.8 %all-to-all-done.2.got_ref = bf16[8,5,16,128]{3,2,1,0:T(8,128)(2,1)S(1)} async-done(((bf16[8,5,16,128]{3,2,1,0:T(8,128)(2,1)}), bf16[8,5,16,128]{3,2,1,0:T(8,128)(2,1)S(1)}, u32[]{:S(2)}, u32[]{:S(2)}) %all-to-all-start.2) | async-done | bytes 163872 | tf_op jit(solution)/shard_map/all_to_all | solution.py:294
  43.4 1.9 %choose_rows.2 = bf16[8,12,16,128]{3,2,1,0:T(8,128)(2,1)} custom-call(s32[128]{0:T(128)S(1)} %reshape.101.asked_ref, bf16[8,5,16,128]{3,2,1,0:T(8,128)(2,1)S(1)} %all-to-all-done.2.got_ref), custom_call_target="tpu_custom_call" | custom-call | tf_op jit(solution)/shard_map/choose_rows/pallas_call | solution.py:42
  45.3 7.7 %all-to-all-start.3 = ((bf16[8,12,16,128]{3,2,1,0:T(8,128)(2,1)}), bf16[8,12,16,128]{3,2,1,0:T(8,128)(2,1)S(1)}, u32[]{:S(2)}, u32[]{:S(2)}) async-start(bf16[8,12,16,128]{3,2,1,0:T(8,128)(2,1)} %choose_rows.2), calls=%async_computation.3 | async-start | bytes 786432 | tf_op jit(solution)/shard_map/all_to_all | solution.py:303
  53.1 2.0 %collective-permute-start = (bf16[4,32,256]{2,1,0:T(8,128)(2,1)}, bf16[4,32,256]{2,1,0:T(8,128)(2,1)S(1)}, u32[]{:S(2)}, u32[]{:S(2)}) collective-permute-start(bf16[4,32,256]{2,1,0:T(8,128)(2,1)} %get-tuple-element.20), channel_id=1, source_target_pairs={{0,4},{4,8},{8,12},{12,16},{16,20},{20,24},{24,28},{28,32},{32,36}... | collective-permute-start | bytes 196616 | tf_op jit(solution)/shard_map/ppermute | solution.py:318
  55.0 2.4 %collective-permute-start.1 = (bf16[4,32,256]{2,1,0:T(8,128)(2,1)}, bf16[4,32,256]{2,1,0:T(8,128)(2,1)S(1)}, u32[]{:S(2)}, u32[]{:S(2)}) collective-permute-start(bf16[4,32,256]{2,1,0:T(8,128)(2,1)} %get-tuple-element.21), channel_id=1, source_target_pairs={{4,0},{8,4},{12,8},{16,12},{20,16},{24,20},{28,24},{32,28},{36,32}... | collective-permute-start | bytes 196616 | tf_op jit(solution)/shard_map/ppermute | solution.py:319
  57.6 2.2 %copy-done.2 = bf16[16,16,64,64]{3,2,1,0:T(8,128)(2,1)S(1)} copy-done((bf16[16,16,64,64]{3,2,1,0:T(8,128)(2,1)S(1)}, bf16[16,16,64,64]{3,2,1,0:T(8,128)(2,1)}, u32[]{:S(2)}) %copy-start.2) | copy-done | bytes 2097176
  59.8 5.7 %order_couplings.1 = (bf16[16,64,256]{2,1,0:T(8,128)(2,1)S(1)}, bf16[4,64,256]{2,1,0:T(8,128)(2,1)S(1)}) custom-call(s32[1]{0:T(128)} %bitcast.2.sub_ref, bf16[16,16,64,64]{3,2,1,0:T(8,128)(2,1)S(1)} %copy-done.2, bf16[4,16,64,64]{3,2,1,0:T(8,128)(2,1)S(1)} %copy-done.6), custom_call_target="tpu_custom_call" | custom-call | tf_op jit(solution)/shard_map/order_couplings/pallas_call | solution.py:42
  65.6 2.7 %near_field.2 = (f32[16,32,64]{2,1,0:T(8,128)S(1)}, bf16[4,256,128]{2,1,0:T(8,128)(2,1)}) custom-call(s32[144]{0:T(256)S(1)} %select_n.110.index_ref, bf16[16,32,256]{2,1,0:T(8,128)(2,1)S(1)} %copy-done.8, bf16[4,32,256]{2,1,0:T(8,128)(2,1)S(1)} %collective-permute-done.low_ref, bf16[4,32,256]{2,1,0:T(8,128)(2,1)S(1)} %collective-permute-done.1.high_ref, ...), custom_call_target="tpu_custom_call" | custom-call | tf_op jit(solution)/shard_map/near_field/pallas_call | solution.py:42
  68.3 4.7 %all-to-all-start.5 = ((bf16[4,256,128]{2,1,0:T(8,128)(2,1)}), bf16[4,256,128]{2,1,0:T(8,128)(2,1)S(1)}, u32[]{:S(2)}, u32[]{:S(2)}) async-start(bf16[4,256,128]{2,1,0:T(8,128)(2,1)} %get-tuple-element.23), calls=%async_computation.5 | async-start | bytes 524288 | tf_op jit(solution)/shard_map/all_to_all | solution.py:285
  73.0 3.6 %far_field.2 = bf16[4,4,64,128]{3,2,1,0:T(8,128)(2,1)S(1)} custom-call(s32[256]{0:T(256)S(1)} %fusion.4.far_ref, s32[64]{0:T(128)S(1)} %compare_select_fusion.coarse_ref, bf16[96,16,128]{2,1,0:T(8,128)(2,1)S(1)} %bitcast.12, bf16[16,64,256]{2,1,0:T(8,128)(2,1)S(1)} %get-tuple-element.17.weights_ref, ...), custom_call_target="tpu_custom_call" | custom-call | tf_op jit(solution)/shard_map/far_field/pallas_call | solution.py:42
  77.3 7.9 %all_to_all.49.field_ref = bf16[4,4,64,128]{3,2,1,0:T(8,128)(2,1)S(1)} all-to-all(bf16[4,4,64,128]{3,2,1,0:T(8,128)(2,1)S(1)} %far_field.2), channel_id=1, replica_groups=mesh['leaf'=64,'sub'=4] {'sub'}, dimensions={0} | all-to-all | bytes 524288 | tf_op jit(solution)/shard_map/all_to_all | solution.py:285
  86.3 10.7 %all_to_all.50.got_ref = bf16[8,5,16,128]{3,2,1,0:T(8,128)(2,1)S(1)} all-to-all(bf16[8,5,16,128]{3,2,1,0:T(8,128)(2,1)S(1)} %get-tuple-element.25), channel_id=1, replica_groups={{0,32,64,96,128,160,192,224},{4,36,68,100,132,164,196,228},{8,40,72,104..., dimensions={0} | all-to-all | bytes 327680 | tf_op jit(solution)/shard_map/all_to_all | solution.py:294
  98.1 16.1 %all_to_all.51 = bf16[8,12,16,128]{3,2,1,0:T(8,128)(2,1)S(1)} all-to-all(bf16[8,12,16,128]{3,2,1,0:T(8,128)(2,1)S(1)} %choose_rows.3), channel_id=1, replica_groups={{0,4,8,12,16,20,24,28},{32,36,40,44,48,52,56,60},{64,68,72,76,80,84,88,..., dimensions={0} | all-to-all | bytes 786432 | tf_op jit(solution)/shard_map/all_to_all | solution.py:303
  114.2 4.2 %far_field.3 = bf16[4,4,64,128]{3,2,1,0:T(8,128)(2,1)} custom-call(s32[256]{0:T(256)S(1)} %fusion.4.far_ref, s32[64]{0:T(128)S(1)} %compare_select_fusion.coarse_ref, bf16[96,16,128]{2,1,0:T(8,128)(2,1)S(1)} %bitcast.13, bf16[16,64,256]{2,1,0:T(8,128)(2,1)S(1)} %get-tuple-element.17.weights_ref, ...), custom_call_target="tpu_custom_call" | custom-call | tf_op jit(solution)/shard_map/far_field/pallas_call | solution.py:42
  118.4 4.5 %all-to-all-start.8 = ((bf16[4,4,64,128]{3,2,1,0:T(8,128)(2,1)}), bf16[4,4,64,128]{3,2,1,0:T(8,128)(2,1)S(1)}, u32[]{:S(2)}, u32[]{:S(2)}) async-start(bf16[4,4,64,128]{3,2,1,0:T(8,128)(2,1)} %far_field.3), calls=%async_computation.8 | async-start | bytes 524288 | tf_op jit(solution)/shard_map/all_to_all | solution.py:285
  122.9 4.7 %collective-permute-start.2 = (bf16[4,32,256]{2,1,0:T(8,128)(2,1)S(1)}, bf16[4,32,256]{2,1,0:T(8,128)(2,1)S(1)}, u32[]{:S(2)}, u32[]{:S(2)}) collective-permute-start(bf16[4,32,256]{2,1,0:T(8,128)(2,1)S(1)} %get-tuple-element.27), channel_id=1, source_target_pairs={{0,4},{4,8},{8,12},{12,16},{16,20},{20,24},{24,28},{28,32},{32,36}... | collective-permute-start | bytes 196616 | tf_op jit(solution)/shard_map/ppermute | solution.py:318
  127.7 1.9 %collective-permute-start.3 = (bf16[4,32,256]{2,1,0:T(8,128)(2,1)S(1)}, bf16[4,32,256]{2,1,0:T(8,128)(2,1)S(1)}, u32[]{:S(2)}, u32[]{:S(2)}) collective-permute-start(bf16[4,32,256]{2,1,0:T(8,128)(2,1)S(1)} %get-tuple-element.28), channel_id=1, source_target_pairs={{4,0},{8,4},{12,8},{16,12},{20,16},{24,20},{28,24},{32,28},{36,32}... | collective-permute-start | bytes 196616 | tf_op jit(solution)/shard_map/ppermute | solution.py:319
  130.6 4.8 %collective-permute-done.3.high_ref = bf16[4,32,256]{2,1,0:T(8,128)(2,1)S(1)} collective-permute-done((bf16[4,32,256]{2,1,0:T(8,128)(2,1)S(1)}, bf16[4,32,256]{2,1,0:T(8,128)(2,1)S(1)}, u32[]{:S(2)}, u32[]{:S(2)}) %collective-permute-start.3) | collective-permute-done | bytes 65568 | tf_op jit(solution)/shard_map/ppermute | solution.py:319
  135.4 2.3 %copy-done.1 = bf16[16,9,64,256]{3,2,1,0:T(8,128)(2,1)S(1)} copy-done((bf16[16,9,64,256]{3,2,1,0:T(8,128)(2,1)S(1)}, bf16[16,9,64,256]{3,2,1,0:T(8,128)(2,1)}, u32[]{:S(2)}) %copy-start.1) | copy-done | bytes 4718616
  137.7 2.7 %near_field.3 = (f32[16,32,64]{2,1,0:T(8,128)S(1)}, bf16[4,256,128]{2,1,0:T(8,128)(2,1)}) custom-call(s32[144]{0:T(256)S(1)} %select_n.110.index_ref, bf16[16,32,256]{2,1,0:T(8,128)(2,1)S(1)} %get-tuple-element.26.x_ref, bf16[4,32,256]{2,1,0:T(8,128)(2,1)S(1)} %collective-permute-done.2.low_ref, bf16[4,32,256]{2,1,0:T(8,128)(2,1)S(1)} %collective-permute-done.3.high_ref, ...), custom_call_target="tpu_custom_call" | custom-call | tf_op jit(solution)/shard_map/near_field/pallas_call | solution.py:42
  (53 shorter events, 14.1 us)
Async XLA Ops:
  0.6 1.0 copy-start.4
  1.6 0.9 copy-start.9
  2.5 50.5 %copy-start.10 = (s32[16,9]{1,0:T(8,128)S(1)}, s32[16,9]{1,0:T(8,128)}, u32[]{:S(2)}) copy-start(s32[16,9]{1,0:T(8,128)} %param.15) | copy-start | bytes 1732
  2.5 54.9 %copy-start.11 = (s32[4,16]{1,0:T(4,128)S(1)}, s32[4,16]{1,0:T(4,128)}, u32[]{:S(2)}) copy-start(s32[4,16]{1,0:T(4,128)} %param.17) | copy-start | bytes 772
  2.5 55.1 %copy-start.6 = (bf16[4,16,64,64]{3,2,1,0:T(8,128)(2,1)S(1)}, bf16[4,16,64,64]{3,2,1,0:T(8,128)(2,1)}, u32[]{:S(2)}) copy-start(bf16[4,16,64,64]{3,2,1,0:T(8,128)(2,1)} %coarse_ref.1) | copy-start | bytes 1572868
  3.6 14.5 %all-to-all-start.1 = ((bf16[4,768,128]{2,1,0:T(8,128)(2,1)}), bf16[4,768,128]{2,1,0:T(8,128)(2,1)S(1)}, u32[]{:S(2)}, u32[]{:S(2)}) async-start(bf16[4,768,128]{2,1,0:T(8,128)(2,1)} %pack.1), calls=%async_computation.1 | async-start | bytes 1572864 | tf_op jit(solution)/shard_map/all_to_all | solution.py:285
  18.0 9.1 %all-to-all-start = ((s32[8,1,16]{2,1,0:T(1,128)}), s32[8,1,16]{2,1,0:T(1,128)S(1)}, u32[]{:S(2)}, u32[]{:S(2)}) async-start(s32[8,1,16]{2,1,0:T(1,128)} %copy.20), calls=%async_computation | async-start | bytes 8192 | tf_op jit(solution)/shard_map/all_to_all | solution.py:252
  26.9 30.6 %copy-start.7 = (bf16[16,32,256]{2,1,0:T(8,128)(2,1)}, bf16[16,32,256]{2,1,0:T(8,128)(2,1)S(1)}, u32[]{:S(2)}) copy-start(bf16[16,32,256]{2,1,0:T(8,128)(2,1)S(1)} %get-tuple-element.19.x_ref) | copy-start | bytes 786436
  27.1 16.3 %all-to-all-start.2 = ((bf16[8,5,16,128]{3,2,1,0:T(8,128)(2,1)}), bf16[8,5,16,128]{3,2,1,0:T(8,128)(2,1)S(1)}, u32[]{:S(2)}, u32[]{:S(2)}) async-start(bf16[8,5,16,128]{3,2,1,0:T(8,128)(2,1)} %get-tuple-element.16), calls=%async_computation.2 | async-start | bytes 327680 | tf_op jit(solution)/shard_map/all_to_all | solution.py:294
  45.3 23.0 %all-to-all-start.3 = ((bf16[8,12,16,128]{3,2,1,0:T(8,128)(2,1)}), bf16[8,12,16,128]{3,2,1,0:T(8,128)(2,1)S(1)}, u32[]{:S(2)}, u32[]{:S(2)}) async-start(bf16[8,12,16,128]{3,2,1,0:T(8,128)(2,1)} %choose_rows.2), calls=%async_computation.3 | async-start | bytes 786432 | tf_op jit(solution)/shard_map/all_to_all | solution.py:303
  53.1 12.5 %collective-permute-start = (bf16[4,32,256]{2,1,0:T(8,128)(2,1)}, bf16[4,32,256]{2,1,0:T(8,128)(2,1)S(1)}, u32[]{:S(2)}, u32[]{:S(2)}) collective-permute-start(bf16[4,32,256]{2,1,0:T(8,128)(2,1)} %get-tuple-element.20), channel_id=1, source_target_pairs={{0,4},{4,8},{8,12},{12,16},{16,20},{20,24},{24,28},{28,32},{32,36}... | collective-permute-start | bytes 196616 | tf_op jit(solution)/shard_map/ppermute | solution.py:318
  55.0 10.5 %collective-permute-start.1 = (bf16[4,32,256]{2,1,0:T(8,128)(2,1)}, bf16[4,32,256]{2,1,0:T(8,128)(2,1)S(1)}, u32[]{:S(2)}, u32[]{:S(2)}) collective-permute-start(bf16[4,32,256]{2,1,0:T(8,128)(2,1)} %get-tuple-element.21), channel_id=1, source_target_pairs={{4,0},{8,4},{12,8},{16,12},{20,16},{24,20},{28,24},{32,28},{36,32}... | collective-permute-start | bytes 196616 | tf_op jit(solution)/shard_map/ppermute | solution.py:319
  57.6 2.2 %copy-start.2 = (bf16[16,16,64,64]{3,2,1,0:T(8,128)(2,1)S(1)}, bf16[16,16,64,64]{3,2,1,0:T(8,128)(2,1)}, u32[]{:S(2)}) copy-start(bf16[16,16,64,64]{3,2,1,0:T(8,128)(2,1)} %couplings_ref.1) | copy-start | bytes 6291460
  59.8 5.7 %copy-start = (bf16[16,9,64,256]{3,2,1,0:T(8,128)(2,1)S(1)}, bf16[16,9,64,256]{3,2,1,0:T(8,128)(2,1)}, u32[]{:S(2)}) copy-start(bf16[16,9,64,256]{3,2,1,0:T(8,128)(2,1)} %blocks_ref.3) | copy-start | bytes 14155780
  59.8 5.7 %copy-start.8 = (bf16[16,32,256]{2,1,0:T(8,128)(2,1)S(1)}, bf16[16,32,256]{2,1,0:T(8,128)(2,1)}, u32[]{:S(2)}) copy-start(bf16[16,32,256]{2,1,0:T(8,128)(2,1)} %copy-done.7) | copy-start | bytes 786436
  59.8 13.2 %copy-start.3 = (bf16[16,64,64]{2,1,0:T(8,128)(2,1)S(1)}, bf16[16,64,64]{2,1,0:T(8,128)(2,1)}, u32[]{:S(2)}) copy-start(bf16[16,64,64]{2,1,0:T(8,128)(2,1)} %param.12) | copy-start | bytes 393220
  68.3 61.3 %copy-start.5 = (bf16[16,64,64]{2,1,0:T(8,128)(2,1)S(1)}, bf16[16,64,64]{2,1,0:T(8,128)(2,1)}, u32[]{:S(2)}) copy-start(bf16[16,64,64]{2,1,0:T(8,128)(2,1)} %basis_ref.5) | copy-start | bytes 393220
  68.3 9.0 %all-to-all-start.5 = ((bf16[4,256,128]{2,1,0:T(8,128)(2,1)}), bf16[4,256,128]{2,1,0:T(8,128)(2,1)S(1)}, u32[]{:S(2)}, u32[]{:S(2)}) async-start(bf16[4,256,128]{2,1,0:T(8,128)(2,1)} %get-tuple-element.23), calls=%async_computation.5 | async-start | bytes 524288 | tf_op jit(solution)/shard_map/all_to_all | solution.py:285
  118.4 22.0 %all-to-all-start.8 = ((bf16[4,4,64,128]{3,2,1,0:T(8,128)(2,1)}), bf16[4,4,64,128]{3,2,1,0:T(8,128)(2,1)S(1)}, u32[]{:S(2)}, u32[]{:S(2)}) async-start(bf16[4,4,64,128]{3,2,1,0:T(8,128)(2,1)} %far_field.3), calls=%async_computation.8 | async-start | bytes 524288 | tf_op jit(solution)/shard_map/all_to_all | solution.py:285
  122.9 7.6 %collective-permute-start.2 = (bf16[4,32,256]{2,1,0:T(8,128)(2,1)S(1)}, bf16[4,32,256]{2,1,0:T(8,128)(2,1)S(1)}, u32[]{:S(2)}, u32[]{:S(2)}) collective-permute-start(bf16[4,32,256]{2,1,0:T(8,128)(2,1)S(1)} %get-tuple-element.27), channel_id=1, source_target_pairs={{0,4},{4,8},{8,12},{12,16},{16,20},{20,24},{24,28},{28,32},{32,36}... | collective-permute-start | bytes 196616 | tf_op jit(solution)/shard_map/ppermute | solution.py:318
  127.7 7.7 %collective-permute-start.3 = (bf16[4,32,256]{2,1,0:T(8,128)(2,1)S(1)}, bf16[4,32,256]{2,1,0:T(8,128)(2,1)S(1)}, u32[]{:S(2)}, u32[]{:S(2)}) collective-permute-start(bf16[4,32,256]{2,1,0:T(8,128)(2,1)S(1)} %get-tuple-element.28), channel_id=1, source_target_pairs={{4,0},{8,4},{12,8},{16,12},{20,16},{24,20},{28,24},{32,28},{36,32}... | collective-permute-start | bytes 196616 | tf_op jit(solution)/shard_map/ppermute | solution.py:319
  135.4 2.3 %copy-start.1 = (bf16[16,9,64,256]{3,2,1,0:T(8,128)(2,1)S(1)}, bf16[16,9,64,256]{3,2,1,0:T(8,128)(2,1)}, u32[]{:S(2)}) copy-start(bf16[16,9,64,256]{3,2,1,0:T(8,128)(2,1)} %blocks_ref.3) | copy-start | bytes 14155780

commit v3 on v0

v3 whole, which is shorter than its diff:
```python
import jax
import jax.numpy as jnp
from jax import lax
from jax.experimental import pallas as pl
from jax.experimental.pallas import tpu as pltpu
from jax.sharding import PartitionSpec as P

RANK = 64
BRANCH = 4
REACH = 4
CAP = 2
LEAVES = 16
PARENTS = 4
PROBES = 32
ROWS = 64
SUBS = 4
OWN = PROBES // SUBS
UNKNOWNS = SUBS * ROWS
NEAR = 9
FAR = 16
PLANES = 8
PLANE = 8
LANES = 128
TILES = PARENTS + 1
LEAF_OUT = PLANES * CAP // 4
OUT_TILES = LEAF_OUT + PLANES
GOT_ROWS = 4 * PLANE * OUT_TILES
PACKED = LEAVES // 2 * PROBES
SENT = 16 * PARENTS + LEAVES // 2 * RANK
BF16, F32 = jnp.bfloat16, jnp.float32

NT = (((1,), (1,)), ((), ()))
VMEM_LIMIT = 16 * 1024 * 1024


def dot(x, y):
    return jnp.dot(x, y, preferred_element_type=F32)


def dot_nt(x, y):
    return lax.dot_general(x, y, NT, preferred_element_type=F32)


def call(kernel, name, outs, args, scratch=(), chunks=1):
    spaces = {"smem": pltpu.SMEM, "vmem": pltpu.VMEM, "hbm": pltpu.HBM, "cut": pltpu.HBM, "any": pl.ANY}
    moved = [j for j, (kind, _) in enumerate(args) if kind in ("hbm", "any", "cut")]
    buffers = [pltpu.VMEM(args[j][1].shape, args[j][1].dtype) for j in moved]
    scratch = list(scratch)

    def body(*refs):
        refs = list(refs)
        sems = refs.pop()
        front = len(args) + len(outs) + len(scratch)
        whole, parts = [], []
        for n, j in enumerate(moved):
            source, target = refs[j], refs[front + n]
            if args[j][0] == "cut":
                size = target.shape[0] // chunks
                for c in range(chunks):
                    part = pl.ds(c * size, size)
                    parts.append(
                        pltpu.make_async_copy(source.at[part], target.at[part], sems.at[len(moved) + c])
                    )
            else:
                whole.append(pltpu.make_async_copy(source, target, sems.at[n]))
            refs[j] = target
        for copy in whole + parts:
            copy.start()
        for copy in whole:
            copy.wait()
        extra = [lambda c: parts[c].wait()] if parts else []
        kernel(*refs[:front], *extra)

    return pl.pallas_call(
        body,
        name=name,
        out_shape=[jax.ShapeDtypeStruct(s, d) for s, d in outs],
        in_specs=[pl.BlockSpec(memory_space=spaces[kind]) for kind, _ in args],
        out_specs=[pl.BlockSpec(memory_space=pltpu.VMEM)] * len(outs),
        scratch_shapes=scratch + buffers + [pltpu.SemaphoreType.DMA((len(moved) + chunks,))],
        compiler_params=pltpu.CompilerParams(vmem_limit_bytes=VMEM_LIMIT),
    )(*[
        pltpu.with_memory_space_constraint(array, pltpu.HBM) if kind in ("hbm", "cut") else array
        for kind, array in args
    ])


def of_kind(kind, *arrays):
    return [(kind, array) for array in arrays]


def lane_block(rows, lanes):
    return lax.broadcasted_iota(jnp.int32, (rows, lanes), 1) // RANK


def diagonal(x, rows):
    block = lane_block(rows, 4 * RANK)
    out = x[:rows]
    for c in range(1, 4):
        out = jnp.where(block == c, x[c * rows : (c + 1) * rows], out)
    return out


def spread_diagonal(x):
    block = lane_block(x.shape[0], 4 * RANK)
    return jnp.concatenate([jnp.where(block == c, x, jnp.zeros_like(x)) for c in range(4)], axis=0)


def to_tile(x):
    return jnp.concatenate([x[:, :LANES], x[:, LANES:]], axis=0).astype(BF16)


def tile_row(tile, c):
    h, g = c // 2, c % 2
    return tile[h * OWN : (h + 1) * OWN, g * RANK : (g + 1) * RANK]


def index_kernel(
    first_ref, far_ref, coarse_ref, near_ref, wanted_ref, far_out_ref, coarse_out_ref, near_out_ref
):
    groups = PLANES * PLANE
    group = lax.broadcasted_iota(jnp.int32, (groups, FAR), 0)
    named = far_ref[...]
    owner = jnp.where(named >= 0, named >> 4, -1)
    place = (named & (LEAVES - 1)).astype(F32)
    hits = [owner[i : i + 1] == group for i in range(LEAVES)]
    least = jnp.full((groups, FAR), LEAVES - 1.0, F32)
    greatest = jnp.zeros((groups, FAR), F32)
    for i in range(LEAVES):
        least = jnp.minimum(least, jnp.where(hits[i], place[i : i + 1], LEAVES - 1.0))
        greatest = jnp.maximum(greatest, jnp.where(hits[i], place[i : i + 1], 0.0))
    least = jnp.min(least, axis=1, keepdims=True)
    greatest = jnp.max(greatest, axis=1, keepdims=True)
    lane = lax.broadcasted_iota(jnp.int32, (PLANE, LANES), 1)
    wanted = jnp.zeros((PLANE, LANES), F32)
    for z in range(PLANES):
        wanted = jnp.where(lane == CAP * z, least[z * PLANE : (z + 1) * PLANE], wanted)
        wanted = jnp.where(lane == CAP * z + 1, greatest[z * PLANE : (z + 1) * PLANE], wanted)
    wanted_ref[...] = wanted.astype(jnp.int32)
    of_entry = [
        jnp.sum(jnp.where(hits[i], least, 0.0), axis=0, keepdims=True) for i in range(LEAVES)
    ]
    second = jnp.where(place == jnp.concatenate(of_entry, axis=0), 0, 1)
    row = (owner & (PLANE - 1)) * (4 * OUT_TILES) + (owner >> 3) * CAP + second
    far_out_ref[...] = jnp.where(named >= 0, row, GOT_ROWS)
    coarse = coarse_ref[...]
    owner = coarse >> 2
    row = (owner & (PLANE - 1)) * (4 * OUT_TILES) + 4 * LEAF_OUT + (owner >> 3) * PARENTS
    coarse_out_ref[...] = jnp.where(coarse >= 0, row + (coarse & (PARENTS - 1)), GOT_ROWS)
    near = near_ref[...]
    near_out_ref[...] = jnp.where(near >= 0, near - first_ref[0] + REACH, LEAVES + 2 * REACH)


def partial_kernel(
    sub_ref, x_ref, basis_ref, transfer_ref, out0_ref, out1_ref, out2_ref, out3_ref, sums_ref
):
    out_refs = [out0_ref, out1_ref, out2_ref, out3_ref]
    x = jnp.transpose(x_ref[...].astype(F32), (1, 0, 2)).astype(BF16)
    for j in range(LEAVES // 2):
        pair = jnp.concatenate([x[2 * j], x[2 * j + 1]], axis=1)
        for out_ref in out_refs:
            out_ref[pl.ds(j * PROBES, PROBES), :] = pair
    parents = []
    sums = []
    for q in range(PARENTS):
        four = x[4 * q : 4 * q + 4].reshape(4 * PROBES, ROWS)
        leaf = diagonal(dot_nt(four, basis_ref[q]), PROBES)
        sums.append(leaf)
        parents.append(dot(leaf.astype(BF16), transfer_ref[q]))
    sums.append(jnp.concatenate(parents, axis=1))
    for t in range(TILES):
        sums_ref[t] = sums[t]
    for k, out_ref in enumerate(out_refs):
        place = probes_of((sub_ref[0] + k) % SUBS)
        for t in range(TILES):
            out_ref[pl.ds(PACKED + 16 * t, 16), :] = to_tile(sums_ref[t, place, :])


def probes_of(sub):
    return pl.ds(pl.multiple_of(sub * OWN, OWN), OWN)


def in_order(sub_ref, piece_refs, slots_ref, rows):
    for k, piece_ref in enumerate(piece_refs):
        slots_ref[(sub_ref[0] + SUBS - k) % SUBS] = piece_ref[:rows]


def first_kernel(
    sub_ref, got0_ref, got1_ref, got2_ref, got3_ref, x_ref, low_ref, high_ref, out_ref, slots_ref
):
    got_refs = [got0_ref, got1_ref, got2_ref, got3_ref]
    for t in range(TILES):
        total = got0_ref[pl.ds(PACKED + 16 * t, 16), :].astype(F32)
        for got_ref in got_refs[1:]:
            total = total + got_ref[pl.ds(PACKED + 16 * t, 16), :].astype(F32)
        tile = total.astype(BF16)
        for z in range(PLANES):
            out_ref[z, t] = tile
    in_order(sub_ref, got_refs, slots_ref, PACKED)
    for i in range(LEAVES):
        half = slice((i % 2) * ROWS, (i % 2 + 1) * ROWS)
        rows = pl.ds((i // 2) * PROBES, PROBES)
        x = jnp.concatenate([slots_ref[s, rows, half] for s in range(SUBS)], axis=1)
        x_ref[i] = x
        if i < REACH:
            low_ref[i] = x
        if i >= LEAVES - REACH:
            high_ref[i - (LEAVES - REACH)] = x


def join_kernel(sub_ref, got0_ref, got1_ref, got2_ref, got3_ref, near_ref, basis_ref, slots_ref):
    in_order(sub_ref, [got0_ref, got1_ref, got2_ref, got3_ref], slots_ref, SENT)
    for q in range(PARENTS):
        tiles = [slots_ref[s, pl.ds(16 * q, 16), :].astype(F32) for s in range(SUBS)]
        near = [jnp.concatenate([tile_row(t, c) for t in tiles], axis=1) for c in range(4)]
        near_ref[q] = jnp.concatenate(near, axis=0).astype(BF16)
    for i in range(LEAVES):
        half = slice((i % 2) * ROWS, (i % 2 + 1) * ROWS)
        rows = pl.ds(16 * PARENTS + (i // 2) * RANK, RANK)
        whole = jnp.concatenate([slots_ref[s, rows, half] for s in range(SUBS)], axis=1)
        basis_ref[i // 4, pl.ds(i % 4 * RANK, RANK), :] = whole


def weights_kernel(_, couplings_ref, coarse_ref, out_ref):
    for q in range(PARENTS + 1):
        for c in range(4):
            for k in range(0, FAR, 2):
                if q < PARENTS:
                    pair = [couplings_ref[4 * q + c, k], couplings_ref[4 * q + c, k + 1]]
                else:
                    pair = [coarse_ref[c, k], coarse_ref[c, k + 1]]
                both = jnp.concatenate(pair, axis=1)
                out_ref[q, pl.ds(c * RANK, RANK), pl.ds(k * RANK, LANES)] = both


def both_halves(row_pair):
    turned = pltpu.roll(row_pair, RANK, 1)
    left = lax.broadcasted_iota(jnp.int32, row_pair.shape, 1) < RANK
    return jnp.where(left, row_pair, turned), jnp.where(left, turned, row_pair)


def unpack_tile(tile, rows_ref, first):
    wide = tile.astype(F32)
    for h in range(2):
        one, two = both_halves(wide[h * OWN : (h + 1) * OWN])
        rows_ref[first + 2 * h] = one
        rows_ref[first + 2 * h + 1] = two


def choose_kernel(asked_ref, got_ref, out_ref, rows_ref):
    for z in range(PLANES):
        for t in range(LEAVES // 4):
            unpack_tile(got_ref[z, t], rows_ref, z * LEAVES + 4 * t)
    left = lax.broadcasted_iota(jnp.int32, (OWN, LANES), 1) < RANK
    for m in range(PLANE):
        for t in range(LEAF_OUT):
            rows = []
            for n in range(4 * t, 4 * t + 4):
                rows.append(rows_ref[n // CAP * LEAVES + asked_ref[m, n]])
            top = jnp.where(left, rows[0], rows[1])
            bottom = jnp.where(left, rows[2], rows[3])
            out_ref[m, t] = jnp.concatenate([top, bottom], axis=0).astype(BF16)
        for z in range(PLANES):
            out_ref[m, LEAF_OUT + z] = got_ref[z, TILES - 1]


def far_field(far_ref, coarse_ref, got_ref, weights_ref, transfer_ref, rows_ref):
    for n in range(PLANE * OUT_TILES):
        unpack_tile(got_ref[n], rows_ref, 4 * n)
    rows_ref[GOT_ROWS] = jnp.zeros((OWN, LANES), F32)
    left = lax.broadcasted_iota(jnp.int32, (OWN, LANES), 1) < RANK

    def apply(index_ref, q, weights):
        picked = []
        for c in range(4):
            pairs = []
            for k in range(0, FAR, 2):
                one = rows_ref[index_ref[4 * q + c, k]]
                two = rows_ref[index_ref[4 * q + c, k + 1]]
                pairs.append(jnp.where(left, one, two))
            picked.append(jnp.concatenate(pairs, axis=1))
        picked = jnp.concatenate(picked, axis=0).astype(BF16)
        return diagonal(dot_nt(picked, weights), OWN)

    coarse = apply(coarse_ref, 0, weights_ref[PARENTS]).astype(BF16)
    fields = []
    for q in range(PARENTS):
        down = dot_nt(coarse[:, q * RANK : (q + 1) * RANK], transfer_ref[q])
        fields.append(apply(far_ref, q, weights_ref[q]) + down)
    return fields


def middle_kernel(
    far_ref,
    coarse_ref,
    got_ref,
    weights_ref,
    transfer_ref,
    basis_ref,
    near_ref,
    x_ref,
    out_ref,
    rows_ref,
):
    fields = far_field(far_ref, coarse_ref, got_ref, weights_ref, transfer_ref, rows_ref)
    tiles = []
    parents = []
    for q in range(PARENTS):
        far = dot(spread_diagonal(fields[q]).astype(BF16), basis_ref[q])
        x = (near_ref[q].astype(F32) + far).astype(BF16)
        x_ref[q] = x
        leaf = diagonal(dot_nt(x, basis_ref[q]), OWN)
        tiles.append(to_tile(leaf))
        parents.append(dot(leaf.astype(BF16), transfer_ref[q]))
    tiles.append(to_tile(jnp.concatenate(parents, axis=1)))
    for t in range(TILES):
        for z in range(PLANES):
            out_ref[z, t] = tiles[t]


def last_field_kernel(
    far_ref, coarse_ref, got_ref, weights_ref, transfer_ref, out_ref, rows_ref
):
    fields = far_field(far_ref, coarse_ref, got_ref, weights_ref, transfer_ref, rows_ref)
    for q in range(PARENTS):
        out_ref[q] = to_tile(fields[q])


def whole_kernel(
    sub_ref,
    got0_ref,
    got1_ref,
    got2_ref,
    got3_ref,
    x_ref,
    low_ref,
    high_ref,
    first_ref,
    got_ref,
):
    in_order(sub_ref, [got0_ref, got1_ref, got2_ref, got3_ref], got_ref, PARENTS)
    sub = sub_ref[0]
    outs = []
    for q in range(PARENTS):
        parts = [got_ref[s, q].astype(F32) for s in range(SUBS)]
        for c in range(4):
            i = 4 * q + c
            rows = slice(c * OWN, (c + 1) * OWN)
            wide = jnp.concatenate([part[rows] for part in parts], axis=0)
            x = wide.astype(BF16)
            x_ref[i] = x
            if i < REACH:
                low_ref[i] = x
            if i >= LEAVES - REACH:
                high_ref[i - (LEAVES - REACH)] = x
            mine = wide[:, :ROWS]
            for s in range(1, SUBS):
                mine = jnp.where(sub == s, wide[:, s * ROWS : (s + 1) * ROWS], mine)
            outs.append(mine)
    first_ref[...] = jnp.transpose(jnp.stack(outs), (1, 0, 2)).astype(BF16)


def output_kernel(
    sub_ref, field0_ref, field1_ref, field2_ref, field3_ref, near_ref, basis_ref, out_ref, field_ref
):
    in_order(sub_ref, [field0_ref, field1_ref, field2_ref, field3_ref], field_ref, PARENTS)
    outs = []
    for q in range(PARENTS):
        tiles = [field_ref[s, q].astype(F32) for s in range(SUBS)]
        field = jnp.concatenate(
            [jnp.concatenate([t[:OWN], t[OWN:]], axis=1) for t in tiles], axis=0
        )
        far = dot(spread_diagonal(field).astype(BF16), basis_ref[q])
        for c in range(4):
            outs.append(near_ref[4 * q + c] + far[c * PROBES : (c + 1) * PROBES])
    out_ref[...] = jnp.transpose(jnp.stack(outs), (1, 0, 2)).astype(BF16)


def near_parts(index_ref, x_ref, low_ref, high_ref, blocks_ref, wide_ref, arrived):
    wide_ref[pl.ds(0, REACH)] = low_ref[...]
    wide_ref[pl.ds(REACH, LEAVES)] = x_ref[...]
    wide_ref[pl.ds(REACH + LEAVES, REACH)] = high_ref[...]
    wide_ref[2 * REACH + LEAVES] = jnp.zeros((PROBES, UNKNOWNS), BF16)
    for q in range(PARENTS):
        arrived(q)
        four = []
        for i in range(4 * q, 4 * q + 4):
            total = jnp.zeros((PROBES, ROWS), F32)
            for k in range(NEAR):
                total = total + dot_nt(wide_ref[index_ref[i, k]], blocks_ref[i, k])
            four.append(total)
        yield four


def near_sent_kernel(
    sub_ref,
    index_ref,
    x_ref,
    low_ref,
    high_ref,
    blocks_ref,
    basis_ref,
    out0_ref,
    out1_ref,
    out2_ref,
    out3_ref,
    wide_ref,
    four_ref,
    arrived,
):
    out_refs = [out0_ref, out1_ref, out2_ref, out3_ref]
    for j in range(LEAVES // 2):
        pair = jnp.concatenate([basis_ref[2 * j], basis_ref[2 * j + 1]], axis=1)
        for out_ref in out_refs:
            out_ref[pl.ds(16 * PARENTS + j * RANK, RANK), :] = pair
    parts = near_parts(index_ref, x_ref, low_ref, high_ref, blocks_ref, wide_ref, arrived)
    for q, four in enumerate(parts):
        four_ref[...] = jnp.concatenate(four, axis=1)
        for k, out_ref in enumerate(out_refs):
            tile = to_tile(four_ref[probes_of((sub_ref[0] + k) % SUBS), :])
            out_ref[pl.ds(16 * q, 16), :] = tile


def near_kernel(index_ref, x_ref, low_ref, high_ref, blocks_ref, out_ref, wide_ref, arrived):
    parts = near_parts(index_ref, x_ref, low_ref, high_ref, blocks_ref, wide_ref, arrived)
    for q, four in enumerate(parts):
        for c in range(4):
            out_ref[4 * q + c] = four[c]


def local(
    probes,
    near_blocks,
    leaf_cluster_basis,
    transfer,
    couplings,
    coarse_couplings,
    near_list,
    distant_interaction_list,
    coarse_list,
):
    groups = PLANES * PLANE
    in_plane = [[z * PLANE + m for m in range(PLANE)] for z in range(PLANES)]
    along_z = [[z * PLANE + m for z in range(PLANES)] for m in range(PLANE)]
    sub = lax.axis_index("sub").reshape(1)
    first_leaf = (lax.axis_index("leaf") * LEAVES).reshape(1)
    four_transfers = transfer.reshape(PARENTS, BRANCH * RANK, RANK)
    four_bases = leaf_cluster_basis.reshape(PARENTS, BRANCH * RANK, ROWS)

    def over_sub(pieces):
        return [pieces[0]] + [
            lax.ppermute(pieces[k], "sub", [(i, (i + k) % SUBS) for i in range(SUBS)])
            for k in range(1, SUBS)
        ]

    wanted, far_index, coarse_index, near_index = call(
        index_kernel,
        "index_tables",
        [
            ((PLANE, LANES), jnp.int32),
            (distant_interaction_list.shape, jnp.int32),
            (coarse_list.shape, jnp.int32),
            (near_list.shape, jnp.int32),
        ],
        of_kind("smem", first_leaf)
        + of_kind("hbm", distant_interaction_list, coarse_list, near_list),
    )
    wanted, sub = lax.optimization_barrier((wanted, sub))
    asked = lax.all_to_all(wanted, "leaf", 0, 0, axis_index_groups=in_plane, tiled=True)

    x_shape = (LEAVES, PROBES, UNKNOWNS)
    edge = (REACH, PROBES, UNKNOWNS)
    tile = (16, LANES)
    message = (PLANES, TILES) + tile
    rows_scratch = [pltpu.VMEM((GOT_ROWS + 1, OWN, LANES), F32)]

    wide_scratch = [pltpu.VMEM((LEAVES + 2 * REACH + 1, PROBES, UNKNOWNS), BF16)]

    def near_args(x, low, high):
        from_below = lax.ppermute(high, "leaf", [(i, i + 1) for i in range(groups - 1)])
        from_above = lax.ppermute(low, "leaf", [(i + 1, i) for i in range(groups - 1)])
        tables = of_kind("smem", near_index)
        return tables + of_kind("vmem", x, from_below, from_above) + of_kind("cut", near_blocks)

    def along(tiles):
        return lax.all_to_all(tiles, "leaf", 0, 0, axis_index_groups=along_z, tiled=True)

    def within(column):
        (chosen,) = call(
            choose_kernel,
            "choose_rows",
            [((PLANE, OUT_TILES) + tile, BF16)],
            of_kind("smem", asked) + of_kind("vmem", column),
            [pltpu.VMEM((PLANES * LEAVES, OWN, LANES), F32)],
        )
        got = lax.all_to_all(chosen, "leaf", 0, 0, axis_index_groups=in_plane, tiled=True)
        return got.reshape((PLANE * OUT_TILES,) + tile)

    packed = call(
        partial_kernel,
        "partial_sums",
        [((PACKED + TILES * 16, LANES), BF16)] * SUBS,
        of_kind("smem", sub) + of_kind("hbm", probes, four_bases, four_transfers),
        [pltpu.VMEM((TILES, PROBES, 4 * RANK), F32)],
    )
    pieces, asked = lax.optimization_barrier((over_sub(packed), asked))
    x0, low, high, tiles = call(
        first_kernel,
        "first_coefficients",
        [(x_shape, BF16), (edge, BF16), (edge, BF16), (message, BF16)],
        of_kind("smem", sub) + of_kind("vmem", *pieces),
        [pltpu.VMEM((SUBS, PACKED, LANES), BF16)],
    )
    column = along(tiles)
    sent = call(
        near_sent_kernel,
        "near_field_sent",
        [((SENT, LANES), BF16)] * SUBS,
        of_kind("smem", sub) + near_args(x0, low, high) + of_kind("hbm", leaf_cluster_basis),
        wide_scratch + [pltpu.VMEM((PROBES, 4 * ROWS), F32)],
        chunks=PARENTS,
    )
    column, sent, later = lax.optimization_barrier((column, sent, sub))
    got = within(column)
    (weights,) = call(
        weights_kernel,
        "join_couplings",
        [((PARENTS + 1, 4 * RANK, FAR * RANK), BF16)],
        of_kind("smem", later) + of_kind("hbm", couplings, coarse_couplings),
    )
    near1, basis = call(
        join_kernel,
        "join_near_basis",
        [((PARENTS, 4 * OWN, UNKNOWNS), BF16), ((PARENTS, 4 * RANK, UNKNOWNS), BF16)],
        of_kind("smem", sub) + of_kind("any", *over_sub(sent)),
        [pltpu.VMEM((SUBS, SENT, LANES), BF16)],
    )
    x1_own, tiles = call(
        middle_kernel,
        "middle",
        [((PARENTS, 4 * OWN, UNKNOWNS), BF16), (message, BF16)],
        of_kind("smem", far_index, coarse_index)
        + of_kind("vmem", got, weights)
        + of_kind("hbm", four_transfers)
        + of_kind("vmem", basis, near1),
        rows_scratch,
    )
    column = along(tiles)
    x1_parts = over_sub([x1_own] * SUBS)
    column, x1_parts = lax.optimization_barrier((column, x1_parts))
    got = within(column)
    x1, low, high, first = call(
        whole_kernel,
        "join_x1",
        [(x_shape, BF16), (edge, BF16), (edge, BF16), (probes.shape, BF16)],
        of_kind("smem", sub) + of_kind("any", *x1_parts),
        [pltpu.VMEM((SUBS, PARENTS, 4 * OWN, UNKNOWNS), BF16)],
    )
    (near2,) = call(
        near_kernel,
        "near_field",
        [((LEAVES, PROBES, ROWS), F32)],
        near_args(x1, low, high),
        wide_scratch,
        chunks=PARENTS,
    )
    got, near2 = lax.optimization_barrier((got, near2))
    (field,) = call(
        last_field_kernel,
        "last_field",
        [((PARENTS,) + tile, BF16)],
        of_kind("smem", far_index, coarse_index)
        + of_kind("vmem", got, weights)
        + of_kind("hbm", four_transfers),
        rows_scratch,
    )
    (second_apply,) = call(
        output_kernel,
        "output",
        [(probes.shape, BF16)],
        of_kind("smem", sub)
        + of_kind("vmem", *over_sub([field] * SUBS))
        + of_kind("any", near2)
        + of_kind("hbm", four_bases),
        [pltpu.VMEM((SUBS, PARENTS) + tile, BF16)],
    )
    return (first, second_apply)


def solution(mesh):
    return jax.shard_map(
        local,
        mesh=mesh,
        in_specs=(
            P(None, "leaf", "sub"),
            P("leaf", None, "sub", None),
            P("leaf", None, "sub"),
            P("leaf", None, None),
            P("leaf", None, None, None),
            P("leaf", None, None, None),
            P("leaf", None),
            P("leaf", None),
            P("leaf", None),
        ),
        out_specs=(P(None, "leaf", "sub"), P(None, "leaf", "sub")),
        check_vma=False,
    )
```

time: 353 us -> 121 us (0.34)
  the two profiles are of different devices: /device:TPU:96 before, /device:TPU:121 now
where the time goes in v3:
time: 121 us
  starting transfers between devices  51.5 us (43%)
  Pallas kernels  29.2 us (24%)
  waiting for transfers between devices  25.4 us (21%)
  blocking collectives  8.49 us (7%)
  local copies, waits for them, and re-layouts  4.94 us (4%)
    pallas_call x13, Pallas kernels, call(): pl.pallas_call(body, name=name, out_shape=[jax.ShapeDtypeStruct(s, d) for...  29.2 us
    ppermute x2, waiting for transfers between devices, near_args(): lax.ppermute(low, 'leaf', [(i + 1, i) for i in range(groups - 1)])  13.9 us
    ppermute x12, starting transfers between devices, over_sub(): lax.ppermute(pieces[k], 'sub', [(i, (i + k) % SUBS) for i in range(SUBS)])  13.5 us
    all_to_all x2, starting transfers between devices, along(): lax.all_to_all(tiles, 'leaf', 0, 0, axis_index_groups=along_z, tiled=True)  11.6 us
    ppermute x12, waiting for transfers between devices, over_sub(): lax.ppermute(pieces[k], 'sub', [(i, (i + k) % SUBS) for i in range(SUBS)])  11.4 us
    all_to_all x2, starting transfers between devices, within(): lax.all_to_all(chosen, 'leaf', 0, 0, axis_index_groups=in_plane, tiled=True)  11.4 us
    ppermute x2, starting transfers between devices, near_args(): lax.ppermute(high, 'leaf', [(i, i + 1) for i in range(groups - 1)])  10.9 us
    all_to_all x1, blocking collectives, local(): lax.all_to_all(wanted, 'leaf', 0, 0, axis_index_groups=in_plane, tiled=True)  8.49 us
  transfers between devices with their start and end apart: 20, of which 10 were waited for; matrix products, arithmetic and copies ran while one was open for 0% of the time, Pallas kernels for 11%

profile of v3, /device:TPU:121, one launch (start us, length us, event | category | flops | bytes accessed | tf_op | source)
XLA Modules:
  0.0 120.5 jit_solution(70562589939122291)
XLA Ops:
  1.7 1.9 %partial_sums.1 = (bf16[336,128]{1,0:T(8,128)(2,1)S(1)}, bf16[336,128]{1,0:T(8,128)(2,1)S(1)}, bf16[336,128]{1,0:T(8,128)(2,1)S(1)}, bf16[336,128]{1,0:T(8,128)(2,1)S(1)}) custom-call(s32[1]{0:T(128)} %bitcast.1.refs_0_, bf16[32,16,64]{2,1,0:T(8,128)(2,1)} %refs_1_.4, bf16[4,256,64]{2,1,0:T(8,128)(2,1)} %bitcast.18, bf16[4,256,64]{2,1,0:T(8,128)(2,1)} %bitcast.15), custom_call_target="tpu_custom_call" | custom-call | tf_op jit(solution)/shard_map/partial_sums/pallas_call | solution.py:74
  4.8 2.5 %collective-permute-start.1 = (bf16[336,128]{1,0:T(8,128)(2,1)S(1)}, bf16[336,128]{1,0:T(8,128)(2,1)S(1)}, u32[]{:S(2)}, u32[]{:S(2)}) collective-permute-start(bf16[336,128]{1,0:T(8,128)(2,1)S(1)} %get-tuple-element.52), channel_id=1, source_target_pairs={{0,2},{1,3},{2,0},{3,1},{4,6},{5,7},{6,4},{7,5},{8,10},{9,11},{10,... | collective-permute-start | bytes 258056 | tf_op jit(solution)/shard_map/ppermute | solution.py:452
  8.5 8.5 %all_to_all.32 = s32[8,1,128]{2,1,0:T(1,128)S(1)} all-to-all(s32[8,1,128]{2,1,0:T(1,128)S(1)} %bitcast.14), channel_id=1, replica_groups={{0,4,8,12,16,20,24,28},{32,36,40,44,48,52,56,60},{64,68,72,76,80,84,88,..., dimensions={0} | all-to-all | bytes 8192 | tf_op jit(solution)/shard_map/all_to_all | solution.py:469
  17.7 7.1 %all-to-all-start.1 = ((bf16[8,5,16,128]{3,2,1,0:T(8,128)(2,1)}), bf16[8,5,16,128]{3,2,1,0:T(8,128)(2,1)S(1)}, u32[]{:S(2)}, u32[]{:S(2)}) async-start(bf16[8,5,16,128]{3,2,1,0:T(8,128)(2,1)} %get-tuple-element.60), calls=%async_computation.1 | async-start | bytes 327680 | tf_op jit(solution)/shard_map/all_to_all | solution.py:486
  24.9 6.9 %collective-permute-start.3 = (bf16[4,32,256]{2,1,0:T(8,128)(2,1)S(1)}, bf16[4,32,256]{2,1,0:T(8,128)(2,1)S(1)}, u32[]{:S(2)}, u32[]{:S(2)}) collective-permute-start(bf16[4,32,256]{2,1,0:T(8,128)(2,1)S(1)} %get-tuple-element.63), channel_id=1, source_target_pairs={{0,4},{4,8},{8,12},{12,16},{16,20},{20,24},{24,28},{28,32},{32,36}... | collective-permute-start | bytes 196616 | tf_op jit(solution)/shard_map/ppermute | solution.py:480
  31.8 1.9 %collective-permute-start.4 = (bf16[4,32,256]{2,1,0:T(8,128)(2,1)S(1)}, bf16[4,32,256]{2,1,0:T(8,128)(2,1)S(1)}, u32[]{:S(2)}, u32[]{:S(2)}) collective-permute-start(bf16[4,32,256]{2,1,0:T(8,128)(2,1)S(1)} %get-tuple-element.64), channel_id=1, source_target_pairs={{4,0},{8,4},{12,8},{16,12},{20,16},{24,20},{28,24},{32,28},{36,32}... | collective-permute-start | bytes 196616 | tf_op jit(solution)/shard_map/ppermute | solution.py:481
  33.7 7.0 %collective-permute-done.4.refs_4_ = bf16[4,32,256]{2,1,0:T(8,128)(2,1)S(1)} collective-permute-done((bf16[4,32,256]{2,1,0:T(8,128)(2,1)S(1)}, bf16[4,32,256]{2,1,0:T(8,128)(2,1)S(1)}, u32[]{:S(2)}, u32[]{:S(2)}) %collective-permute-start.4) | collective-permute-done | bytes 65568 | tf_op jit(solution)/shard_map/ppermute | solution.py:481
  40.7 4.1 %near_field_sent.1 = (bf16[576,128]{1,0:T(8,128)(2,1)S(1)}, bf16[576,128]{1,0:T(8,128)(2,1)S(1)}, bf16[576,128]{1,0:T(8,128)(2,1)S(1)}, bf16[576,128]{1,0:T(8,128)(2,1)S(1)}) custom-call(s32[1]{0:T(128)} %bitcast.1.refs_0_, s32[16,9]{1,0:T(8,128)S(1)} %get-tuple-element.61.refs_1_.refs_0_, bf16[16,32,256]{2,1,0:T(8,128)(2,1)S(1)} %get-tuple-element.62.refs_2_, ...), custom_call_target="tpu_custom_call" | custom-call | tf_op jit(solution)/shard_map/near_field_sent/pallas_call | solution.py:74
  47.1 4.3 %all-to-all-start.2 = ((bf16[8,12,16,128]{3,2,1,0:T(8,128)(2,1)}), bf16[8,12,16,128]{3,2,1,0:T(8,128)(2,1)S(1)}, u32[]{:S(2)}, u32[]{:S(2)}) async-start(bf16[8,12,16,128]{3,2,1,0:T(8,128)(2,1)} %choose_rows.2), calls=%async_computation.2 | async-start | bytes 786432 | tf_op jit(solution)/shard_map/all_to_all | solution.py:496
  52.3 1.9 %collective-permute-start.7 = (bf16[576,128]{1,0:T(8,128)(2,1)S(1)}, bf16[576,128]{1,0:T(8,128)(2,1)S(1)}, u32[]{:S(2)}, u32[]{:S(2)}) collective-permute-start(bf16[576,128]{1,0:T(8,128)(2,1)S(1)} %get-tuple-element.74), channel_id=1, source_target_pairs={{0,3},{1,0},{2,1},{3,2},{4,7},{5,4},{6,5},{7,6},{8,11},{9,8},{10,9... | collective-permute-start | bytes 442376 | tf_op jit(solution)/shard_map/ppermute | solution.py:452
  54.2 3.3 %join_couplings.1.refs_3_ = bf16[5,256,1024]{2,1,0:T(8,128)(2,1)S(1)} custom-call(s32[1]{0:T(128)} %bitcast.1.refs_0_, bf16[16,16,64,64]{3,2,1,0:T(8,128)(2,1)} %refs_1_.5, bf16[4,16,64,64]{3,2,1,0:T(8,128)(2,1)} %refs_2_.3), custom_call_target="tpu_custom_call" | custom-call | tf_op jit(solution)/shard_map/join_couplings/pallas_call | solution.py:74
  57.4 3.4 %collective-permute-done.5.refs_2_ = bf16[576,128]{1,0:T(8,128)(2,1)S(1)} collective-permute-done((bf16[576,128]{1,0:T(8,128)(2,1)S(1)}, bf16[576,128]{1,0:T(8,128)(2,1)S(1)}, u32[]{:S(2)}, u32[]{:S(2)}) %collective-permute-start.5) | collective-permute-done | bytes 147488 | tf_op jit(solution)/shard_map/ppermute | solution.py:452
  63.7 4.0 %middle.1 = (bf16[4,32,256]{2,1,0:T(8,128)(2,1)S(1)}, bf16[8,5,16,128]{3,2,1,0:T(8,128)(2,1)S(1)}) custom-call(s32[16,16]{1,0:T(8,128)S(1)} %get-tuple-element.48.refs_0_, s32[4,16]{1,0:T(4,128)S(1)} %get-tuple-element.49.refs_1_, bf16[96,16,128]{2,1,0:T(8,128)(2,1)S(1)} %bitcast.10, bf16[5,256,1024]{2,1,0:T(8,128)(2,1)S(1)} %join_couplings.1.refs_3_, ...), custom_call_target="tpu_custom_call" | custom-call | tf_op jit(solution)/shard_map/middle/pallas_call | solution.py:74
  69.0 4.5 %all-to-all-start.3 = ((bf16[8,5,16,128]{3,2,1,0:T(8,128)(2,1)}), bf16[8,5,16,128]{3,2,1,0:T(8,128)(2,1)S(1)}, u32[]{:S(2)}, u32[]{:S(2)}) async-start(bf16[8,5,16,128]{3,2,1,0:T(8,128)(2,1)} %copy-done), calls=%async_computation.3 | async-start | bytes 327680 | tf_op jit(solution)/shard_map/all_to_all | solution.py:486
  73.5 3.0 %collective-permute-start.10 = (bf16[4,32,256]{2,1,0:T(8,128)(2,1)}, bf16[4,32,256]{2,1,0:T(8,128)(2,1)S(1)}, u32[]{:S(2)}, u32[]{:S(2)}) collective-permute-start(bf16[4,32,256]{2,1,0:T(8,128)(2,1)} %copy-done.5), channel_id=1, source_target_pairs={{0,3},{1,0},{2,1},{3,2},{4,7},{5,4},{6,5},{7,6},{8,11},{9,8},{10,9... | collective-permute-start | bytes 196616 | tf_op jit(solution)/shard_map/ppermute | solution.py:452
  78.6 2.9 %collective-permute-done.9.refs_3_ = bf16[4,32,256]{2,1,0:T(8,128)(2,1)S(1)} collective-permute-done((bf16[4,32,256]{2,1,0:T(8,128)(2,1)}, bf16[4,32,256]{2,1,0:T(8,128)(2,1)S(1)}, u32[]{:S(2)}, u32[]{:S(2)}) %collective-permute-start.9) | collective-permute-done | bytes 65568 | tf_op jit(solution)/shard_map/ppermute | solution.py:452
  83.3 7.1 %all-to-all-start.4 = ((bf16[8,12,16,128]{3,2,1,0:T(8,128)(2,1)}), bf16[8,12,16,128]{3,2,1,0:T(8,128)(2,1)S(1)}, u32[]{:S(2)}, u32[]{:S(2)}) async-start(bf16[8,12,16,128]{3,2,1,0:T(8,128)(2,1)} %choose_rows.3), calls=%async_computation.4 | async-start | bytes 786432 | tf_op jit(solution)/shard_map/all_to_all | solution.py:496
  92.8 4.0 %collective-permute-start.11 = (bf16[4,32,256]{2,1,0:T(8,128)(2,1)S(1)}, bf16[4,32,256]{2,1,0:T(8,128)(2,1)S(1)}, u32[]{:S(2)}, u32[]{:S(2)}) collective-permute-start(bf16[4,32,256]{2,1,0:T(8,128)(2,1)S(1)} %get-tuple-element.86), channel_id=1, source_target_pairs={{0,4},{4,8},{8,12},{12,16},{16,20},{20,24},{24,28},{28,32},{32,36}... | collective-permute-start | bytes 196616 | tf_op jit(solution)/shard_map/ppermute | solution.py:480
  96.8 2.1 %collective-permute-start.12 = (bf16[4,32,256]{2,1,0:T(8,128)(2,1)S(1)}, bf16[4,32,256]{2,1,0:T(8,128)(2,1)S(1)}, u32[]{:S(2)}, u32[]{:S(2)}) collective-permute-start(bf16[4,32,256]{2,1,0:T(8,128)(2,1)S(1)} %get-tuple-element.87), channel_id=1, source_target_pairs={{4,0},{8,4},{12,8},{16,12},{20,16},{24,20},{28,24},{32,28},{36,32}... | collective-permute-start | bytes 196616 | tf_op jit(solution)/shard_map/ppermute | solution.py:481
  98.9 7.0 %collective-permute-done.12.refs_3_ = bf16[4,32,256]{2,1,0:T(8,128)(2,1)S(1)} collective-permute-done((bf16[4,32,256]{2,1,0:T(8,128)(2,1)S(1)}, bf16[4,32,256]{2,1,0:T(8,128)(2,1)S(1)}, u32[]{:S(2)}, u32[]{:S(2)}) %collective-permute-start.12) | collective-permute-done | bytes 65568 | tf_op jit(solution)/shard_map/ppermute | solution.py:481
  106.5 3.7 %near_field.1.refs_5_ = f32[16,32,64]{2,1,0:T(8,128)S(1)} custom-call(s32[16,9]{1,0:T(8,128)S(1)} %copy-done.8, bf16[16,32,256]{2,1,0:T(8,128)(2,1)S(1)} %get-tuple-element.85.refs_1_, bf16[4,32,256]{2,1,0:T(8,128)(2,1)S(1)} %collective-permute-done.11.refs_2_, bf16[4,32,256]{2,1,0:T(8,128)(2,1)S(1)} %collective-permute-done.12.refs_3_, ...), custom_call_target="tpu_custom_call" | custom-call | tf_op jit(solution)/shard_map/near_field/pallas_call | solution.py:74
  110.3 2.9 %last_field.1.refs_1_ = bf16[4,16,128]{2,1,0:T(8,128)(2,1)S(1)} custom-call(s32[16,16]{1,0:T(8,128)S(1)} %get-tuple-element.48.refs_0_, s32[4,16]{1,0:T(4,128)S(1)} %get-tuple-element.49.refs_1_, bf16[96,16,128]{2,1,0:T(8,128)(2,1)S(1)} %bitcast.11, bf16[5,256,1024]{2,1,0:T(8,128)(2,1)S(1)} %join_couplings.1.refs_3_, bf16[4,256,64]{2,1,0:T(8,128)(2,1)} %bitcast.17), custom_call_target="tpu_custom_call" | custom-call | tf_op jit(solution)/shard_map/last_field/pallas_call | solution.py:74
  115.8 2.1 %collective-permute-done.14.refs_3_ = bf16[4,16,128]{2,1,0:T(8,128)(2,1)S(1)} collective-permute-done((bf16[4,16,128]{2,1,0:T(8,128)(2,1)S(1)}, bf16[4,16,128]{2,1,0:T(8,128)(2,1)S(1)}, u32[]{:S(2)}, u32[]{:S(2)}) %collective-permute-start.14) | collective-permute-done | bytes 16416 | tf_op jit(solution)/shard_map/ppermute | solution.py:452
  118.5 1.9 %output.1 = bf16[32,16,64]{2,1,0:T(8,128)(2,1)} custom-call(s32[1]{0:T(128)} %bitcast.1.refs_0_, bf16[4,16,128]{2,1,0:T(8,128)(2,1)S(1)} %last_field.1.refs_1_, bf16[4,16,128]{2,1,0:T(8,128)(2,1)S(1)} %collective-permute-done.13.refs_2_, bf16[4,16,128]{2,1,0:T(8,128)(2,1)S(1)} %collective-permute-done.14.refs_3_, ...), custom_call_target="tpu_custom_call" | custom-call | tf_op jit(solution)/shard_map/output/pallas_call | solution.py:74
  (48 shorter events, 21.7 us)
Async XLA Ops:
  1.7 50.6 %copy-start.7 = (s32[16,9]{1,0:T(8,128)}, s32[16,9]{1,0:T(8,128)S(1)}, u32[]{:S(2)}) copy-start(s32[16,9]{1,0:T(8,128)S(1)} %get-tuple-element.61.refs_1_.refs_0_) | copy-start | bytes 1732
  3.6 13.4 %collective-permute-start = (bf16[336,128]{1,0:T(8,128)(2,1)S(1)}, bf16[336,128]{1,0:T(8,128)(2,1)S(1)}, u32[]{:S(2)}, u32[]{:S(2)}) collective-permute-start(bf16[336,128]{1,0:T(8,128)(2,1)S(1)} %get-tuple-element.51), channel_id=1, source_target_pairs={{0,1},{1,2},{2,3},{3,0},{4,5},{5,6},{6,7},{7,4},{8,9},{9,10},{10,1... | collective-permute-start | bytes 258056 | tf_op jit(solution)/shard_map/ppermute | solution.py:452
  4.8 12.1 %collective-permute-start.1 = (bf16[336,128]{1,0:T(8,128)(2,1)S(1)}, bf16[336,128]{1,0:T(8,128)(2,1)S(1)}, u32[]{:S(2)}, u32[]{:S(2)}) collective-permute-start(bf16[336,128]{1,0:T(8,128)(2,1)S(1)} %get-tuple-element.52), channel_id=1, source_target_pairs={{0,2},{1,3},{2,0},{3,1},{4,6},{5,7},{6,4},{7,5},{8,10},{9,11},{10,... | collective-permute-start | bytes 258056 | tf_op jit(solution)/shard_map/ppermute | solution.py:452
  7.3 9.7 %collective-permute-start.2 = (bf16[336,128]{1,0:T(8,128)(2,1)S(1)}, bf16[336,128]{1,0:T(8,128)(2,1)S(1)}, u32[]{:S(2)}, u32[]{:S(2)}) collective-permute-start(bf16[336,128]{1,0:T(8,128)(2,1)S(1)} %get-tuple-element.53), channel_id=1, source_target_pairs={{0,3},{1,0},{2,1},{3,2},{4,7},{5,4},{6,5},{7,6},{8,11},{9,8},{10,9... | collective-permute-start | bytes 258056 | tf_op jit(solution)/shard_map/ppermute | solution.py:452
  17.7 27.8 %all-to-all-start.1 = ((bf16[8,5,16,128]{3,2,1,0:T(8,128)(2,1)}), bf16[8,5,16,128]{3,2,1,0:T(8,128)(2,1)S(1)}, u32[]{:S(2)}, u32[]{:S(2)}) async-start(bf16[8,5,16,128]{3,2,1,0:T(8,128)(2,1)} %get-tuple-element.60), calls=%async_computation.1 | async-start | bytes 327680 | tf_op jit(solution)/shard_map/all_to_all | solution.py:486
  24.9 8.9 %collective-permute-start.3 = (bf16[4,32,256]{2,1,0:T(8,128)(2,1)S(1)}, bf16[4,32,256]{2,1,0:T(8,128)(2,1)S(1)}, u32[]{:S(2)}, u32[]{:S(2)}) collective-permute-start(bf16[4,32,256]{2,1,0:T(8,128)(2,1)S(1)} %get-tuple-element.63), channel_id=1, source_target_pairs={{0,4},{4,8},{8,12},{12,16},{16,20},{20,24},{24,28},{28,32},{32,36}... | collective-permute-start | bytes 196616 | tf_op jit(solution)/shard_map/ppermute | solution.py:480
  31.8 8.9 %collective-permute-start.4 = (bf16[4,32,256]{2,1,0:T(8,128)(2,1)S(1)}, bf16[4,32,256]{2,1,0:T(8,128)(2,1)S(1)}, u32[]{:S(2)}, u32[]{:S(2)}) collective-permute-start(bf16[4,32,256]{2,1,0:T(8,128)(2,1)S(1)} %get-tuple-element.64), channel_id=1, source_target_pairs={{4,0},{8,4},{12,8},{16,12},{20,16},{24,20},{28,24},{32,28},{36,32}... | collective-permute-start | bytes 196616 | tf_op jit(solution)/shard_map/ppermute | solution.py:481
  47.1 15.8 %all-to-all-start.2 = ((bf16[8,12,16,128]{3,2,1,0:T(8,128)(2,1)}), bf16[8,12,16,128]{3,2,1,0:T(8,128)(2,1)S(1)}, u32[]{:S(2)}, u32[]{:S(2)}) async-start(bf16[8,12,16,128]{3,2,1,0:T(8,128)(2,1)} %choose_rows.2), calls=%async_computation.2 | async-start | bytes 786432 | tf_op jit(solution)/shard_map/all_to_all | solution.py:496
  51.4 9.8 %copy-start.2 = (bf16[576,128]{1,0:T(8,128)(2,1)S(1)}, bf16[576,128]{1,0:T(8,128)(2,1)}, u32[]{:S(2)}) copy-start(bf16[576,128]{1,0:T(8,128)(2,1)} %copy-done.1) | copy-start | bytes 442372
  51.4 9.5 %collective-permute-start.5 = (bf16[576,128]{1,0:T(8,128)(2,1)S(1)}, bf16[576,128]{1,0:T(8,128)(2,1)S(1)}, u32[]{:S(2)}, u32[]{:S(2)}) collective-permute-start(bf16[576,128]{1,0:T(8,128)(2,1)S(1)} %get-tuple-element.72), channel_id=1, source_target_pairs={{0,1},{1,2},{2,3},{3,0},{4,5},{5,6},{6,7},{7,4},{8,9},{9,10},{10,1... | collective-permute-start | bytes 442376 | tf_op jit(solution)/shard_map/ppermute | solution.py:452
  51.7 9.2 %collective-permute-start.6 = (bf16[576,128]{1,0:T(8,128)(2,1)S(1)}, bf16[576,128]{1,0:T(8,128)(2,1)S(1)}, u32[]{:S(2)}, u32[]{:S(2)}) collective-permute-start(bf16[576,128]{1,0:T(8,128)(2,1)S(1)} %get-tuple-element.73), channel_id=1, source_target_pairs={{0,2},{1,3},{2,0},{3,1},{4,6},{5,7},{6,4},{7,5},{8,10},{9,11},{10,... | collective-permute-start | bytes 442376 | tf_op jit(solution)/shard_map/ppermute | solution.py:452
  52.3 8.9 %collective-permute-start.7 = (bf16[576,128]{1,0:T(8,128)(2,1)S(1)}, bf16[576,128]{1,0:T(8,128)(2,1)S(1)}, u32[]{:S(2)}, u32[]{:S(2)}) collective-permute-start(bf16[576,128]{1,0:T(8,128)(2,1)S(1)} %get-tuple-element.74), channel_id=1, source_target_pairs={{0,3},{1,0},{2,1},{3,2},{4,7},{5,4},{6,5},{7,6},{8,11},{9,8},{10,9... | collective-permute-start | bytes 442376 | tf_op jit(solution)/shard_map/ppermute | solution.py:452
  62.9 0.8 copy-start.4
  69.0 12.8 %all-to-all-start.3 = ((bf16[8,5,16,128]{3,2,1,0:T(8,128)(2,1)}), bf16[8,5,16,128]{3,2,1,0:T(8,128)(2,1)S(1)}, u32[]{:S(2)}, u32[]{:S(2)}) async-start(bf16[8,5,16,128]{3,2,1,0:T(8,128)(2,1)} %copy-done), calls=%async_computation.3 | async-start | bytes 327680 | tf_op jit(solution)/shard_map/all_to_all | solution.py:486
  73.5 5.1 %collective-permute-start.10 = (bf16[4,32,256]{2,1,0:T(8,128)(2,1)}, bf16[4,32,256]{2,1,0:T(8,128)(2,1)S(1)}, u32[]{:S(2)}, u32[]{:S(2)}) collective-permute-start(bf16[4,32,256]{2,1,0:T(8,128)(2,1)} %copy-done.5), channel_id=1, source_target_pairs={{0,3},{1,0},{2,1},{3,2},{4,7},{5,4},{6,5},{7,6},{8,11},{9,8},{10,9... | collective-permute-start | bytes 196616 | tf_op jit(solution)/shard_map/ppermute | solution.py:452
  76.5 4.9 %collective-permute-start.9 = (bf16[4,32,256]{2,1,0:T(8,128)(2,1)}, bf16[4,32,256]{2,1,0:T(8,128)(2,1)S(1)}, u32[]{:S(2)}, u32[]{:S(2)}) collective-permute-start(bf16[4,32,256]{2,1,0:T(8,128)(2,1)} %copy-done.5), channel_id=1, source_target_pairs={{0,2},{1,3},{2,0},{3,1},{4,6},{5,7},{6,4},{7,5},{8,10},{9,11},{10,... | collective-permute-start | bytes 196616 | tf_op jit(solution)/shard_map/ppermute | solution.py:452
  76.5 5.2 %collective-permute-start.8 = (bf16[4,32,256]{2,1,0:T(8,128)(2,1)}, bf16[4,32,256]{2,1,0:T(8,128)(2,1)S(1)}, u32[]{:S(2)}, u32[]{:S(2)}) collective-permute-start(bf16[4,32,256]{2,1,0:T(8,128)(2,1)} %copy-done.5), channel_id=1, source_target_pairs={{0,1},{1,2},{2,3},{3,0},{4,5},{5,6},{6,7},{7,4},{8,9},{9,10},{10,1... | collective-permute-start | bytes 196616 | tf_op jit(solution)/shard_map/ppermute | solution.py:452
  83.3 27.0 %all-to-all-start.4 = ((bf16[8,12,16,128]{3,2,1,0:T(8,128)(2,1)}), bf16[8,12,16,128]{3,2,1,0:T(8,128)(2,1)S(1)}, u32[]{:S(2)}, u32[]{:S(2)}) async-start(bf16[8,12,16,128]{3,2,1,0:T(8,128)(2,1)} %choose_rows.3), calls=%async_computation.4 | async-start | bytes 786432 | tf_op jit(solution)/shard_map/all_to_all | solution.py:496
  90.4 0.8 copy-start.6
  92.8 6.1 %collective-permute-start.11 = (bf16[4,32,256]{2,1,0:T(8,128)(2,1)S(1)}, bf16[4,32,256]{2,1,0:T(8,128)(2,1)S(1)}, u32[]{:S(2)}, u32[]{:S(2)}) collective-permute-start(bf16[4,32,256]{2,1,0:T(8,128)(2,1)S(1)} %get-tuple-element.86), channel_id=1, source_target_pairs={{0,4},{4,8},{8,12},{12,16},{16,20},{20,24},{24,28},{28,32},{32,36}... | collective-permute-start | bytes 196616 | tf_op jit(solution)/shard_map/ppermute | solution.py:480
  96.8 9.1 %collective-permute-start.12 = (bf16[4,32,256]{2,1,0:T(8,128)(2,1)S(1)}, bf16[4,32,256]{2,1,0:T(8,128)(2,1)S(1)}, u32[]{:S(2)}, u32[]{:S(2)}) collective-permute-start(bf16[4,32,256]{2,1,0:T(8,128)(2,1)S(1)} %get-tuple-element.87), channel_id=1, source_target_pairs={{4,0},{8,4},{12,8},{16,12},{20,16},{24,20},{28,24},{32,28},{36,32}... | collective-permute-start | bytes 196616 | tf_op jit(solution)/shard_map/ppermute | solution.py:481
  113.2 2.7 %collective-permute-start.15 = (bf16[4,16,128]{2,1,0:T(8,128)(2,1)S(1)}, bf16[4,16,128]{2,1,0:T(8,128)(2,1)S(1)}, u32[]{:S(2)}, u32[]{:S(2)}) collective-permute-start(bf16[4,16,128]{2,1,0:T(8,128)(2,1)S(1)} %last_field.1.refs_1_), channel_id=1, source_target_pairs={{0,3},{1,0},{2,1},{3,2},{4,7},{5,4},{6,5},{7,6},{8,11},{9,8},{10,9... | collective-permute-start | bytes 49160 | tf_op jit(solution)/shard_map/ppermute | solution.py:452
  113.8 4.1 %collective-permute-start.14 = (bf16[4,16,128]{2,1,0:T(8,128)(2,1)S(1)}, bf16[4,16,128]{2,1,0:T(8,128)(2,1)S(1)}, u32[]{:S(2)}, u32[]{:S(2)}) collective-permute-start(bf16[4,16,128]{2,1,0:T(8,128)(2,1)S(1)} %last_field.1.refs_1_), channel_id=1, source_target_pairs={{0,2},{1,3},{2,0},{3,1},{4,6},{5,7},{6,4},{7,5},{8,10},{9,11},{10,... | collective-permute-start | bytes 49160 | tf_op jit(solution)/shard_map/ppermute | solution.py:452
  114.7 3.8 %collective-permute-start.13 = (bf16[4,16,128]{2,1,0:T(8,128)(2,1)S(1)}, bf16[4,16,128]{2,1,0:T(8,128)(2,1)S(1)}, u32[]{:S(2)}, u32[]{:S(2)}) collective-permute-start(bf16[4,16,128]{2,1,0:T(8,128)(2,1)S(1)} %last_field.1.refs_1_), channel_id=1, source_target_pairs={{0,1},{1,2},{2,3},{3,0},{4,5},{5,6},{6,7},{7,4},{8,9},{9,10},{10,1... | collective-permute-start | bytes 49160 | tf_op jit(solution)/shard_map/ppermute | solution.py:452
  (5 other events, 3.3 us)

commit v4 on v3

--- a/solution.py
+++ b/solution.py
@@ -41,43 +41,69 @@
     return lax.dot_general(x, y, NT, preferred_element_type=F32)
 
 
-def call(kernel, name, outs, args, scratch=(), chunks=1):
+class Arriving:
+    def __init__(self, source, target, sems, parts):
+        size = target.shape[0] // parts
+        self.target, self.size, self.pending = target, size, {}
+        for c in range(parts):
+            part = pl.ds(c * size, size)
+            copy = pltpu.make_async_copy(source.at[part], target.at[part], sems.at[c])
+            copy.start()
+            self.pending[c] = copy
+
+    def finish(self, part=None):
+        for c in list(self.pending) if part is None else [part]:
+            if c in self.pending:
+                self.pending.pop(c).wait()
+
+    def __getitem__(self, index):
+        first = index[0] if isinstance(index, tuple) else index
+        self.finish(first // self.size if isinstance(first, int) else None)
+        return self.target[index]
+
+
+def call(kernel, name, outs, args, scratch=()):
     spaces = {"smem": pltpu.SMEM, "vmem": pltpu.VMEM, "hbm": pltpu.HBM, "cut": pltpu.HBM, "any": pl.ANY}
-    moved = [j for j, (kind, _) in enumerate(args) if kind in ("hbm", "any", "cut")]
+    parts = {"hbm": 1, "any": 1, "cut": 4}
+    moved = [j for j, (kind, _) in enumerate(args) if kind in parts]
+    away = [j for j, out in enumerate(outs) if len(out) == 3]
+    scratch = list(scratch)
     buffers = [pltpu.VMEM(args[j][1].shape, args[j][1].dtype) for j in moved]
-    scratch = list(scratch)
+    buffers += [pltpu.VMEM(outs[j][0], outs[j][1]) for j in away]
 
     def body(*refs):
         refs = list(refs)
         sems = refs.pop()
         front = len(args) + len(outs) + len(scratch)
-        whole, parts = [], []
+        used, arriving = 0, []
         for n, j in enumerate(moved):
-            source, target = refs[j], refs[front + n]
-            if args[j][0] == "cut":
-                size = target.shape[0] // chunks
-                for c in range(chunks):
-                    part = pl.ds(c * size, size)
-                    parts.append(
-                        pltpu.make_async_copy(source.at[part], target.at[part], sems.at[len(moved) + c])
-                    )
-            else:
-                whole.append(pltpu.make_async_copy(source, target, sems.at[n]))
-            refs[j] = target
-        for copy in whole + parts:
+            count = parts[args[j][0]]
+            refs[j] = Arriving(refs[j], refs[front + n], sems.at[pl.ds(used, count)], count)
+            arriving.append(refs[j])
+            used += count
+        leaving = []
+        for n, j in enumerate(away):
+            target, source = refs[len(args) + j], refs[front + len(moved) + n]
+            leaving.append(pltpu.make_async_copy(source, target, sems.at[used + n]))
+            refs[len(args) + j] = source
+        kernel(*refs[:front])
+        for copy in leaving:
             copy.start()
-        for copy in whole:
+        for buffer in arriving:
+            buffer.finish()
+        for copy in leaving:
             copy.wait()
-        extra = [lambda c: parts[c].wait()] if parts else []
-        kernel(*refs[:front], *extra)
-
+
+    count = sum(parts[args[j][0]] for j in moved) + len(away)
     return pl.pallas_call(
         body,
         name=name,
-        out_shape=[jax.ShapeDtypeStruct(s, d) for s, d in outs],
+        out_shape=[jax.ShapeDtypeStruct(out[0], out[1]) for out in outs],
         in_specs=[pl.BlockSpec(memory_space=spaces[kind]) for kind, _ in args],
-        out_specs=[pl.BlockSpec(memory_space=pltpu.VMEM)] * len(outs),
-        scratch_shapes=scratch + buffers + [pltpu.SemaphoreType.DMA((len(moved) + chunks,))],
+        out_specs=[
+            pl.BlockSpec(memory_space=pltpu.HBM if j in away else pltpu.VMEM) for j in range(len(outs))
+        ],
+        scratch_shapes=scratch + buffers + [pltpu.SemaphoreType.DMA((max(count, 1),))],
         compiler_params=pltpu.CompilerParams(vmem_limit_bytes=VMEM_LIMIT),
     )(*[
         pltpu.with_memory_space_constraint(array, pltpu.HBM) if kind in ("hbm", "cut") else array
@@ -115,9 +141,7 @@
     return tile[h * OWN : (h + 1) * OWN, g * RANK : (g + 1) * RANK]
 
 
-def index_kernel(
-    first_ref, far_ref, coarse_ref, near_ref, wanted_ref, far_out_ref, coarse_out_ref, near_out_ref
-):
+def index_kernel(_, far_ref, coarse_ref, wanted_ref, far_out_ref, coarse_out_ref):
     groups = PLANES * PLANE
     group = lax.broadcasted_iota(jnp.int32, (groups, FAR), 0)
     named = far_ref[...]
@@ -147,8 +171,6 @@
     owner = coarse >> 2
     row = (owner & (PLANE - 1)) * (4 * OUT_TILES) + 4 * LEAF_OUT + (owner >> 3) * PARENTS
     coarse_out_ref[...] = jnp.where(coarse >= 0, row + (coarse & (PARENTS - 1)), GOT_ROWS)
-    near = near_ref[...]
-    near_out_ref[...] = jnp.where(near >= 0, near - first_ref[0] + REACH, LEAVES + 2 * REACH)
 
 
 def partial_kernel(
@@ -182,7 +204,7 @@
 
 def in_order(sub_ref, piece_refs, slots_ref, rows):
     for k, piece_ref in enumerate(piece_refs):
-        slots_ref[(sub_ref[0] + SUBS - k) % SUBS] = piece_ref[:rows]
+        slots_ref[(sub_ref[0] + SUBS - k) % SUBS] = piece_ref[pl.ds(0, rows)]
 
 
 def first_kernel(
@@ -376,25 +398,30 @@
     out_ref[...] = jnp.transpose(jnp.stack(outs), (1, 0, 2)).astype(BF16)
 
 
-def near_parts(index_ref, x_ref, low_ref, high_ref, blocks_ref, wide_ref, arrived):
+def near_parts(first_ref, list_ref, x_ref, low_ref, high_ref, blocks_ref, wide_ref):
     wide_ref[pl.ds(0, REACH)] = low_ref[...]
     wide_ref[pl.ds(REACH, LEAVES)] = x_ref[...]
     wide_ref[pl.ds(REACH + LEAVES, REACH)] = high_ref[...]
     wide_ref[2 * REACH + LEAVES] = jnp.zeros((PROBES, UNKNOWNS), BF16)
-    for q in range(PARENTS):
-        arrived(q)
+
+    def of_slot(i, k):
+        leaf = list_ref[i, k]
+        place = jnp.where(leaf >= 0, leaf - first_ref[0] + REACH, LEAVES + 2 * REACH)
+        return wide_ref[place]
+
+    for q in range(PARENTS):
         four = []
         for i in range(4 * q, 4 * q + 4):
-            total = jnp.zeros((PROBES, ROWS), F32)
-            for k in range(NEAR):
-                total = total + dot_nt(wide_ref[index_ref[i, k]], blocks_ref[i, k])
-            four.append(total)
+            x = jnp.concatenate([of_slot(i, k) for k in range(NEAR)], axis=1)
+            blocks = jnp.concatenate([blocks_ref[i, k] for k in range(NEAR)], axis=1)
+            four.append(dot_nt(x, blocks))
         yield four
 
 
 def near_sent_kernel(
     sub_ref,
-    index_ref,
+    first_ref,
+    list_ref,
     x_ref,
     low_ref,
     high_ref,
@@ -406,23 +433,22 @@
     out3_ref,
     wide_ref,
     four_ref,
-    arrived,
 ):
     out_refs = [out0_ref, out1_ref, out2_ref, out3_ref]
-    for j in range(LEAVES // 2):
-        pair = jnp.concatenate([basis_ref[2 * j], basis_ref[2 * j + 1]], axis=1)
-        for out_ref in out_refs:
-            out_ref[pl.ds(16 * PARENTS + j * RANK, RANK), :] = pair
-    parts = near_parts(index_ref, x_ref, low_ref, high_ref, blocks_ref, wide_ref, arrived)
+    parts = near_parts(first_ref, list_ref, x_ref, low_ref, high_ref, blocks_ref, wide_ref)
     for q, four in enumerate(parts):
         four_ref[...] = jnp.concatenate(four, axis=1)
         for k, out_ref in enumerate(out_refs):
             tile = to_tile(four_ref[probes_of((sub_ref[0] + k) % SUBS), :])
             out_ref[pl.ds(16 * q, 16), :] = tile
-
-
-def near_kernel(index_ref, x_ref, low_ref, high_ref, blocks_ref, out_ref, wide_ref, arrived):
-    parts = near_parts(index_ref, x_ref, low_ref, high_ref, blocks_ref, wide_ref, arrived)
+    for j in range(LEAVES // 2):
+        pair = jnp.concatenate([basis_ref[2 * j], basis_ref[2 * j + 1]], axis=1)
+        for out_ref in out_refs:
+            out_ref[pl.ds(16 * PARENTS + j * RANK, RANK), :] = pair
+
+
+def near_kernel(first_ref, list_ref, x_ref, low_ref, high_ref, blocks_ref, out_ref, wide_ref):
+    parts = near_parts(first_ref, list_ref, x_ref, low_ref, high_ref, blocks_ref, wide_ref)
     for q, four in enumerate(parts):
         for c in range(4):
             out_ref[4 * q + c] = four[c]
@@ -453,107 +479,101 @@
             for k in range(1, SUBS)
         ]
 
-    wanted, far_index, coarse_index, near_index = call(
+    x_shape = (LEAVES, PROBES, UNKNOWNS)
+    edge = (REACH, PROBES, UNKNOWNS)
+    tile = (16, LANES)
+    message = (PLANES, TILES) + tile
+    rows_scratch = [pltpu.VMEM((GOT_ROWS + 1, OWN, LANES), F32)]
+
+    wide_scratch = [pltpu.VMEM((LEAVES + 2 * REACH + 1, PROBES, UNKNOWNS), BF16)]
+
+    def near_args(x, low, high):
+        from_below = lax.ppermute(high, "leaf", [(i, i + 1) for i in range(groups - 1)])
+        from_above = lax.ppermute(low, "leaf", [(i + 1, i) for i in range(groups - 1)])
+        tables = of_kind("smem", first_leaf, near_list)
+        return tables + of_kind("vmem", x, from_below, from_above) + of_kind("cut", near_blocks)
+
+    def along(tiles):
+        return lax.all_to_all(tiles, "leaf", 0, 0, axis_index_groups=along_z, tiled=True)
+
+    def within(column, asked):
+        (chosen,) = call(
+            choose_kernel,
+            "choose_rows",
+            [((PLANE, OUT_TILES) + tile, BF16, True)],
+            of_kind("smem", asked) + of_kind("vmem", column),
+            [pltpu.VMEM((PLANES * LEAVES, OWN, LANES), F32)],
+        )
+        got = lax.all_to_all(chosen, "leaf", 0, 0, axis_index_groups=in_plane, tiled=True)
+        return got.reshape((PLANE * OUT_TILES,) + tile)
+
+    packed = call(
+        partial_kernel,
+        "partial_sums",
+        [((PACKED + TILES * 16, LANES), BF16)] * SUBS,
+        of_kind("smem", sub) + of_kind("hbm", probes, four_bases, four_transfers),
+        [pltpu.VMEM((TILES, PROBES, 4 * RANK), F32)],
+    )
+    first_leaf, packed = lax.optimization_barrier((first_leaf, packed))
+    wanted, far_index, coarse_index = call(
         index_kernel,
         "index_tables",
         [
             ((PLANE, LANES), jnp.int32),
             (distant_interaction_list.shape, jnp.int32),
             (coarse_list.shape, jnp.int32),
-            (near_list.shape, jnp.int32),
         ],
-        of_kind("smem", first_leaf)
-        + of_kind("hbm", distant_interaction_list, coarse_list, near_list),
-    )
-    wanted, sub = lax.optimization_barrier((wanted, sub))
-    asked = lax.all_to_all(wanted, "leaf", 0, 0, axis_index_groups=in_plane, tiled=True)
-
-    x_shape = (LEAVES, PROBES, UNKNOWNS)
-    edge = (REACH, PROBES, UNKNOWNS)
-    tile = (16, LANES)
-    message = (PLANES, TILES) + tile
-    rows_scratch = [pltpu.VMEM((GOT_ROWS + 1, OWN, LANES), F32)]
-
-    wide_scratch = [pltpu.VMEM((LEAVES + 2 * REACH + 1, PROBES, UNKNOWNS), BF16)]
-
-    def near_args(x, low, high):
-        from_below = lax.ppermute(high, "leaf", [(i, i + 1) for i in range(groups - 1)])
-        from_above = lax.ppermute(low, "leaf", [(i + 1, i) for i in range(groups - 1)])
-        tables = of_kind("smem", near_index)
-        return tables + of_kind("vmem", x, from_below, from_above) + of_kind("cut", near_blocks)
-
-    def along(tiles):
-        return lax.all_to_all(tiles, "leaf", 0, 0, axis_index_groups=along_z, tiled=True)
-
-    def within(column):
-        (chosen,) = call(
-            choose_kernel,
-            "choose_rows",
-            [((PLANE, OUT_TILES) + tile, BF16)],
-            of_kind("smem", asked) + of_kind("vmem", column),
-            [pltpu.VMEM((PLANES * LEAVES, OWN, LANES), F32)],
-        )
-        got = lax.all_to_all(chosen, "leaf", 0, 0, axis_index_groups=in_plane, tiled=True)
-        return got.reshape((PLANE * OUT_TILES,) + tile)
-
-    packed = call(
-        partial_kernel,
-        "partial_sums",
-        [((PACKED + TILES * 16, LANES), BF16)] * SUBS,
-        of_kind("smem", sub) + of_kind("hbm", probes, four_bases, four_transfers),
-        [pltpu.VMEM((TILES, PROBES, 4 * RANK), F32)],
-    )
-    pieces, asked = lax.optimization_barrier((over_sub(packed), asked))
+        of_kind("smem", first_leaf) + of_kind("hbm", distant_interaction_list, coarse_list),
+    )
+    pieces, wanted = lax.optimization_barrier((over_sub(packed), wanted))
     x0, low, high, tiles = call(
         first_kernel,
         "first_coefficients",
-        [(x_shape, BF16), (edge, BF16), (edge, BF16), (message, BF16)],
+        [(x_shape, BF16), (edge, BF16), (edge, BF16), (message, BF16, True)],
         of_kind("smem", sub) + of_kind("vmem", *pieces),
         [pltpu.VMEM((SUBS, PACKED, LANES), BF16)],
     )
-    column = along(tiles)
+    column, wanted = lax.optimization_barrier((along(tiles), wanted))
+    asked = lax.all_to_all(wanted, "leaf", 0, 0, axis_index_groups=in_plane, tiled=True)
     sent = call(
         near_sent_kernel,
         "near_field_sent",
-        [((SENT, LANES), BF16)] * SUBS,
+        [((SENT, LANES), BF16, True)] + [((SENT, LANES), BF16)] * (SUBS - 1),
         of_kind("smem", sub) + near_args(x0, low, high) + of_kind("hbm", leaf_cluster_basis),
         wide_scratch + [pltpu.VMEM((PROBES, 4 * ROWS), F32)],
-        chunks=PARENTS,
     )
     column, sent, later = lax.optimization_barrier((column, sent, sub))
-    got = within(column)
+    got = within(column, asked)
     (weights,) = call(
         weights_kernel,
         "join_couplings",
-        [((PARENTS + 1, 4 * RANK, FAR * RANK), BF16)],
-        of_kind("smem", later) + of_kind("hbm", couplings, coarse_couplings),
+        [((PARENTS + 1, 4 * RANK, FAR * RANK), BF16, True)],
+        of_kind("smem", later) + of_kind("cut", couplings, coarse_couplings),
     )
     near1, basis = call(
         join_kernel,
         "join_near_basis",
-        [((PARENTS, 4 * OWN, UNKNOWNS), BF16), ((PARENTS, 4 * RANK, UNKNOWNS), BF16)],
+        [((PARENTS, 4 * OWN, UNKNOWNS), BF16, True), ((PARENTS, 4 * RANK, UNKNOWNS), BF16, True)],
         of_kind("smem", sub) + of_kind("any", *over_sub(sent)),
         [pltpu.VMEM((SUBS, SENT, LANES), BF16)],
     )
     x1_own, tiles = call(
         middle_kernel,
         "middle",
-        [((PARENTS, 4 * OWN, UNKNOWNS), BF16), (message, BF16)],
+        [((PARENTS, 4 * OWN, UNKNOWNS), BF16, True), (message, BF16, True)],
         of_kind("smem", far_index, coarse_index)
-        + of_kind("vmem", got, weights)
+        + of_kind("vmem", got)
+        + of_kind("any", weights)
         + of_kind("hbm", four_transfers)
-        + of_kind("vmem", basis, near1),
+        + of_kind("any", basis, near1),
         rows_scratch,
     )
-    column = along(tiles)
-    x1_parts = over_sub([x1_own] * SUBS)
-    column, x1_parts = lax.optimization_barrier((column, x1_parts))
-    got = within(column)
+    got = within(along(tiles), asked)
     x1, low, high, first = call(
         whole_kernel,
         "join_x1",
         [(x_shape, BF16), (edge, BF16), (edge, BF16), (probes.shape, BF16)],
-        of_kind("smem", sub) + of_kind("any", *x1_parts),
+        of_kind("smem", sub) + of_kind("any", *over_sub([x1_own] * SUBS)),
         [pltpu.VMEM((SUBS, PARENTS, 4 * OWN, UNKNOWNS), BF16)],
     )
     (near2,) = call(
@@ -562,7 +582,6 @@
         [((LEAVES, PROBES, ROWS), F32)],
         near_args(x1, low, high),
         wide_scratch,
-        chunks=PARENTS,
     )
     got, near2 = lax.optimization_barrier((got, near2))
     (field,) = call(
@@ -570,7 +589,8 @@
         "last_field",
         [((PARENTS,) + tile, BF16)],
         of_kind("smem", far_index, coarse_index)
-        + of_kind("vmem", got, weights)
+        + of_kind("vmem", got)
+        + of_kind("any", weights)
         + of_kind("hbm", four_transfers),
         rows_scratch,
     )
@@ -580,8 +600,7 @@
         [(probes.shape, BF16)],
         of_kind("smem", sub)
         + of_kind("vmem", *over_sub([field] * SUBS))
-        + of_kind("any", near2)
-        + of_kind("hbm", four_bases),
+        + of_kind("vmem", near2, four_bases),
         [pltpu.VMEM((SUBS, PARENTS) + tile, BF16)],
     )
     return (first, second_apply)

time: 121 us -> 124 us (1.025)
  the two profiles are of different devices: /device:TPU:121 before, /device:TPU:1 now
where the time goes in v4:
time: 124 us; the launch traced here: 123 us
  starting transfers between devices  55.6 us (45%)
  Pallas kernels  28.9 us (23%)
  waiting for transfers between devices  18.8 us (15%)
  blocking collectives  13 us (10%)
  local copies, waits for them, and re-layouts  5.67 us (5%)
    pallas_call x13, Pallas kernels, call(): pl.pallas_call(body, name=name, out_shape=[jax.ShapeDtypeStruct(out[0], o...  28.9 us
    ppermute x12, starting transfers between devices, over_sub(): lax.ppermute(pieces[k], 'sub', [(i, (i + k) % SUBS) for i in range(SUBS)])  14.8 us
    ppermute x12, waiting for transfers between devices, over_sub(): lax.ppermute(pieces[k], 'sub', [(i, (i + k) % SUBS) for i in range(SUBS)])  13.7 us
    all_to_all x1, blocking collectives, along(): lax.all_to_all(tiles, 'leaf', 0, 0, axis_index_groups=along_z, tiled=True)  13 us
    all_to_all x2, starting transfers between devices, within(): lax.all_to_all(chosen, 'leaf', 0, 0, axis_index_groups=in_plane, tiled=True)  11.7 us
    ppermute x2, starting transfers between devices, near_args(): lax.ppermute(high, 'leaf', [(i, i + 1) for i in range(groups - 1)])  8.99 us
    all_to_all x1, starting transfers between devices, along(): lax.all_to_all(tiles, 'leaf', 0, 0, axis_index_groups=along_z, tiled=True)  8.66 us
    all_to_all x1, starting transfers between devices, local(): lax.all_to_all(wanted, 'leaf', 0, 0, axis_index_groups=in_plane, tiled=True)  7.5 us
  transfers between devices with their start and end apart: 20, of which 11 were waited for; matrix products, arithmetic and copies ran while one was open for 0% of the time, Pallas kernels for 13%

profile of v4, /device:TPU:1, one launch (start us, length us, event | category | flops | bytes accessed | tf_op | source)
XLA Modules:
  0.0 123.0 jit_solution(17110295674219648659)
XLA Ops:
  0.6 1.8 %partial_sums.1 = (bf16[336,128]{1,0:T(8,128)(2,1)S(1)}, bf16[336,128]{1,0:T(8,128)(2,1)S(1)}, bf16[336,128]{1,0:T(8,128)(2,1)S(1)}, bf16[336,128]{1,0:T(8,128)(2,1)S(1)}) custom-call(s32[1]{0:T(128)} %bitcast.refs_0_, bf16[32,16,64]{2,1,0:T(8,128)(2,1)} %refs_1_.4, bf16[4,256,64]{2,1,0:T(8,128)(2,1)} %bitcast.10, bf16[4,256,64]{2,1,0:T(8,128)(2,1)} %bitcast.16), custom_call_target="tpu_custom_call" | custom-call | tf_op jit(solution)/shard_map/partial_sums/pallas_call | solution.py:98
  2.5 2.1 %collective-permute-start = (bf16[336,128]{1,0:T(8,128)(2,1)S(1)}, bf16[336,128]{1,0:T(8,128)(2,1)S(1)}, u32[]{:S(2)}, u32[]{:S(2)}) collective-permute-start(bf16[336,128]{1,0:T(8,128)(2,1)S(1)} %get-tuple-element.53), channel_id=1, source_target_pairs={{0,1},{1,2},{2,3},{3,0},{4,5},{5,6},{6,7},{7,4},{8,9},{9,10},{10,1... | collective-permute-start | bytes 258056 | tf_op jit(solution)/shard_map/ppermute | solution.py:478
  4.6 2.5 %collective-permute-start.1 = (bf16[336,128]{1,0:T(8,128)(2,1)S(1)}, bf16[336,128]{1,0:T(8,128)(2,1)S(1)}, u32[]{:S(2)}, u32[]{:S(2)}) collective-permute-start(bf16[336,128]{1,0:T(8,128)(2,1)S(1)} %get-tuple-element.54), channel_id=1, source_target_pairs={{0,2},{1,3},{2,0},{3,1},{4,6},{5,7},{6,4},{7,5},{8,10},{9,11},{10,... | collective-permute-start | bytes 258056 | tf_op jit(solution)/shard_map/ppermute | solution.py:478
  11.5 8.7 %all-to-all-start = ((bf16[8,5,16,128]{3,2,1,0:T(8,128)(2,1)}), bf16[8,5,16,128]{3,2,1,0:T(8,128)(2,1)S(1)}, u32[]{:S(2)}, u32[]{:S(2)}) async-start(bf16[8,5,16,128]{3,2,1,0:T(8,128)(2,1)} %get-tuple-element.61), calls=%async_computation | async-start | bytes 327680 | tf_op jit(solution)/shard_map/all_to_all | solution.py:497
  20.1 5.0 %collective-permute-start.3 = (bf16[4,32,256]{2,1,0:T(8,128)(2,1)S(1)}, bf16[4,32,256]{2,1,0:T(8,128)(2,1)S(1)}, u32[]{:S(2)}, u32[]{:S(2)}) collective-permute-start(bf16[4,32,256]{2,1,0:T(8,128)(2,1)S(1)} %get-tuple-element.66), channel_id=1, source_target_pairs={{0,4},{4,8},{8,12},{12,16},{16,20},{20,24},{24,28},{28,32},{32,36}... | collective-permute-start | bytes 196616 | tf_op jit(solution)/shard_map/ppermute | solution.py:491
  25.1 1.9 %collective-permute-start.4 = (bf16[4,32,256]{2,1,0:T(8,128)(2,1)S(1)}, bf16[4,32,256]{2,1,0:T(8,128)(2,1)S(1)}, u32[]{:S(2)}, u32[]{:S(2)}) collective-permute-start(bf16[4,32,256]{2,1,0:T(8,128)(2,1)S(1)} %get-tuple-element.67), channel_id=1, source_target_pairs={{4,0},{8,4},{12,8},{16,12},{20,16},{24,20},{28,24},{32,28},{36,32}... | collective-permute-start | bytes 196616 | tf_op jit(solution)/shard_map/ppermute | solution.py:492
  28.4 7.5 %all-to-all-start.1 = ((s32[8,1,128]{2,1,0:T(1,128)}), s32[8,1,128]{2,1,0:T(1,128)S(1)}, u32[]{:S(2)}, u32[]{:S(2)}) async-start(s32[8,1,128]{2,1,0:T(1,128)} %bitcast.5), calls=%async_computation.1 | async-start | bytes 8192 | tf_op jit(solution)/shard_map/all_to_all | solution.py:537
  36.6 4.4 %near_field_sent.1 = (bf16[576,128]{1,0:T(8,128)(2,1)S(1)}, bf16[576,128]{1,0:T(8,128)(2,1)S(1)}, bf16[576,128]{1,0:T(8,128)(2,1)S(1)}, bf16[576,128]{1,0:T(8,128)(2,1)S(1)}) custom-call(s32[1]{0:T(128)} %bitcast.refs_0_, s32[1]{0:T(128)} %bitcast.1.refs_0_.refs_1_, s32[16,9]{1,0:T(8,128)S(1)} %copy-done.7, ...), custom_call_target="tpu_custom_call" | custom-call | tf_op jit(solution)/shard_map/near_field_sent/pallas_call | solution.py:98
  43.2 4.8 %all-to-all-start.2 = ((bf16[8,12,16,128]{3,2,1,0:T(8,128)(2,1)}), bf16[8,12,16,128]{3,2,1,0:T(8,128)(2,1)S(1)}, u32[]{:S(2)}, u32[]{:S(2)}) async-start(bf16[8,12,16,128]{3,2,1,0:T(8,128)(2,1)} %choose_rows.2), calls=%async_computation.2 | async-start | bytes 786432 | tf_op jit(solution)/shard_map/all_to_all | solution.py:507
  48.7 2.9 %collective-permute-start.6 = (bf16[576,128]{1,0:T(8,128)(2,1)S(1)}, bf16[576,128]{1,0:T(8,128)(2,1)S(1)}, u32[]{:S(2)}, u32[]{:S(2)}) collective-permute-start(bf16[576,128]{1,0:T(8,128)(2,1)S(1)} %get-tuple-element.76), channel_id=1, source_target_pairs={{0,2},{1,3},{2,0},{3,1},{4,6},{5,7},{6,4},{7,5},{8,10},{9,11},{10,... | collective-permute-start | bytes 442376 | tf_op jit(solution)/shard_map/ppermute | solution.py:478
  52.1 3.1 %join_couplings.1.refs_3_ = bf16[5,256,1024]{2,1,0:T(8,128)(2,1)S(1)} custom-call(s32[1]{0:T(128)} %bitcast.refs_0_, bf16[16,16,64,64]{3,2,1,0:T(8,128)(2,1)} %refs_1_.6, bf16[4,16,64,64]{3,2,1,0:T(8,128)(2,1)} %refs_2_.5), custom_call_target="tpu_custom_call" | custom-call | tf_op jit(solution)/shard_map/join_couplings/pallas_call | solution.py:98
  55.2 3.5 %collective-permute-done.6.refs_3_ = bf16[576,128]{1,0:T(8,128)(2,1)S(1)} collective-permute-done((bf16[576,128]{1,0:T(8,128)(2,1)S(1)}, bf16[576,128]{1,0:T(8,128)(2,1)S(1)}, u32[]{:S(2)}, u32[]{:S(2)}) %collective-permute-start.6) | collective-permute-done | bytes 147488 | tf_op jit(solution)/shard_map/ppermute | solution.py:478
  62.1 4.1 %middle.1 = (bf16[4,32,256]{2,1,0:T(8,128)(2,1)S(1)}, bf16[8,5,16,128]{3,2,1,0:T(8,128)(2,1)S(1)}) custom-call(s32[16,16]{1,0:T(8,128)S(1)} %copy-done.10, s32[4,16]{1,0:T(4,128)S(1)} %get-tuple-element.51.refs_1_, bf16[96,16,128]{2,1,0:T(8,128)(2,1)S(1)} %bitcast.12, bf16[5,256,1024]{2,1,0:T(8,128)(2,1)S(1)} %join_couplings.1.refs_3_, ...), custom_call_target="tpu_custom_call" | custom-call | tf_op jit(solution)/shard_map/middle/pallas_call | solution.py:98
  66.9 13.0 %all_to_all.31.refs_1_ = bf16[8,5,16,128]{3,2,1,0:T(8,128)(2,1)S(1)} all-to-all(bf16[8,5,16,128]{3,2,1,0:T(8,128)(2,1)S(1)} %get-tuple-element.82), channel_id=1, replica_groups={{0,32,64,96,128,160,192,224},{4,36,68,100,132,164,196,228},{8,40,72,104..., dimensions={0} | all-to-all | bytes 327680 | tf_op jit(solution)/shard_map/all_to_all | solution.py:497
  81.5 6.9 %all-to-all-start.4 = ((bf16[8,12,16,128]{3,2,1,0:T(8,128)(2,1)}), bf16[8,12,16,128]{3,2,1,0:T(8,128)(2,1)S(1)}, u32[]{:S(2)}, u32[]{:S(2)}) async-start(bf16[8,12,16,128]{3,2,1,0:T(8,128)(2,1)} %choose_rows.3), calls=%async_computation.4 | async-start | bytes 786432 | tf_op jit(solution)/shard_map/all_to_all | solution.py:507
  88.4 2.5 %collective-permute-start.10 = (bf16[4,32,256]{2,1,0:T(8,128)(2,1)}, bf16[4,32,256]{2,1,0:T(8,128)(2,1)S(1)}, u32[]{:S(2)}, u32[]{:S(2)}) collective-permute-start(bf16[4,32,256]{2,1,0:T(8,128)(2,1)} %copy-done.5), channel_id=1, source_target_pairs={{0,3},{1,0},{2,1},{3,2},{4,7},{5,4},{6,5},{7,6},{8,11},{9,8},{10,9... | collective-permute-start | bytes 196616 | tf_op jit(solution)/shard_map/ppermute | solution.py:478
  91.7 2.3 %collective-permute-done.10.refs_4_ = bf16[4,32,256]{2,1,0:T(8,128)(2,1)S(1)} collective-permute-done((bf16[4,32,256]{2,1,0:T(8,128)(2,1)}, bf16[4,32,256]{2,1,0:T(8,128)(2,1)S(1)}, u32[]{:S(2)}, u32[]{:S(2)}) %collective-permute-start.10) | collective-permute-done | bytes 65568 | tf_op jit(solution)/shard_map/ppermute | solution.py:478
  94.1 1.7 %collective-permute-done.9.refs_3_ = bf16[4,32,256]{2,1,0:T(8,128)(2,1)S(1)} collective-permute-done((bf16[4,32,256]{2,1,0:T(8,128)(2,1)}, bf16[4,32,256]{2,1,0:T(8,128)(2,1)S(1)}, u32[]{:S(2)}, u32[]{:S(2)}) %collective-permute-start.9) | collective-permute-done | bytes 65568 | tf_op jit(solution)/shard_map/ppermute | solution.py:478
  95.8 2.0 %collective-permute-done.8.refs_2_ = bf16[4,32,256]{2,1,0:T(8,128)(2,1)S(1)} collective-permute-done((bf16[4,32,256]{2,1,0:T(8,128)(2,1)}, bf16[4,32,256]{2,1,0:T(8,128)(2,1)S(1)}, u32[]{:S(2)}, u32[]{:S(2)}) %collective-permute-start.8) | collective-permute-done | bytes 65568 | tf_op jit(solution)/shard_map/ppermute | solution.py:478
  100.1 4.0 %collective-permute-start.11 = (bf16[4,32,256]{2,1,0:T(8,128)(2,1)S(1)}, bf16[4,32,256]{2,1,0:T(8,128)(2,1)S(1)}, u32[]{:S(2)}, u32[]{:S(2)}) collective-permute-start(bf16[4,32,256]{2,1,0:T(8,128)(2,1)S(1)} %get-tuple-element.84), channel_id=1, source_target_pairs={{0,4},{4,8},{8,12},{12,16},{16,20},{20,24},{24,28},{28,32},{32,36}... | collective-permute-start | bytes 196616 | tf_op jit(solution)/shard_map/ppermute | solution.py:491
  104.1 1.9 %collective-permute-start.12 = (bf16[4,32,256]{2,1,0:T(8,128)(2,1)S(1)}, bf16[4,32,256]{2,1,0:T(8,128)(2,1)S(1)}, u32[]{:S(2)}, u32[]{:S(2)}) collective-permute-start(bf16[4,32,256]{2,1,0:T(8,128)(2,1)S(1)} %get-tuple-element.85), channel_id=1, source_target_pairs={{4,0},{8,4},{12,8},{16,12},{20,16},{24,20},{28,24},{32,28},{36,32}... | collective-permute-start | bytes 196616 | tf_op jit(solution)/shard_map/ppermute | solution.py:492
  106.0 3.6 %collective-permute-done.12.refs_4_ = bf16[4,32,256]{2,1,0:T(8,128)(2,1)S(1)} collective-permute-done((bf16[4,32,256]{2,1,0:T(8,128)(2,1)S(1)}, bf16[4,32,256]{2,1,0:T(8,128)(2,1)S(1)}, u32[]{:S(2)}, u32[]{:S(2)}) %collective-permute-start.12) | collective-permute-done | bytes 65568 | tf_op jit(solution)/shard_map/ppermute | solution.py:492
  109.7 3.7 %near_field.1.refs_5_ = f32[16,32,64]{2,1,0:T(8,128)S(1)} custom-call(s32[1]{0:T(128)} %bitcast.1.refs_0_.refs_1_, s32[16,9]{1,0:T(8,128)S(1)} %copy-done.8, bf16[16,32,256]{2,1,0:T(8,128)(2,1)S(1)} %get-tuple-element.83.refs_2_, bf16[4,32,256]{2,1,0:T(8,128)(2,1)S(1)} %collective-permute-done.11.refs_3_, ...), custom_call_target="tpu_custom_call" | custom-call | tf_op jit(solution)/shard_map/near_field/pallas_call | solution.py:98
  114.1 2.7 %last_field.1.refs_1_ = bf16[4,16,128]{2,1,0:T(8,128)(2,1)S(1)} custom-call(s32[16,16]{1,0:T(8,128)S(1)} %copy-done.11, s32[4,16]{1,0:T(4,128)S(1)} %get-tuple-element.51.refs_1_, bf16[96,16,128]{2,1,0:T(8,128)(2,1)S(1)} %bitcast.13, bf16[5,256,1024]{2,1,0:T(8,128)(2,1)S(1)} %join_couplings.1.refs_3_, bf16[4,256,64]{2,1,0:T(8,128)(2,1)} %bitcast.18), custom_call_target="tpu_custom_call" | custom-call | tf_op jit(solution)/shard_map/last_field/pallas_call | solution.py:98
  (54 shorter events, 25.2 us)
Async XLA Ops:
  2.5 7.3 %collective-permute-start = (bf16[336,128]{1,0:T(8,128)(2,1)S(1)}, bf16[336,128]{1,0:T(8,128)(2,1)S(1)}, u32[]{:S(2)}, u32[]{:S(2)}) collective-permute-start(bf16[336,128]{1,0:T(8,128)(2,1)S(1)} %get-tuple-element.53), channel_id=1, source_target_pairs={{0,1},{1,2},{2,3},{3,0},{4,5},{5,6},{6,7},{7,4},{8,9},{9,10},{10,1... | collective-permute-start | bytes 258056 | tf_op jit(solution)/shard_map/ppermute | solution.py:478
  4.6 5.9 %collective-permute-start.1 = (bf16[336,128]{1,0:T(8,128)(2,1)S(1)}, bf16[336,128]{1,0:T(8,128)(2,1)S(1)}, u32[]{:S(2)}, u32[]{:S(2)}) collective-permute-start(bf16[336,128]{1,0:T(8,128)(2,1)S(1)} %get-tuple-element.54), channel_id=1, source_target_pairs={{0,2},{1,3},{2,0},{3,1},{4,6},{5,7},{6,4},{7,5},{8,10},{9,11},{10,... | collective-permute-start | bytes 258056 | tf_op jit(solution)/shard_map/ppermute | solution.py:478
  7.0 3.6 %collective-permute-start.2 = (bf16[336,128]{1,0:T(8,128)(2,1)S(1)}, bf16[336,128]{1,0:T(8,128)(2,1)S(1)}, u32[]{:S(2)}, u32[]{:S(2)}) collective-permute-start(bf16[336,128]{1,0:T(8,128)(2,1)S(1)} %get-tuple-element.55), channel_id=1, source_target_pairs={{0,3},{1,0},{2,1},{3,2},{4,7},{5,4},{6,5},{7,6},{8,11},{9,8},{10,9... | collective-permute-start | bytes 258056 | tf_op jit(solution)/shard_map/ppermute | solution.py:478
  9.8 1.7 %copy-start.9 = (s32[16,16]{1,0:T(8,128)}, s32[16,16]{1,0:T(8,128)S(1)}, u32[]{:S(2)}) copy-start(s32[16,16]{1,0:T(8,128)S(1)} %get-tuple-element.50.refs_0_) | copy-start | bytes 3076
  11.5 17.0 %all-to-all-start = ((bf16[8,5,16,128]{3,2,1,0:T(8,128)(2,1)}), bf16[8,5,16,128]{3,2,1,0:T(8,128)(2,1)S(1)}, u32[]{:S(2)}, u32[]{:S(2)}) async-start(bf16[8,5,16,128]{3,2,1,0:T(8,128)(2,1)} %get-tuple-element.61), calls=%async_computation | async-start | bytes 327680 | tf_op jit(solution)/shard_map/all_to_all | solution.py:497
  20.1 15.8 %collective-permute-start.3 = (bf16[4,32,256]{2,1,0:T(8,128)(2,1)S(1)}, bf16[4,32,256]{2,1,0:T(8,128)(2,1)S(1)}, u32[]{:S(2)}, u32[]{:S(2)}) collective-permute-start(bf16[4,32,256]{2,1,0:T(8,128)(2,1)S(1)} %get-tuple-element.66), channel_id=1, source_target_pairs={{0,4},{4,8},{8,12},{12,16},{16,20},{20,24},{24,28},{28,32},{32,36}... | collective-permute-start | bytes 196616 | tf_op jit(solution)/shard_map/ppermute | solution.py:491
  25.1 10.8 %collective-permute-start.4 = (bf16[4,32,256]{2,1,0:T(8,128)(2,1)S(1)}, bf16[4,32,256]{2,1,0:T(8,128)(2,1)S(1)}, u32[]{:S(2)}, u32[]{:S(2)}) collective-permute-start(bf16[4,32,256]{2,1,0:T(8,128)(2,1)S(1)} %get-tuple-element.67), channel_id=1, source_target_pairs={{4,0},{8,4},{12,8},{16,12},{20,16},{24,20},{28,24},{32,28},{36,32}... | collective-permute-start | bytes 196616 | tf_op jit(solution)/shard_map/ppermute | solution.py:492
  28.4 13.2 %all-to-all-start.1 = ((s32[8,1,128]{2,1,0:T(1,128)}), s32[8,1,128]{2,1,0:T(1,128)S(1)}, u32[]{:S(2)}, u32[]{:S(2)}) async-start(s32[8,1,128]{2,1,0:T(1,128)} %bitcast.5), calls=%async_computation.1 | async-start | bytes 8192 | tf_op jit(solution)/shard_map/all_to_all | solution.py:537
  43.2 17.3 %all-to-all-start.2 = ((bf16[8,12,16,128]{3,2,1,0:T(8,128)(2,1)}), bf16[8,12,16,128]{3,2,1,0:T(8,128)(2,1)S(1)}, u32[]{:S(2)}, u32[]{:S(2)}) async-start(bf16[8,12,16,128]{3,2,1,0:T(8,128)(2,1)} %choose_rows.2), calls=%async_computation.2 | async-start | bytes 786432 | tf_op jit(solution)/shard_map/all_to_all | solution.py:507
  48.0 10.7 %copy-start.2 = (bf16[576,128]{1,0:T(8,128)(2,1)S(1)}, bf16[576,128]{1,0:T(8,128)(2,1)}, u32[]{:S(2)}) copy-start(bf16[576,128]{1,0:T(8,128)(2,1)} %copy-done.1) | copy-start | bytes 442372
  48.0 7.1 %collective-permute-start.5 = (bf16[576,128]{1,0:T(8,128)(2,1)S(1)}, bf16[576,128]{1,0:T(8,128)(2,1)S(1)}, u32[]{:S(2)}, u32[]{:S(2)}) collective-permute-start(bf16[576,128]{1,0:T(8,128)(2,1)S(1)} %get-tuple-element.75), channel_id=1, source_target_pairs={{0,1},{1,2},{2,3},{3,0},{4,5},{5,6},{6,7},{7,4},{8,9},{9,10},{10,1... | collective-permute-start | bytes 442376 | tf_op jit(solution)/shard_map/ppermute | solution.py:478
  48.7 10.0 %collective-permute-start.6 = (bf16[576,128]{1,0:T(8,128)(2,1)S(1)}, bf16[576,128]{1,0:T(8,128)(2,1)S(1)}, u32[]{:S(2)}, u32[]{:S(2)}) collective-permute-start(bf16[576,128]{1,0:T(8,128)(2,1)S(1)} %get-tuple-element.76), channel_id=1, source_target_pairs={{0,2},{1,3},{2,0},{3,1},{4,6},{5,7},{6,4},{7,5},{8,10},{9,11},{10,... | collective-permute-start | bytes 442376 | tf_op jit(solution)/shard_map/ppermute | solution.py:478
  51.6 7.1 %collective-permute-start.7 = (bf16[576,128]{1,0:T(8,128)(2,1)S(1)}, bf16[576,128]{1,0:T(8,128)(2,1)S(1)}, u32[]{:S(2)}, u32[]{:S(2)}) collective-permute-start(bf16[576,128]{1,0:T(8,128)(2,1)S(1)} %get-tuple-element.77), channel_id=1, source_target_pairs={{0,3},{1,0},{2,1},{3,2},{4,7},{5,4},{6,5},{7,6},{8,11},{9,8},{10,9... | collective-permute-start | bytes 442376 | tf_op jit(solution)/shard_map/ppermute | solution.py:478
  55.1 54.5 %copy-start.8 = (s32[16,9]{1,0:T(8,128)S(1)}, s32[16,9]{1,0:T(8,128)}, u32[]{:S(2)}) copy-start(s32[16,9]{1,0:T(8,128)} %refs_1_.7) | copy-start | bytes 1732
  81.5 31.9 %all-to-all-start.4 = ((bf16[8,12,16,128]{3,2,1,0:T(8,128)(2,1)}), bf16[8,12,16,128]{3,2,1,0:T(8,128)(2,1)S(1)}, u32[]{:S(2)}, u32[]{:S(2)}) async-start(bf16[8,12,16,128]{3,2,1,0:T(8,128)(2,1)} %choose_rows.3), calls=%async_computation.4 | async-start | bytes 786432 | tf_op jit(solution)/shard_map/all_to_all | solution.py:507
  88.4 5.7 %collective-permute-start.10 = (bf16[4,32,256]{2,1,0:T(8,128)(2,1)}, bf16[4,32,256]{2,1,0:T(8,128)(2,1)S(1)}, u32[]{:S(2)}, u32[]{:S(2)}) collective-permute-start(bf16[4,32,256]{2,1,0:T(8,128)(2,1)} %copy-done.5), channel_id=1, source_target_pairs={{0,3},{1,0},{2,1},{3,2},{4,7},{5,4},{6,5},{7,6},{8,11},{9,8},{10,9... | collective-permute-start | bytes 196616 | tf_op jit(solution)/shard_map/ppermute | solution.py:478
  90.9 4.8 %collective-permute-start.9 = (bf16[4,32,256]{2,1,0:T(8,128)(2,1)}, bf16[4,32,256]{2,1,0:T(8,128)(2,1)S(1)}, u32[]{:S(2)}, u32[]{:S(2)}) collective-permute-start(bf16[4,32,256]{2,1,0:T(8,128)(2,1)} %copy-done.5), channel_id=1, source_target_pairs={{0,2},{1,3},{2,0},{3,1},{4,6},{5,7},{6,4},{7,5},{8,10},{9,11},{10,... | collective-permute-start | bytes 196616 | tf_op jit(solution)/shard_map/ppermute | solution.py:478
  91.7 6.0 %collective-permute-start.8 = (bf16[4,32,256]{2,1,0:T(8,128)(2,1)}, bf16[4,32,256]{2,1,0:T(8,128)(2,1)S(1)}, u32[]{:S(2)}, u32[]{:S(2)}) collective-permute-start(bf16[4,32,256]{2,1,0:T(8,128)(2,1)} %copy-done.5), channel_id=1, source_target_pairs={{0,1},{1,2},{2,3},{3,0},{4,5},{5,6},{6,7},{7,4},{8,9},{9,10},{10,1... | collective-permute-start | bytes 196616 | tf_op jit(solution)/shard_map/ppermute | solution.py:478
  100.1 5.9 %collective-permute-start.11 = (bf16[4,32,256]{2,1,0:T(8,128)(2,1)S(1)}, bf16[4,32,256]{2,1,0:T(8,128)(2,1)S(1)}, u32[]{:S(2)}, u32[]{:S(2)}) collective-permute-start(bf16[4,32,256]{2,1,0:T(8,128)(2,1)S(1)} %get-tuple-element.84), channel_id=1, source_target_pairs={{0,4},{4,8},{8,12},{12,16},{16,20},{20,24},{24,28},{28,32},{32,36}... | collective-permute-start | bytes 196616 | tf_op jit(solution)/shard_map/ppermute | solution.py:491
  104.1 5.6 %collective-permute-start.12 = (bf16[4,32,256]{2,1,0:T(8,128)(2,1)S(1)}, bf16[4,32,256]{2,1,0:T(8,128)(2,1)S(1)}, u32[]{:S(2)}, u32[]{:S(2)}) collective-permute-start(bf16[4,32,256]{2,1,0:T(8,128)(2,1)S(1)} %get-tuple-element.85), channel_id=1, source_target_pairs={{4,0},{8,4},{12,8},{16,12},{20,16},{24,20},{28,24},{32,28},{36,32}... | collective-permute-start | bytes 196616 | tf_op jit(solution)/shard_map/ppermute | solution.py:492
  109.7 12.2 %copy-start = (bf16[16,64,64]{2,1,0:T(8,128)(2,1)S(1)}, bf16[16,64,64]{2,1,0:T(8,128)(2,1)}, u32[]{:S(2)}) copy-start(bf16[16,64,64]{2,1,0:T(8,128)(2,1)} %refs_7_.1) | copy-start | bytes 393220
  116.8 3.0 %collective-permute-start.15 = (bf16[4,16,128]{2,1,0:T(8,128)(2,1)S(1)}, bf16[4,16,128]{2,1,0:T(8,128)(2,1)S(1)}, u32[]{:S(2)}, u32[]{:S(2)}) collective-permute-start(bf16[4,16,128]{2,1,0:T(8,128)(2,1)S(1)} %last_field.1.refs_1_), channel_id=1, source_target_pairs={{0,3},{1,0},{2,1},{3,2},{4,7},{5,4},{6,5},{7,6},{8,11},{9,8},{10,9... | collective-permute-start | bytes 49160 | tf_op jit(solution)/shard_map/ppermute | solution.py:478
  117.2 4.1 %collective-permute-start.14 = (bf16[4,16,128]{2,1,0:T(8,128)(2,1)S(1)}, bf16[4,16,128]{2,1,0:T(8,128)(2,1)S(1)}, u32[]{:S(2)}, u32[]{:S(2)}) collective-permute-start(bf16[4,16,128]{2,1,0:T(8,128)(2,1)S(1)} %last_field.1.refs_1_), channel_id=1, source_target_pairs={{0,2},{1,3},{2,0},{3,1},{4,6},{5,7},{6,4},{7,5},{8,10},{9,11},{10,... | collective-permute-start | bytes 49160 | tf_op jit(solution)/shard_map/ppermute | solution.py:478
  118.0 3.9 %collective-permute-start.13 = (bf16[4,16,128]{2,1,0:T(8,128)(2,1)S(1)}, bf16[4,16,128]{2,1,0:T(8,128)(2,1)S(1)}, u32[]{:S(2)}, u32[]{:S(2)}) collective-permute-start(bf16[4,16,128]{2,1,0:T(8,128)(2,1)S(1)} %last_field.1.refs_1_), channel_id=1, source_target_pairs={{0,1},{1,2},{2,3},{3,0},{4,5},{5,6},{6,7},{7,4},{8,9},{9,10},{10,1... | collective-permute-start | bytes 49160 | tf_op jit(solution)/shard_map/ppermute | solution.py:478
  (8 other events, 5.7 us)

commit v5 on v4

--- a/solution.py
+++ b/solution.py
@@ -26,7 +26,7 @@
 OUT_TILES = LEAF_OUT + PLANES
 GOT_ROWS = 4 * PLANE * OUT_TILES
 PACKED = LEAVES // 2 * PROBES
-SENT = 16 * PARENTS + LEAVES // 2 * RANK
+SENT = PACKED + LEAVES // 2 * RANK
 BF16, F32 = jnp.bfloat16, jnp.float32
 
 NT = (((1,), (1,)), ((), ()))
@@ -62,10 +62,36 @@
         return self.target[index]
 
 
+class Leaving:
+    def __init__(self, source, target, sems, parts):
+        size = target.shape[0] // parts
+        self.source, self.started = source, []
+        self.waiting = {}
+        for c in range(parts):
+            part = pl.ds(c * size, size)
+            self.waiting[c] = pltpu.make_async_copy(source.at[part], target.at[part], sems.at[c])
+
+    def __setitem__(self, index, value):
+        self.source[index] = value
+
+    def send(self, part=None):
+        for c in list(self.waiting) if part is None else [part]:
+            copy = self.waiting.pop(c)
+            copy.start()
+            self.started.append(copy)
+
+    def finish(self):
+        self.send()
+        for copy in self.started:
+            copy.wait()
+
+
+PARTS = {"hbm": 1, "any": 1, "cut": 4}
+
+
 def call(kernel, name, outs, args, scratch=()):
-    spaces = {"smem": pltpu.SMEM, "vmem": pltpu.VMEM, "hbm": pltpu.HBM, "cut": pltpu.HBM, "any": pl.ANY}
-    parts = {"hbm": 1, "any": 1, "cut": 4}
-    moved = [j for j, (kind, _) in enumerate(args) if kind in parts]
+    spaces = {"smem": pltpu.SMEM, "table": pltpu.SMEM, "vmem": pltpu.VMEM, "any": pl.ANY}
+    moved = [j for j, (kind, _) in enumerate(args) if kind in PARTS]
     away = [j for j, out in enumerate(outs) if len(out) == 3]
     scratch = list(scratch)
     buffers = [pltpu.VMEM(args[j][1].shape, args[j][1].dtype) for j in moved]
@@ -75,38 +101,36 @@
         refs = list(refs)
         sems = refs.pop()
         front = len(args) + len(outs) + len(scratch)
-        used, arriving = 0, []
+        used = 0
         for n, j in enumerate(moved):
-            count = parts[args[j][0]]
+            count = PARTS[args[j][0]]
             refs[j] = Arriving(refs[j], refs[front + n], sems.at[pl.ds(used, count)], count)
-            arriving.append(refs[j])
             used += count
-        leaving = []
         for n, j in enumerate(away):
             target, source = refs[len(args) + j], refs[front + len(moved) + n]
-            leaving.append(pltpu.make_async_copy(source, target, sems.at[used + n]))
-            refs[len(args) + j] = source
+            count = outs[j][2]
+            refs[len(args) + j] = Leaving(source, target, sems.at[pl.ds(used, count)], count)
+            used += count
         kernel(*refs[:front])
-        for copy in leaving:
-            copy.start()
-        for buffer in arriving:
-            buffer.finish()
-        for copy in leaving:
-            copy.wait()
-
-    count = sum(parts[args[j][0]] for j in moved) + len(away)
+        for ref in refs[:front]:
+            if isinstance(ref, (Arriving, Leaving)):
+                ref.finish()
+
+    count = sum(PARTS[args[j][0]] for j in moved) + sum(outs[j][2] for j in away)
     return pl.pallas_call(
         body,
         name=name,
-        out_shape=[jax.ShapeDtypeStruct(out[0], out[1]) for out in outs],
-        in_specs=[pl.BlockSpec(memory_space=spaces[kind]) for kind, _ in args],
+        out_shape=[
+            pltpu.HBM(out[0], out[1]) if len(out) == 3 else jax.ShapeDtypeStruct(*out) for out in outs
+        ],
+        in_specs=[pl.BlockSpec(memory_space=spaces.get(kind, pltpu.HBM)) for kind, _ in args],
         out_specs=[
             pl.BlockSpec(memory_space=pltpu.HBM if j in away else pltpu.VMEM) for j in range(len(outs))
         ],
         scratch_shapes=scratch + buffers + [pltpu.SemaphoreType.DMA((max(count, 1),))],
         compiler_params=pltpu.CompilerParams(vmem_limit_bytes=VMEM_LIMIT),
     )(*[
-        pltpu.with_memory_space_constraint(array, pltpu.HBM) if kind in ("hbm", "cut") else array
+        array if kind in ("smem", "vmem", "any") else pltpu.with_memory_space_constraint(array, pltpu.HBM)
         for kind, array in args
     ])
 
@@ -134,11 +158,6 @@
 
 def to_tile(x):
     return jnp.concatenate([x[:, :LANES], x[:, LANES:]], axis=0).astype(BF16)
-
-
-def tile_row(tile, c):
-    h, g = c // 2, c % 2
-    return tile[h * OWN : (h + 1) * OWN, g * RANK : (g + 1) * RANK]
 
 
 def index_kernel(_, far_ref, coarse_ref, wanted_ref, far_out_ref, coarse_out_ref):
@@ -218,6 +237,7 @@
         tile = total.astype(BF16)
         for z in range(PLANES):
             out_ref[z, t] = tile
+    out_ref.send()
     in_order(sub_ref, got_refs, slots_ref, PACKED)
     for i in range(LEAVES):
         half = slice((i % 2) * ROWS, (i % 2 + 1) * ROWS)
@@ -232,15 +252,15 @@
 
 def join_kernel(sub_ref, got0_ref, got1_ref, got2_ref, got3_ref, near_ref, basis_ref, slots_ref):
     in_order(sub_ref, [got0_ref, got1_ref, got2_ref, got3_ref], slots_ref, SENT)
-    for q in range(PARENTS):
-        tiles = [slots_ref[s, pl.ds(16 * q, 16), :].astype(F32) for s in range(SUBS)]
-        near = [jnp.concatenate([tile_row(t, c) for t in tiles], axis=1) for c in range(4)]
-        near_ref[q] = jnp.concatenate(near, axis=0).astype(BF16)
+
+    def whole(i, start, size):
+        half = slice((i % 2) * ROWS, (i % 2 + 1) * ROWS)
+        rows = pl.ds(start + (i // 2) * size, size)
+        return jnp.concatenate([slots_ref[s, rows, half] for s in range(SUBS)], axis=1)
+
     for i in range(LEAVES):
-        half = slice((i % 2) * ROWS, (i % 2 + 1) * ROWS)
-        rows = pl.ds(16 * PARENTS + (i // 2) * RANK, RANK)
-        whole = jnp.concatenate([slots_ref[s, rows, half] for s in range(SUBS)], axis=1)
-        basis_ref[i // 4, pl.ds(i % 4 * RANK, RANK), :] = whole
+        near_ref[i // 4, pl.ds(i % 4 * PROBES, PROBES), :] = whole(i, 0, PROBES)
+        basis_ref[i // 4, pl.ds(i % 4 * RANK, RANK), :] = whole(i, PACKED, RANK)
 
 
 def weights_kernel(_, couplings_ref, coarse_ref, out_ref):
@@ -284,6 +304,8 @@
             out_ref[m, t] = jnp.concatenate([top, bottom], axis=0).astype(BF16)
         for z in range(PLANES):
             out_ref[m, LEAF_OUT + z] = got_ref[z, TILES - 1]
+        if m % 4 == 3:
+            out_ref.send(m // 4)
 
 
 def far_field(far_ref, coarse_ref, got_ref, weights_ref, transfer_ref, rows_ref):
@@ -312,26 +334,57 @@
     return fields
 
 
-def middle_kernel(
-    far_ref,
-    coarse_ref,
-    got_ref,
-    weights_ref,
+def field_kernel(
+    far_ref, coarse_ref, got_ref, weights_ref, transfer_ref, out_ref, rows_ref
+):
+    fields = far_field(far_ref, coarse_ref, got_ref, weights_ref, transfer_ref, rows_ref)
+    for q in range(PARENTS):
+        out_ref[q] = to_tile(fields[q])
+
+
+def field_of(field_ref, q):
+    tiles = [field_ref[s, q].astype(F32) for s in range(SUBS)]
+    field = [jnp.concatenate([t[:OWN], t[OWN:]], axis=1) for t in tiles]
+    return spread_diagonal(jnp.concatenate(field, axis=0)).astype(BF16)
+
+
+def second_kernel(
+    sub_ref,
+    field0_ref,
+    field1_ref,
+    field2_ref,
+    field3_ref,
+    near_ref,
+    basis_ref,
     transfer_ref,
-    basis_ref,
-    near_ref,
     x_ref,
+    low_ref,
+    high_ref,
     out_ref,
-    rows_ref,
-):
-    fields = far_field(far_ref, coarse_ref, got_ref, weights_ref, transfer_ref, rows_ref)
+    field_ref,
+    four_ref,
+):
+    in_order(sub_ref, [field0_ref, field1_ref, field2_ref, field3_ref], field_ref, PARENTS)
+    own = probes_of(sub_ref[0])
     tiles = []
     parents = []
     for q in range(PARENTS):
-        far = dot(spread_diagonal(fields[q]).astype(BF16), basis_ref[q])
-        x = (near_ref[q].astype(F32) + far).astype(BF16)
-        x_ref[q] = x
-        leaf = diagonal(dot_nt(x, basis_ref[q]), OWN)
+        far = dot(field_of(field_ref, q), basis_ref[q])
+        x = near_ref[q].astype(F32) + far
+        mine = []
+        for c in range(4):
+            i = 4 * q + c
+            four_ref[c] = x[c * PROBES : (c + 1) * PROBES]
+            mine.append(four_ref[c, own, :])
+            leaf = x[c * PROBES : (c + 1) * PROBES].astype(BF16)
+            x_ref[i] = leaf
+            if i < REACH:
+                low_ref[i] = leaf
+            if i >= LEAVES - REACH:
+                high_ref[i - (LEAVES - REACH)] = leaf
+        x_ref.send(q)
+        mine = jnp.concatenate(mine, axis=0).astype(BF16)
+        leaf = diagonal(dot_nt(mine, basis_ref[q]), OWN)
         tiles.append(to_tile(leaf))
         parents.append(dot(leaf.astype(BF16), transfer_ref[q]))
     tiles.append(to_tile(jnp.concatenate(parents, axis=1)))
@@ -340,59 +393,13 @@
             out_ref[z, t] = tiles[t]
 
 
-def last_field_kernel(
-    far_ref, coarse_ref, got_ref, weights_ref, transfer_ref, out_ref, rows_ref
-):
-    fields = far_field(far_ref, coarse_ref, got_ref, weights_ref, transfer_ref, rows_ref)
-    for q in range(PARENTS):
-        out_ref[q] = to_tile(fields[q])
-
-
-def whole_kernel(
-    sub_ref,
-    got0_ref,
-    got1_ref,
-    got2_ref,
-    got3_ref,
-    x_ref,
-    low_ref,
-    high_ref,
-    first_ref,
-    got_ref,
-):
-    in_order(sub_ref, [got0_ref, got1_ref, got2_ref, got3_ref], got_ref, PARENTS)
-    sub = sub_ref[0]
-    outs = []
-    for q in range(PARENTS):
-        parts = [got_ref[s, q].astype(F32) for s in range(SUBS)]
-        for c in range(4):
-            i = 4 * q + c
-            rows = slice(c * OWN, (c + 1) * OWN)
-            wide = jnp.concatenate([part[rows] for part in parts], axis=0)
-            x = wide.astype(BF16)
-            x_ref[i] = x
-            if i < REACH:
-                low_ref[i] = x
-            if i >= LEAVES - REACH:
-                high_ref[i - (LEAVES - REACH)] = x
-            mine = wide[:, :ROWS]
-            for s in range(1, SUBS):
-                mine = jnp.where(sub == s, wide[:, s * ROWS : (s + 1) * ROWS], mine)
-            outs.append(mine)
-    first_ref[...] = jnp.transpose(jnp.stack(outs), (1, 0, 2)).astype(BF16)
-
-
 def output_kernel(
     sub_ref, field0_ref, field1_ref, field2_ref, field3_ref, near_ref, basis_ref, out_ref, field_ref
 ):
     in_order(sub_ref, [field0_ref, field1_ref, field2_ref, field3_ref], field_ref, PARENTS)
     outs = []
     for q in range(PARENTS):
-        tiles = [field_ref[s, q].astype(F32) for s in range(SUBS)]
-        field = jnp.concatenate(
-            [jnp.concatenate([t[:OWN], t[OWN:]], axis=1) for t in tiles], axis=0
-        )
-        far = dot(spread_diagonal(field).astype(BF16), basis_ref[q])
+        far = dot(field_of(field_ref, q), basis_ref[q])
         for c in range(4):
             outs.append(near_ref[4 * q + c] + far[c * PROBES : (c + 1) * PROBES])
     out_ref[...] = jnp.transpose(jnp.stack(outs), (1, 0, 2)).astype(BF16)
@@ -419,39 +426,33 @@
 
 
 def near_sent_kernel(
-    sub_ref,
-    first_ref,
-    list_ref,
-    x_ref,
-    low_ref,
-    high_ref,
-    blocks_ref,
-    basis_ref,
-    out0_ref,
-    out1_ref,
-    out2_ref,
-    out3_ref,
-    wide_ref,
-    four_ref,
-):
-    out_refs = [out0_ref, out1_ref, out2_ref, out3_ref]
+    first_ref, list_ref, x_ref, low_ref, high_ref, blocks_ref, basis_ref, out_ref, wide_ref
+):
     parts = near_parts(first_ref, list_ref, x_ref, low_ref, high_ref, blocks_ref, wide_ref)
     for q, four in enumerate(parts):
-        four_ref[...] = jnp.concatenate(four, axis=1)
-        for k, out_ref in enumerate(out_refs):
-            tile = to_tile(four_ref[probes_of((sub_ref[0] + k) % SUBS), :])
-            out_ref[pl.ds(16 * q, 16), :] = tile
+        for j in range(2):
+            pair = jnp.concatenate(four[2 * j : 2 * j + 2], axis=1).astype(BF16)
+            out_ref[pl.ds((2 * q + j) * PROBES, PROBES), :] = pair
     for j in range(LEAVES // 2):
         pair = jnp.concatenate([basis_ref[2 * j], basis_ref[2 * j + 1]], axis=1)
-        for out_ref in out_refs:
-            out_ref[pl.ds(16 * PARENTS + j * RANK, RANK), :] = pair
-
-
-def near_kernel(first_ref, list_ref, x_ref, low_ref, high_ref, blocks_ref, out_ref, wide_ref):
+        out_ref[pl.ds(PACKED + j * RANK, RANK), :] = pair
+
+
+def near_kernel(
+    sub_ref, first_ref, list_ref, x_ref, low_ref, high_ref, blocks_ref, out_ref, mine_ref, wide_ref
+):
     parts = near_parts(first_ref, list_ref, x_ref, low_ref, high_ref, blocks_ref, wide_ref)
     for q, four in enumerate(parts):
         for c in range(4):
             out_ref[4 * q + c] = four[c]
+    outs = []
+    for i in range(LEAVES):
+        x = x_ref[i].astype(F32)
+        mine = x[:, :ROWS]
+        for s in range(1, SUBS):
+            mine = jnp.where(sub_ref[0] == s, x[:, s * ROWS : (s + 1) * ROWS], mine)
+        outs.append(mine)
+    mine_ref[...] = jnp.transpose(jnp.stack(outs), (1, 0, 2)).astype(BF16)
 
 
 def local(
@@ -487,11 +488,15 @@
 
     wide_scratch = [pltpu.VMEM((LEAVES + 2 * REACH + 1, PROBES, UNKNOWNS), BF16)]
 
-    def near_args(x, low, high):
+    def halos(low, high):
         from_below = lax.ppermute(high, "leaf", [(i, i + 1) for i in range(groups - 1)])
         from_above = lax.ppermute(low, "leaf", [(i + 1, i) for i in range(groups - 1)])
-        tables = of_kind("smem", first_leaf, near_list)
-        return tables + of_kind("vmem", x, from_below, from_above) + of_kind("cut", near_blocks)
+        return from_below, from_above
+
+    def near_args(x, from_below, from_above):
+        tables = of_kind("smem", first_leaf) + of_kind("table", near_list)
+        edges = of_kind("vmem", from_below, from_above)
+        return tables + of_kind("hbm", x) + edges + of_kind("cut", near_blocks)
 
     def along(tiles):
         return lax.all_to_all(tiles, "leaf", 0, 0, axis_index_groups=along_z, tiled=True)
@@ -500,7 +505,7 @@
         (chosen,) = call(
             choose_kernel,
             "choose_rows",
-            [((PLANE, OUT_TILES) + tile, BF16, True)],
+            [((PLANE, OUT_TILES) + tile, BF16, 2)],
             of_kind("smem", asked) + of_kind("vmem", column),
             [pltpu.VMEM((PLANES * LEAVES, OWN, LANES), F32)],
         )
@@ -520,8 +525,8 @@
         "index_tables",
         [
             ((PLANE, LANES), jnp.int32),
-            (distant_interaction_list.shape, jnp.int32),
-            (coarse_list.shape, jnp.int32),
+            (distant_interaction_list.shape, jnp.int32, 1),
+            (coarse_list.shape, jnp.int32, 1),
         ],
         of_kind("smem", first_leaf) + of_kind("hbm", distant_interaction_list, coarse_list),
     )
@@ -529,79 +534,75 @@
     x0, low, high, tiles = call(
         first_kernel,
         "first_coefficients",
-        [(x_shape, BF16), (edge, BF16), (edge, BF16), (message, BF16, True)],
+        [(x_shape, BF16, 1), (edge, BF16), (edge, BF16), (message, BF16, 1)],
         of_kind("smem", sub) + of_kind("vmem", *pieces),
         [pltpu.VMEM((SUBS, PACKED, LANES), BF16)],
     )
     column, wanted = lax.optimization_barrier((along(tiles), wanted))
     asked = lax.all_to_all(wanted, "leaf", 0, 0, axis_index_groups=in_plane, tiled=True)
-    sent = call(
+    (sent,) = call(
         near_sent_kernel,
         "near_field_sent",
-        [((SENT, LANES), BF16, True)] + [((SENT, LANES), BF16)] * (SUBS - 1),
-        of_kind("smem", sub) + near_args(x0, low, high) + of_kind("hbm", leaf_cluster_basis),
-        wide_scratch + [pltpu.VMEM((PROBES, 4 * ROWS), F32)],
+        [((SENT, LANES), BF16, 1)],
+        near_args(x0, *halos(low, high)) + of_kind("hbm", leaf_cluster_basis),
+        wide_scratch,
     )
     column, sent, later = lax.optimization_barrier((column, sent, sub))
     got = within(column, asked)
     (weights,) = call(
         weights_kernel,
         "join_couplings",
-        [((PARENTS + 1, 4 * RANK, FAR * RANK), BF16, True)],
+        [((PARENTS + 1, 4 * RANK, FAR * RANK), BF16)],
         of_kind("smem", later) + of_kind("cut", couplings, coarse_couplings),
     )
+
+    def far(got):
+        (field,) = call(
+            field_kernel,
+            "far_field",
+            [((PARENTS,) + tile, BF16)],
+            of_kind("table", far_index, coarse_index)
+            + of_kind("vmem", got, weights, four_transfers),
+            rows_scratch,
+        )
+        return field
+
+    field_scratch = pltpu.VMEM((SUBS, PARENTS) + tile, BF16)
+    field1, pieces = far(got), over_sub([sent] * SUBS)
     near1, basis = call(
         join_kernel,
         "join_near_basis",
-        [((PARENTS, 4 * OWN, UNKNOWNS), BF16, True), ((PARENTS, 4 * RANK, UNKNOWNS), BF16, True)],
-        of_kind("smem", sub) + of_kind("any", *over_sub(sent)),
+        [((PARENTS, 4 * PROBES, UNKNOWNS), BF16), ((PARENTS, 4 * RANK, UNKNOWNS), BF16)],
+        of_kind("smem", sub) + of_kind("hbm", pieces[0]) + of_kind("any", *pieces[1:]),
         [pltpu.VMEM((SUBS, SENT, LANES), BF16)],
     )
-    x1_own, tiles = call(
-        middle_kernel,
-        "middle",
-        [((PARENTS, 4 * OWN, UNKNOWNS), BF16, True), (message, BF16, True)],
-        of_kind("smem", far_index, coarse_index)
-        + of_kind("vmem", got)
-        + of_kind("any", weights)
-        + of_kind("hbm", four_transfers)
-        + of_kind("any", basis, near1),
-        rows_scratch,
-    )
-    got = within(along(tiles), asked)
-    x1, low, high, first = call(
-        whole_kernel,
-        "join_x1",
-        [(x_shape, BF16), (edge, BF16), (edge, BF16), (probes.shape, BF16)],
-        of_kind("smem", sub) + of_kind("any", *over_sub([x1_own] * SUBS)),
-        [pltpu.VMEM((SUBS, PARENTS, 4 * OWN, UNKNOWNS), BF16)],
-    )
-    (near2,) = call(
+    x1, low, high, tiles = call(
+        second_kernel,
+        "second_coefficients",
+        [(x_shape, BF16, 4), (edge, BF16), (edge, BF16), (message, BF16, 1)],
+        of_kind("smem", sub)
+        + of_kind("vmem", *over_sub([field1] * SUBS))
+        + of_kind("vmem", near1, basis, four_transfers),
+        [field_scratch, pltpu.VMEM((4, PROBES, UNKNOWNS), F32)],
+    )
+    column, edges = lax.optimization_barrier((along(tiles), halos(low, high)))
+    got = within(column, asked)
+    near2, first = call(
         near_kernel,
         "near_field",
-        [((LEAVES, PROBES, ROWS), F32)],
-        near_args(x1, low, high),
+        [((LEAVES, PROBES, ROWS), F32), (probes.shape, BF16)],
+        of_kind("smem", sub) + near_args(x1, *edges),
         wide_scratch,
     )
     got, near2 = lax.optimization_barrier((got, near2))
-    (field,) = call(
-        last_field_kernel,
-        "last_field",
-        [((PARENTS,) + tile, BF16)],
-        of_kind("smem", far_index, coarse_index)
-        + of_kind("vmem", got)
-        + of_kind("any", weights)
-        + of_kind("hbm", four_transfers),
-        rows_scratch,
-    )
     (second_apply,) = call(
         output_kernel,
         "output",
         [(probes.shape, BF16)],
         of_kind("smem", sub)
-        + of_kind("vmem", *over_sub([field] * SUBS))
+        + of_kind("vmem", *over_sub([far(got)] * SUBS))
         + of_kind("vmem", near2, four_bases),
-        [pltpu.VMEM((SUBS, PARENTS) + tile, BF16)],
+        [field_scratch],
     )
     return (first, second_apply)
 

time: 124 us -> 113 us (0.911)
  the two profiles are of different devices: /device:TPU:1 before, /device:TPU:96 now
where the time goes in v5:
time: 113 us; the launch traced here: 112 us
  starting transfers between devices  63.6 us (56%)
  Pallas kernels  30.1 us (27%)
  waiting for transfers between devices  12.3 us (11%)
  local copies, waits for them, and re-layouts  4.6 us (4%)
    pallas_call x13, Pallas kernels, call(): pl.pallas_call(body, name=name, out_shape=[pltpu.HBM(out[0], out[1]) if l...  30.1 us
    ppermute x12, starting transfers between devices, over_sub(): lax.ppermute(pieces[k], 'sub', [(i, (i + k) % SUBS) for i in range(SUBS)])  16.5 us
    all_to_all x2, starting transfers between devices, along(): lax.all_to_all(tiles, 'leaf', 0, 0, axis_index_groups=along_z, tiled=True)  14.7 us
    all_to_all x2, starting transfers between devices, within(): lax.all_to_all(chosen, 'leaf', 0, 0, axis_index_groups=in_plane, tiled=True)  13.8 us
    ppermute x2, starting transfers between devices, halos(): lax.ppermute(low, 'leaf', [(i + 1, i) for i in range(groups - 1)])  11.5 us
    ppermute x12, waiting for transfers between devices, over_sub(): lax.ppermute(pieces[k], 'sub', [(i, (i + k) % SUBS) for i in range(SUBS)])  6.84 us
    unnamed x16, local copies, waits for them, and re-layouts  4.6 us
    all_to_all x2, waiting for transfers between devices, within(): lax.all_to_all(chosen, 'leaf', 0, 0, axis_index_groups=in_plane, tiled=True)  4.18 us
  transfers between devices with their start and end apart: 21, of which 10 were waited for; matrix products, arithmetic and copies ran while one was open for 0% of the time, Pallas kernels for 17%

profile of v5, /device:TPU:96, one launch (start us, length us, event | category | flops | bytes accessed | tf_op | source)
XLA Modules:
  0.0 111.7 jit_solution(12894900394349369696)
XLA Ops:
  0.6 1.8 %partial_sums.1 = (bf16[336,128]{1,0:T(8,128)(2,1)S(1)}, bf16[336,128]{1,0:T(8,128)(2,1)S(1)}, bf16[336,128]{1,0:T(8,128)(2,1)S(1)}, bf16[336,128]{1,0:T(8,128)(2,1)S(1)}) custom-call(s32[1]{0:T(128)} %bitcast.refs_0_, bf16[32,16,64]{2,1,0:T(8,128)(2,1)} %refs_1_.4, bf16[4,256,64]{2,1,0:T(8,128)(2,1)} %bitcast.14, bf16[4,256,64]{2,1,0:T(8,128)(2,1)} %bitcast.10), custom_call_target="tpu_custom_call" | custom-call | tf_op jit(solution)/shard_map/partial_sums/pallas_call | solution.py:120
  4.0 2.7 %collective-permute-start.1 = (bf16[336,128]{1,0:T(8,128)(2,1)S(1)}, bf16[336,128]{1,0:T(8,128)(2,1)S(1)}, u32[]{:S(2)}, u32[]{:S(2)}) collective-permute-start(bf16[336,128]{1,0:T(8,128)(2,1)S(1)} %get-tuple-element.50), channel_id=1, source_target_pairs={{0,2},{1,3},{2,0},{3,1},{4,6},{5,7},{6,4},{7,5},{8,10},{9,11},{10,... | collective-permute-start | bytes 258056 | tf_op jit(solution)/shard_map/ppermute | solution.py:479
  8.2 2.8 %index_tables.1 = (s32[8,128]{1,0:T(8,128)}, s32[16,16]{1,0:T(8,128)}, s32[4,16]{1,0:T(4,128)}) custom-call(s32[1]{0:T(128)} %bitcast.1.refs_0_.refs_1_, s32[16,16]{1,0:T(8,128)} %refs_1_.5, s32[4,16]{1,0:T(4,128)} %refs_2_.3), custom_call_target="tpu_custom_call" | custom-call | tf_op jit(solution)/shard_map/index_tables/pallas_call | solution.py:120
  12.1 7.7 %all-to-all-start = ((bf16[8,5,16,128]{3,2,1,0:T(8,128)(2,1)}), bf16[8,5,16,128]{3,2,1,0:T(8,128)(2,1)S(1)}, u32[]{:S(2)}, u32[]{:S(2)}) async-start(bf16[8,5,16,128]{3,2,1,0:T(8,128)(2,1)} %get-tuple-element.57), calls=%async_computation | async-start | bytes 327680 | tf_op jit(solution)/shard_map/all_to_all | solution.py:502
  19.8 1.9 %collective-permute-start.3 = (bf16[4,32,256]{2,1,0:T(8,128)(2,1)S(1)}, bf16[4,32,256]{2,1,0:T(8,128)(2,1)S(1)}, u32[]{:S(2)}, u32[]{:S(2)}) collective-permute-start(bf16[4,32,256]{2,1,0:T(8,128)(2,1)S(1)} %get-tuple-element.62), channel_id=1, source_target_pairs={{0,4},{4,8},{8,12},{12,16},{16,20},{20,24},{24,28},{28,32},{32,36}... | collective-permute-start | bytes 196616 | tf_op jit(solution)/shard_map/ppermute | solution.py:492
  21.7 5.8 %collective-permute-start.4 = (bf16[4,32,256]{2,1,0:T(8,128)(2,1)S(1)}, bf16[4,32,256]{2,1,0:T(8,128)(2,1)S(1)}, u32[]{:S(2)}, u32[]{:S(2)}) collective-permute-start(bf16[4,32,256]{2,1,0:T(8,128)(2,1)S(1)} %get-tuple-element.63), channel_id=1, source_target_pairs={{4,0},{8,4},{12,8},{16,12},{20,16},{24,20},{28,24},{32,28},{36,32}... | collective-permute-start | bytes 196616 | tf_op jit(solution)/shard_map/ppermute | solution.py:493
  27.5 3.3 %all-to-all-start.1 = ((s32[8,1,128]{2,1,0:T(1,128)}), s32[8,1,128]{2,1,0:T(1,128)S(1)}, u32[]{:S(2)}, u32[]{:S(2)}) async-start(s32[8,1,128]{2,1,0:T(1,128)} %bitcast.5), calls=%async_computation.1 | async-start | bytes 8192 | tf_op jit(solution)/shard_map/all_to_all | solution.py:542
  30.9 5.0 %near_field_sent.1.refs_1_ = bf16[768,128]{1,0:T(8,128)(2,1)} custom-call(s32[1]{0:T(128)} %bitcast.1.refs_0_.refs_1_, s32[16,9]{1,0:T(8,128)} %refs_2_.5, bf16[16,32,256]{2,1,0:T(8,128)(2,1)} %get-tuple-element.61.refs_2_, bf16[4,32,256]{2,1,0:T(8,128)(2,1)S(1)} %collective-permute-done.3.refs_3_, bf16[4,32,256]{2,1,0:T(8,128)(2,1)S(1)} %collective-permute-done.4.refs_4_, ...), custom_call_target="tpu_custom_call" | custom-call | tf_op jit(solution)/shard_map/near_field_sent/pallas_call | solution.py:120
  37.5 6.2 %all-to-all-start.2 = ((bf16[8,12,16,128]{3,2,1,0:T(8,128)(2,1)}), bf16[8,12,16,128]{3,2,1,0:T(8,128)(2,1)S(1)}, u32[]{:S(2)}, u32[]{:S(2)}) async-start(bf16[8,12,16,128]{3,2,1,0:T(8,128)(2,1)} %choose_rows.2), calls=%async_computation.2 | async-start | bytes 786432 | tf_op jit(solution)/shard_map/all_to_all | solution.py:512
  43.7 2.6 %collective-permute-start.10 = (bf16[768,128]{1,0:T(8,128)(2,1)}, bf16[768,128]{1,0:T(8,128)(2,1)S(1)}, u32[]{:S(2)}, u32[]{:S(2)}) collective-permute-start(bf16[768,128]{1,0:T(8,128)(2,1)} %near_field_sent.1.refs_1_), channel_id=1, source_target_pairs={{0,3},{1,0},{2,1},{3,2},{4,7},{5,4},{6,5},{7,6},{8,11},{9,8},{10,9... | collective-permute-start | bytes 589832 | tf_op jit(solution)/shard_map/ppermute | solution.py:479
  47.4 2.9 %join_couplings.1.refs_3_ = bf16[5,256,1024]{2,1,0:T(8,128)(2,1)S(1)} custom-call(s32[1]{0:T(128)} %bitcast.refs_0_, bf16[16,16,64,64]{3,2,1,0:T(8,128)(2,1)} %refs_1_.7, bf16[4,16,64,64]{3,2,1,0:T(8,128)(2,1)} %refs_2_.4), custom_call_target="tpu_custom_call" | custom-call | tf_op jit(solution)/shard_map/join_couplings/pallas_call | solution.py:120
  50.3 2.4 %all-to-all-done.2 = bf16[8,12,16,128]{3,2,1,0:T(8,128)(2,1)S(1)} async-done(((bf16[8,12,16,128]{3,2,1,0:T(8,128)(2,1)}), bf16[8,12,16,128]{3,2,1,0:T(8,128)(2,1)S(1)}, u32[]{:S(2)}, u32[]{:S(2)}) %all-to-all-start.2) | async-done | bytes 393248 | tf_op jit(solution)/shard_map/all_to_all | solution.py:512
  52.7 2.0 %far_field.2.refs_1_ = bf16[4,16,128]{2,1,0:T(8,128)(2,1)S(1)} custom-call(s32[16,16]{1,0:T(8,128)} %get-tuple-element.46.refs_0_, s32[4,16]{1,0:T(4,128)} %get-tuple-element.47.refs_1_, bf16[96,16,128]{2,1,0:T(8,128)(2,1)S(1)} %bitcast.16, bf16[5,256,1024]{2,1,0:T(8,128)(2,1)S(1)} %join_couplings.1.refs_3_, bf16[4,256,64]{2,1,0:T(8,128)(2,1)S(1)} %bitcast.11), custom_call_target="tpu_custom_call" | custom-call | tf_op jit(solution)/shard_map/far_field/pallas_call | solution.py:120
  54.7 2.7 %collective-permute-start.7 = (bf16[4,16,128]{2,1,0:T(8,128)(2,1)S(1)}, bf16[4,16,128]{2,1,0:T(8,128)(2,1)S(1)}, u32[]{:S(2)}, u32[]{:S(2)}) collective-permute-start(bf16[4,16,128]{2,1,0:T(8,128)(2,1)S(1)} %far_field.2.refs_1_), channel_id=1, source_target_pairs={{0,3},{1,0},{2,1},{3,2},{4,7},{5,4},{6,5},{7,6},{8,11},{9,8},{10,9... | collective-permute-start | bytes 49160 | tf_op jit(solution)/shard_map/ppermute | solution.py:479
  60.7 2.0 %collective-permute-done.6.refs_3_ = bf16[4,16,128]{2,1,0:T(8,128)(2,1)S(1)} collective-permute-done((bf16[4,16,128]{2,1,0:T(8,128)(2,1)S(1)}, bf16[4,16,128]{2,1,0:T(8,128)(2,1)S(1)}, u32[]{:S(2)}, u32[]{:S(2)}) %collective-permute-start.6) | collective-permute-done | bytes 16416 | tf_op jit(solution)/shard_map/ppermute | solution.py:479
  62.9 2.4 %second_coefficients.1 = (bf16[16,32,256]{2,1,0:T(8,128)(2,1)}, bf16[4,32,256]{2,1,0:T(8,128)(2,1)S(1)}, bf16[4,32,256]{2,1,0:T(8,128)(2,1)S(1)}, bf16[8,5,16,128]{3,2,1,0:T(8,128)(2,1)}) custom-call(s32[1]{0:T(128)} %bitcast.refs_0_, bf16[4,16,128]{2,1,0:T(8,128)(2,1)S(1)} %far_field.2.refs_1_, bf16[4,16,128]{2,1,0:T(8,128)(2,1)S(1)} %collective-permute-done.5.refs_2_, ...), custom_call_target="tpu_custom_call" | custom-call | tf_op jit(solution)/shard_map/second_coefficients/pallas_call | solution.py:120
  65.3 7.0 %all-to-all-start.3 = ((bf16[8,5,16,128]{3,2,1,0:T(8,128)(2,1)}), bf16[8,5,16,128]{3,2,1,0:T(8,128)(2,1)S(1)}, u32[]{:S(2)}, u32[]{:S(2)}) async-start(bf16[8,5,16,128]{3,2,1,0:T(8,128)(2,1)} %get-tuple-element.70), calls=%async_computation.3 | async-start | bytes 327680 | tf_op jit(solution)/shard_map/all_to_all | solution.py:502
  72.3 1.9 %collective-permute-start.11 = (bf16[4,32,256]{2,1,0:T(8,128)(2,1)S(1)}, bf16[4,32,256]{2,1,0:T(8,128)(2,1)S(1)}, u32[]{:S(2)}, u32[]{:S(2)}) collective-permute-start(bf16[4,32,256]{2,1,0:T(8,128)(2,1)S(1)} %get-tuple-element.71), channel_id=1, source_target_pairs={{0,4},{4,8},{8,12},{12,16},{16,20},{20,24},{24,28},{28,32},{32,36}... | collective-permute-start | bytes 196616 | tf_op jit(solution)/shard_map/ppermute | solution.py:492
  74.2 5.8 %collective-permute-start.12 = (bf16[4,32,256]{2,1,0:T(8,128)(2,1)S(1)}, bf16[4,32,256]{2,1,0:T(8,128)(2,1)S(1)}, u32[]{:S(2)}, u32[]{:S(2)}) collective-permute-start(bf16[4,32,256]{2,1,0:T(8,128)(2,1)S(1)} %get-tuple-element.72), channel_id=1, source_target_pairs={{4,0},{8,4},{12,8},{16,12},{20,16},{24,20},{28,24},{32,28},{36,32}... | collective-permute-start | bytes 196616 | tf_op jit(solution)/shard_map/ppermute | solution.py:493
  84.1 7.6 %all-to-all-start.4 = ((bf16[8,12,16,128]{3,2,1,0:T(8,128)(2,1)}), bf16[8,12,16,128]{3,2,1,0:T(8,128)(2,1)S(1)}, u32[]{:S(2)}, u32[]{:S(2)}) async-start(bf16[8,12,16,128]{3,2,1,0:T(8,128)(2,1)} %choose_rows.3), calls=%async_computation.4 | async-start | bytes 786432 | tf_op jit(solution)/shard_map/all_to_all | solution.py:512
  93.3 4.8 %near_field.1 = (f32[16,32,64]{2,1,0:T(8,128)S(1)}, bf16[32,16,64]{2,1,0:T(8,128)(2,1)}) custom-call(s32[1]{0:T(128)} %bitcast.refs_0_, s32[1]{0:T(128)} %bitcast.1.refs_0_.refs_1_, s32[16,9]{1,0:T(8,128)} %refs_2_.5, bf16[16,32,256]{2,1,0:T(8,128)(2,1)} %get-tuple-element.69.refs_3_, bf16[4,32,256]{2,1,0:T(8,128)(2,1)S(1)} %copy-done.5, ...), custom_call_target="tpu_custom_call" | custom-call | tf_op jit(solution)/shard_map/near_field/pallas_call | solution.py:120
  98.9 1.8 %all-to-all-done.4 = bf16[8,12,16,128]{3,2,1,0:T(8,128)(2,1)S(1)} async-done(((bf16[8,12,16,128]{3,2,1,0:T(8,128)(2,1)}), bf16[8,12,16,128]{3,2,1,0:T(8,128)(2,1)S(1)}, u32[]{:S(2)}, u32[]{:S(2)}) %all-to-all-start.4) | async-done | bytes 393248 | tf_op jit(solution)/shard_map/all_to_all | solution.py:512
  100.6 2.0 %far_field.3.refs_1_ = bf16[4,16,128]{2,1,0:T(8,128)(2,1)S(1)} custom-call(s32[16,16]{1,0:T(8,128)} %get-tuple-element.46.refs_0_, s32[4,16]{1,0:T(4,128)} %get-tuple-element.47.refs_1_, bf16[96,16,128]{2,1,0:T(8,128)(2,1)S(1)} %bitcast.17, bf16[5,256,1024]{2,1,0:T(8,128)(2,1)S(1)} %join_couplings.1.refs_3_, bf16[4,256,64]{2,1,0:T(8,128)(2,1)S(1)} %bitcast.13), custom_call_target="tpu_custom_call" | custom-call | tf_op jit(solution)/shard_map/far_field/pallas_call | solution.py:120
  106.5 2.1 %collective-permute-done.14.refs_3_ = bf16[4,16,128]{2,1,0:T(8,128)(2,1)S(1)} collective-permute-done((bf16[4,16,128]{2,1,0:T(8,128)(2,1)S(1)}, bf16[4,16,128]{2,1,0:T(8,128)(2,1)S(1)}, u32[]{:S(2)}, u32[]{:S(2)}) %collective-permute-start.14) | collective-permute-done | bytes 16416 | tf_op jit(solution)/shard_map/ppermute | solution.py:479
  (47 shorter events, 23.3 us)
Async XLA Ops:
  2.5 8.5 %collective-permute-start = (bf16[336,128]{1,0:T(8,128)(2,1)S(1)}, bf16[336,128]{1,0:T(8,128)(2,1)S(1)}, u32[]{:S(2)}, u32[]{:S(2)}) collective-permute-start(bf16[336,128]{1,0:T(8,128)(2,1)S(1)} %get-tuple-element.49), channel_id=1, source_target_pairs={{0,1},{1,2},{2,3},{3,0},{4,5},{5,6},{6,7},{7,4},{8,9},{9,10},{10,1... | collective-permute-start | bytes 258056 | tf_op jit(solution)/shard_map/ppermute | solution.py:479
  4.0 6.9 %collective-permute-start.1 = (bf16[336,128]{1,0:T(8,128)(2,1)S(1)}, bf16[336,128]{1,0:T(8,128)(2,1)S(1)}, u32[]{:S(2)}, u32[]{:S(2)}) collective-permute-start(bf16[336,128]{1,0:T(8,128)(2,1)S(1)} %get-tuple-element.50), channel_id=1, source_target_pairs={{0,2},{1,3},{2,0},{3,1},{4,6},{5,7},{6,4},{7,5},{8,10},{9,11},{10,... | collective-permute-start | bytes 258056 | tf_op jit(solution)/shard_map/ppermute | solution.py:479
  6.8 4.5 %collective-permute-start.2 = (bf16[336,128]{1,0:T(8,128)(2,1)S(1)}, bf16[336,128]{1,0:T(8,128)(2,1)S(1)}, u32[]{:S(2)}, u32[]{:S(2)}) collective-permute-start(bf16[336,128]{1,0:T(8,128)(2,1)S(1)} %get-tuple-element.51), channel_id=1, source_target_pairs={{0,3},{1,0},{2,1},{3,2},{4,7},{5,4},{6,5},{7,6},{8,11},{9,8},{10,9... | collective-permute-start | bytes 258056 | tf_op jit(solution)/shard_map/ppermute | solution.py:479
  12.1 15.4 %all-to-all-start = ((bf16[8,5,16,128]{3,2,1,0:T(8,128)(2,1)}), bf16[8,5,16,128]{3,2,1,0:T(8,128)(2,1)S(1)}, u32[]{:S(2)}, u32[]{:S(2)}) async-start(bf16[8,5,16,128]{3,2,1,0:T(8,128)(2,1)} %get-tuple-element.57), calls=%async_computation | async-start | bytes 327680 | tf_op jit(solution)/shard_map/all_to_all | solution.py:502
  19.8 11.0 %collective-permute-start.3 = (bf16[4,32,256]{2,1,0:T(8,128)(2,1)S(1)}, bf16[4,32,256]{2,1,0:T(8,128)(2,1)S(1)}, u32[]{:S(2)}, u32[]{:S(2)}) collective-permute-start(bf16[4,32,256]{2,1,0:T(8,128)(2,1)S(1)} %get-tuple-element.62), channel_id=1, source_target_pairs={{0,4},{4,8},{8,12},{12,16},{16,20},{20,24},{24,28},{28,32},{32,36}... | collective-permute-start | bytes 196616 | tf_op jit(solution)/shard_map/ppermute | solution.py:492
  21.7 9.1 %collective-permute-start.4 = (bf16[4,32,256]{2,1,0:T(8,128)(2,1)S(1)}, bf16[4,32,256]{2,1,0:T(8,128)(2,1)S(1)}, u32[]{:S(2)}, u32[]{:S(2)}) collective-permute-start(bf16[4,32,256]{2,1,0:T(8,128)(2,1)S(1)} %get-tuple-element.63), channel_id=1, source_target_pairs={{4,0},{8,4},{12,8},{16,12},{20,16},{24,20},{28,24},{32,28},{36,32}... | collective-permute-start | bytes 196616 | tf_op jit(solution)/shard_map/ppermute | solution.py:493
  27.5 8.4 %all-to-all-start.1 = ((s32[8,1,128]{2,1,0:T(1,128)}), s32[8,1,128]{2,1,0:T(1,128)S(1)}, u32[]{:S(2)}, u32[]{:S(2)}) async-start(s32[8,1,128]{2,1,0:T(1,128)} %bitcast.5), calls=%async_computation.1 | async-start | bytes 8192 | tf_op jit(solution)/shard_map/all_to_all | solution.py:542
  37.5 15.2 %copy-start = (bf16[16,64,64]{2,1,0:T(8,128)(2,1)S(1)}, bf16[16,64,64]{2,1,0:T(8,128)(2,1)}, u32[]{:S(2)}) copy-start(bf16[16,64,64]{2,1,0:T(8,128)(2,1)} %param.12) | copy-start | bytes 393220
  37.5 15.2 %all-to-all-start.2 = ((bf16[8,12,16,128]{3,2,1,0:T(8,128)(2,1)}), bf16[8,12,16,128]{3,2,1,0:T(8,128)(2,1)S(1)}, u32[]{:S(2)}, u32[]{:S(2)}) async-start(bf16[8,12,16,128]{3,2,1,0:T(8,128)(2,1)} %choose_rows.2), calls=%async_computation.2 | async-start | bytes 786432 | tf_op jit(solution)/shard_map/all_to_all | solution.py:512
  43.7 14.1 %collective-permute-start.10 = (bf16[768,128]{1,0:T(8,128)(2,1)}, bf16[768,128]{1,0:T(8,128)(2,1)S(1)}, u32[]{:S(2)}, u32[]{:S(2)}) collective-permute-start(bf16[768,128]{1,0:T(8,128)(2,1)} %near_field_sent.1.refs_1_), channel_id=1, source_target_pairs={{0,3},{1,0},{2,1},{3,2},{4,7},{5,4},{6,5},{7,6},{8,11},{9,8},{10,9... | collective-permute-start | bytes 589832 | tf_op jit(solution)/shard_map/ppermute | solution.py:479
  46.4 12.1 %collective-permute-start.9 = (bf16[768,128]{1,0:T(8,128)(2,1)}, bf16[768,128]{1,0:T(8,128)(2,1)}, u32[]{:S(2)}, u32[]{:S(2)}) collective-permute-start(bf16[768,128]{1,0:T(8,128)(2,1)} %near_field_sent.1.refs_1_), channel_id=1, source_target_pairs={{0,2},{1,3},{2,0},{3,1},{4,6},{5,7},{6,4},{7,5},{8,10},{9,11},{10,... | collective-permute-start | bytes 589832 | tf_op jit(solution)/shard_map/ppermute | solution.py:479
  46.7 12.5 %collective-permute-start.8 = (bf16[768,128]{1,0:T(8,128)(2,1)}, bf16[768,128]{1,0:T(8,128)(2,1)}, u32[]{:S(2)}, u32[]{:S(2)}) collective-permute-start(bf16[768,128]{1,0:T(8,128)(2,1)} %near_field_sent.1.refs_1_), channel_id=1, source_target_pairs={{0,1},{1,2},{2,3},{3,0},{4,5},{5,6},{6,7},{7,4},{8,9},{9,10},{10,1... | collective-permute-start | bytes 589832 | tf_op jit(solution)/shard_map/ppermute | solution.py:479
  54.7 6.0 %collective-permute-start.7 = (bf16[4,16,128]{2,1,0:T(8,128)(2,1)S(1)}, bf16[4,16,128]{2,1,0:T(8,128)(2,1)S(1)}, u32[]{:S(2)}, u32[]{:S(2)}) collective-permute-start(bf16[4,16,128]{2,1,0:T(8,128)(2,1)S(1)} %far_field.2.refs_1_), channel_id=1, source_target_pairs={{0,3},{1,0},{2,1},{3,2},{4,7},{5,4},{6,5},{7,6},{8,11},{9,8},{10,9... | collective-permute-start | bytes 49160 | tf_op jit(solution)/shard_map/ppermute | solution.py:479
  57.5 5.2 %collective-permute-start.6 = (bf16[4,16,128]{2,1,0:T(8,128)(2,1)S(1)}, bf16[4,16,128]{2,1,0:T(8,128)(2,1)S(1)}, u32[]{:S(2)}, u32[]{:S(2)}) collective-permute-start(bf16[4,16,128]{2,1,0:T(8,128)(2,1)S(1)} %far_field.2.refs_1_), channel_id=1, source_target_pairs={{0,2},{1,3},{2,0},{3,1},{4,6},{5,7},{6,4},{7,5},{8,10},{9,11},{10,... | collective-permute-start | bytes 49160 | tf_op jit(solution)/shard_map/ppermute | solution.py:479
  57.8 5.0 %collective-permute-start.5 = (bf16[4,16,128]{2,1,0:T(8,128)(2,1)S(1)}, bf16[4,16,128]{2,1,0:T(8,128)(2,1)S(1)}, u32[]{:S(2)}, u32[]{:S(2)}) collective-permute-start(bf16[4,16,128]{2,1,0:T(8,128)(2,1)S(1)} %far_field.2.refs_1_), channel_id=1, source_target_pairs={{0,1},{1,2},{2,3},{3,0},{4,5},{5,6},{6,7},{7,4},{8,9},{9,10},{10,1... | collective-permute-start | bytes 49160 | tf_op jit(solution)/shard_map/ppermute | solution.py:479
  65.3 17.2 %all-to-all-start.3 = ((bf16[8,5,16,128]{3,2,1,0:T(8,128)(2,1)}), bf16[8,5,16,128]{3,2,1,0:T(8,128)(2,1)S(1)}, u32[]{:S(2)}, u32[]{:S(2)}) async-start(bf16[8,5,16,128]{3,2,1,0:T(8,128)(2,1)} %get-tuple-element.70), calls=%async_computation.3 | async-start | bytes 327680 | tf_op jit(solution)/shard_map/all_to_all | solution.py:502
  72.3 7.7 %collective-permute-start.11 = (bf16[4,32,256]{2,1,0:T(8,128)(2,1)S(1)}, bf16[4,32,256]{2,1,0:T(8,128)(2,1)S(1)}, u32[]{:S(2)}, u32[]{:S(2)}) collective-permute-start(bf16[4,32,256]{2,1,0:T(8,128)(2,1)S(1)} %get-tuple-element.71), channel_id=1, source_target_pairs={{0,4},{4,8},{8,12},{12,16},{16,20},{20,24},{24,28},{28,32},{32,36}... | collective-permute-start | bytes 196616 | tf_op jit(solution)/shard_map/ppermute | solution.py:492
  74.2 7.6 %collective-permute-start.12 = (bf16[4,32,256]{2,1,0:T(8,128)(2,1)S(1)}, bf16[4,32,256]{2,1,0:T(8,128)(2,1)S(1)}, u32[]{:S(2)}, u32[]{:S(2)}) collective-permute-start(bf16[4,32,256]{2,1,0:T(8,128)(2,1)S(1)} %get-tuple-element.72), channel_id=1, source_target_pairs={{4,0},{8,4},{12,8},{16,12},{20,16},{24,20},{28,24},{32,28},{36,32}... | collective-permute-start | bytes 196616 | tf_op jit(solution)/shard_map/ppermute | solution.py:493
  84.1 16.6 %all-to-all-start.4 = ((bf16[8,12,16,128]{3,2,1,0:T(8,128)(2,1)}), bf16[8,12,16,128]{3,2,1,0:T(8,128)(2,1)S(1)}, u32[]{:S(2)}, u32[]{:S(2)}) async-start(bf16[8,12,16,128]{3,2,1,0:T(8,128)(2,1)} %choose_rows.3), calls=%async_computation.4 | async-start | bytes 786432 | tf_op jit(solution)/shard_map/all_to_all | solution.py:512
  93.3 16.3 %copy-start.1 = (bf16[16,64,64]{2,1,0:T(8,128)(2,1)S(1)}, bf16[16,64,64]{2,1,0:T(8,128)(2,1)}, u32[]{:S(2)}) copy-start(bf16[16,64,64]{2,1,0:T(8,128)(2,1)} %refs_6_.2) | copy-start | bytes 393220
  102.7 3.8 %collective-permute-start.15 = (bf16[4,16,128]{2,1,0:T(8,128)(2,1)S(1)}, bf16[4,16,128]{2,1,0:T(8,128)(2,1)S(1)}, u32[]{:S(2)}, u32[]{:S(2)}) collective-permute-start(bf16[4,16,128]{2,1,0:T(8,128)(2,1)S(1)} %far_field.3.refs_1_), channel_id=1, source_target_pairs={{0,3},{1,0},{2,1},{3,2},{4,7},{5,4},{6,5},{7,6},{8,11},{9,8},{10,9... | collective-permute-start | bytes 49160 | tf_op jit(solution)/shard_map/ppermute | solution.py:479
  103.3 5.3 %collective-permute-start.14 = (bf16[4,16,128]{2,1,0:T(8,128)(2,1)S(1)}, bf16[4,16,128]{2,1,0:T(8,128)(2,1)S(1)}, u32[]{:S(2)}, u32[]{:S(2)}) collective-permute-start(bf16[4,16,128]{2,1,0:T(8,128)(2,1)S(1)} %far_field.3.refs_1_), channel_id=1, source_target_pairs={{0,2},{1,3},{2,0},{3,1},{4,6},{5,7},{6,4},{7,5},{8,10},{9,11},{10,... | collective-permute-start | bytes 49160 | tf_op jit(solution)/shard_map/ppermute | solution.py:479
  104.7 4.9 %collective-permute-start.13 = (bf16[4,16,128]{2,1,0:T(8,128)(2,1)S(1)}, bf16[4,16,128]{2,1,0:T(8,128)(2,1)S(1)}, u32[]{:S(2)}, u32[]{:S(2)}) collective-permute-start(bf16[4,16,128]{2,1,0:T(8,128)(2,1)S(1)} %far_field.3.refs_1_), channel_id=1, source_target_pairs={{0,1},{1,2},{2,3},{3,0},{4,5},{5,6},{6,7},{7,4},{8,9},{9,10},{10,1... | collective-permute-start | bytes 49160 | tf_op jit(solution)/shard_map/ppermute | solution.py:479
  109.7 1.0 copy-start.3
  (5 other events, 3.7 us)

commit v6 on v5

--- a/solution.py
+++ b/solution.py
@@ -58,6 +58,8 @@
 
     def __getitem__(self, index):
         first = index[0] if isinstance(index, tuple) else index
+        if isinstance(first, slice) and first.start is not None:
+            first = first.start
         self.finish(first // self.size if isinstance(first, int) else None)
         return self.target[index]
 
@@ -267,10 +269,9 @@
     for q in range(PARENTS + 1):
         for c in range(4):
             for k in range(0, FAR, 2):
-                if q < PARENTS:
-                    pair = [couplings_ref[4 * q + c, k], couplings_ref[4 * q + c, k + 1]]
-                else:
-                    pair = [coarse_ref[c, k], coarse_ref[c, k + 1]]
+                ref, i = (couplings_ref, 4 * q + c) if q < PARENTS else (coarse_ref, c)
+                n = (i * FAR + k) * RANK
+                pair = [ref[n : n + RANK], ref[n + RANK : n + 2 * RANK]]
                 both = jnp.concatenate(pair, axis=1)
                 out_ref[q, pl.ds(c * RANK, RANK), pl.ds(k * RANK, LANES)] = both
 
@@ -420,7 +421,8 @@
         four = []
         for i in range(4 * q, 4 * q + 4):
             x = jnp.concatenate([of_slot(i, k) for k in range(NEAR)], axis=1)
-            blocks = jnp.concatenate([blocks_ref[i, k] for k in range(NEAR)], axis=1)
+            starts = [(i * NEAR + k) * ROWS for k in range(NEAR)]
+            blocks = jnp.concatenate([blocks_ref[n : n + ROWS] for n in starts], axis=1)
             four.append(dot_nt(x, blocks))
         yield four
 
@@ -445,6 +447,7 @@
     for q, four in enumerate(parts):
         for c in range(4):
             out_ref[4 * q + c] = four[c]
+        out_ref.send(q)
     outs = []
     for i in range(LEAVES):
         x = x_ref[i].astype(F32)
@@ -493,10 +496,10 @@
         from_above = lax.ppermute(low, "leaf", [(i + 1, i) for i in range(groups - 1)])
         return from_below, from_above
 
-    def near_args(x, from_below, from_above):
+    def near_args(x, from_below, from_above, where):
         tables = of_kind("smem", first_leaf) + of_kind("table", near_list)
-        edges = of_kind("vmem", from_below, from_above)
-        return tables + of_kind("hbm", x) + edges + of_kind("cut", near_blocks)
+        blocks = of_kind("cut", near_blocks.reshape(-1, UNKNOWNS))
+        return tables + of_kind("hbm", x) + of_kind(where, from_below, from_above) + blocks
 
     def along(tiles):
         return lax.all_to_all(tiles, "leaf", 0, 0, axis_index_groups=along_z, tiled=True)
@@ -544,7 +547,7 @@
         near_sent_kernel,
         "near_field_sent",
         [((SENT, LANES), BF16, 1)],
-        near_args(x0, *halos(low, high)) + of_kind("hbm", leaf_cluster_basis),
+        near_args(x0, *halos(low, high), "vmem") + of_kind("hbm", leaf_cluster_basis),
         wide_scratch,
     )
     column, sent, later = lax.optimization_barrier((column, sent, sub))
@@ -553,7 +556,7 @@
         weights_kernel,
         "join_couplings",
         [((PARENTS + 1, 4 * RANK, FAR * RANK), BF16)],
-        of_kind("smem", later) + of_kind("cut", couplings, coarse_couplings),
+        of_kind("smem", later) + of_kind("cut", couplings.reshape(-1, RANK), coarse_couplings.reshape(-1, RANK)),
     )
 
     def far(got):
@@ -590,8 +593,8 @@
     near2, first = call(
         near_kernel,
         "near_field",
-        [((LEAVES, PROBES, ROWS), F32), (probes.shape, BF16)],
-        of_kind("smem", sub) + near_args(x1, *edges),
+        [((LEAVES, PROBES, ROWS), F32, 4), (probes.shape, BF16)],
+        of_kind("smem", sub) + near_args(x1, *edges, "hbm"),
         wide_scratch,
     )
     got, near2 = lax.optimization_barrier((got, near2))
@@ -601,7 +604,8 @@
         [(probes.shape, BF16)],
         of_kind("smem", sub)
         + of_kind("vmem", *over_sub([far(got)] * SUBS))
-        + of_kind("vmem", near2, four_bases),
+        + of_kind("hbm", near2)
+        + of_kind("vmem", four_bases),
         [field_scratch],
     )
     return (first, second_apply)

time: 113 us -> 112 us (level)
  local copies, waits for them, and re-layouts: 4.6 us -> 0.63 us
  waiting for transfers between devices: 12.3 us -> 14 us
  Pallas kernels: 30.1 us -> 31.7 us
    unnamed x16 -> x6, local copies, waits for them, and re-layouts: 4.6 us -> 0.63 us
    all_to_all x2, waiting for transfers between devices: 4.18 us -> 5.87 us  [within(): lax.all_to_all(chosen, 'leaf', 0, 0, axis_index_groups=in_plane, tiled=True)]
    pallas_call x13, Pallas kernels: 30.1 us -> 31.7 us  [call(): pl.pallas_call(body, name=name, out_shape=[pltpu.HBM(out[0], out[1]) if l...]
  transfers between devices with their start and end apart: 21 -> 21, of which waited for: 10 -> 10; matrix products, arithmetic and copies ran while one was open for 0% -> 0% of each run, Pallas kernels for 17% -> 18%
where the time goes in v6:
time: 112 us; the launch traced here: 111 us
  starting transfers between devices  63.7 us (57%)
  Pallas kernels  31.7 us (28%)
  waiting for transfers between devices  14 us (12%)
    pallas_call x13, Pallas kernels, call(): pl.pallas_call(body, name=name, out_shape=[pltpu.HBM(out[0], out[1]) if l...  31.7 us
    ppermute x12, starting transfers between devices, over_sub(): lax.ppermute(pieces[k], 'sub', [(i, (i + k) % SUBS) for i in range(SUBS)])  16.4 us
    all_to_all x2, starting transfers between devices, along(): lax.all_to_all(tiles, 'leaf', 0, 0, axis_index_groups=along_z, tiled=True)  14.7 us
    all_to_all x2, starting transfers between devices, within(): lax.all_to_all(chosen, 'leaf', 0, 0, axis_index_groups=in_plane, tiled=True)  13.9 us
    ppermute x2, starting transfers between devices, halos(): lax.ppermute(low, 'leaf', [(i + 1, i) for i in range(groups - 1)])  11.5 us
    ppermute x12, waiting for transfers between devices, over_sub(): lax.ppermute(pieces[k], 'sub', [(i, (i + k) % SUBS) for i in range(SUBS)])  6.87 us
    all_to_all x2, waiting for transfers between devices, within(): lax.all_to_all(chosen, 'leaf', 0, 0, axis_index_groups=in_plane, tiled=True)  5.87 us
    ppermute x2, starting transfers between devices, halos(): lax.ppermute(high, 'leaf', [(i, i + 1) for i in range(groups - 1)])  3.82 us
  transfers between devices with their start and end apart: 21, of which 10 were waited for; matrix products, arithmetic and copies ran while one was open for 0% of the time, Pallas kernels for 18%

profile of v6, /device:TPU:96, one launch (start us, length us, event | category | flops | bytes accessed | tf_op | source)
XLA Modules:
  0.0 111.1 jit_solution(13908490865670619763)
XLA Ops:
  4.0 2.7 %collective-permute-start.1 = (bf16[336,128]{1,0:T(8,128)(2,1)S(1)}, bf16[336,128]{1,0:T(8,128)(2,1)S(1)}, u32[]{:S(2)}, u32[]{:S(2)}) collective-permute-start(bf16[336,128]{1,0:T(8,128)(2,1)S(1)} %get-tuple-element.50), channel_id=1, source_target_pairs={{0,2},{1,3},{2,0},{3,1},{4,6},{5,7},{6,4},{7,5},{8,10},{9,11},{10,... | collective-permute-start | bytes 258056 | tf_op jit(solution)/shard_map/ppermute | solution.py:482
  8.2 2.7 %index_tables.1 = (s32[8,128]{1,0:T(8,128)}, s32[16,16]{1,0:T(8,128)}, s32[4,16]{1,0:T(4,128)}) custom-call(s32[1]{0:T(128)} %bitcast.1.refs_0_.refs_1_, s32[16,16]{1,0:T(8,128)} %refs_1_.4, s32[4,16]{1,0:T(4,128)} %refs_2_.2), custom_call_target="tpu_custom_call" | custom-call | tf_op jit(solution)/shard_map/index_tables/pallas_call | solution.py:122
  12.2 7.7 %all-to-all-start = ((bf16[8,5,16,128]{3,2,1,0:T(8,128)(2,1)}), bf16[8,5,16,128]{3,2,1,0:T(8,128)(2,1)S(1)}, u32[]{:S(2)}, u32[]{:S(2)}) async-start(bf16[8,5,16,128]{3,2,1,0:T(8,128)(2,1)} %get-tuple-element.57), calls=%async_computation | async-start | bytes 327680 | tf_op jit(solution)/shard_map/all_to_all | solution.py:505
  19.8 1.9 %collective-permute-start.3 = (bf16[4,32,256]{2,1,0:T(8,128)(2,1)S(1)}, bf16[4,32,256]{2,1,0:T(8,128)(2,1)S(1)}, u32[]{:S(2)}, u32[]{:S(2)}) collective-permute-start(bf16[4,32,256]{2,1,0:T(8,128)(2,1)S(1)} %get-tuple-element.62), channel_id=1, source_target_pairs={{0,4},{4,8},{8,12},{12,16},{16,20},{20,24},{24,28},{28,32},{32,36}... | collective-permute-start | bytes 196616 | tf_op jit(solution)/shard_map/ppermute | solution.py:495
  21.7 5.8 %collective-permute-start.4 = (bf16[4,32,256]{2,1,0:T(8,128)(2,1)S(1)}, bf16[4,32,256]{2,1,0:T(8,128)(2,1)S(1)}, u32[]{:S(2)}, u32[]{:S(2)}) collective-permute-start(bf16[4,32,256]{2,1,0:T(8,128)(2,1)S(1)} %get-tuple-element.63), channel_id=1, source_target_pairs={{4,0},{8,4},{12,8},{16,12},{20,16},{24,20},{28,24},{32,28},{36,32}... | collective-permute-start | bytes 196616 | tf_op jit(solution)/shard_map/ppermute | solution.py:496
  27.5 3.3 %all-to-all-start.1 = ((s32[8,1,128]{2,1,0:T(1,128)}), s32[8,1,128]{2,1,0:T(1,128)S(1)}, u32[]{:S(2)}, u32[]{:S(2)}) async-start(s32[8,1,128]{2,1,0:T(1,128)} %bitcast.5), calls=%async_computation.1 | async-start | bytes 8192 | tf_op jit(solution)/shard_map/all_to_all | solution.py:545
  30.9 5.0 %near_field_sent.1.refs_1_ = bf16[768,128]{1,0:T(8,128)(2,1)} custom-call(s32[1]{0:T(128)} %bitcast.1.refs_0_.refs_1_, s32[16,9]{1,0:T(8,128)} %refs_2_.3, bf16[16,32,256]{2,1,0:T(8,128)(2,1)} %get-tuple-element.61.refs_2_, bf16[4,32,256]{2,1,0:T(8,128)(2,1)S(1)} %collective-permute-done.3.refs_3_, bf16[4,32,256]{2,1,0:T(8,128)(2,1)S(1)} %collective-permute-done.4.refs_4_, ...), custom_call_target="tpu_custom_call" | custom-call | tf_op jit(solution)/shard_map/near_field_sent/pallas_call | solution.py:122
  37.5 6.2 %all-to-all-start.2 = ((bf16[8,12,16,128]{3,2,1,0:T(8,128)(2,1)}), bf16[8,12,16,128]{3,2,1,0:T(8,128)(2,1)S(1)}, u32[]{:S(2)}, u32[]{:S(2)}) async-start(bf16[8,12,16,128]{3,2,1,0:T(8,128)(2,1)} %choose_rows.2), calls=%async_computation.2 | async-start | bytes 786432 | tf_op jit(solution)/shard_map/all_to_all | solution.py:515
  43.7 2.6 %collective-permute-start.10 = (bf16[768,128]{1,0:T(8,128)(2,1)}, bf16[768,128]{1,0:T(8,128)(2,1)S(1)}, u32[]{:S(2)}, u32[]{:S(2)}) collective-permute-start(bf16[768,128]{1,0:T(8,128)(2,1)} %near_field_sent.1.refs_1_), channel_id=1, source_target_pairs={{0,3},{1,0},{2,1},{3,2},{4,7},{5,4},{6,5},{7,6},{8,11},{9,8},{10,9... | collective-permute-start | bytes 589832 | tf_op jit(solution)/shard_map/ppermute | solution.py:482
  47.4 2.9 %join_couplings.1.refs_3_ = bf16[5,256,1024]{2,1,0:T(8,128)(2,1)S(1)} custom-call(s32[1]{0:T(128)} %bitcast.refs_0_, bf16[16384,64]{1,0:T(8,128)(2,1)} %bitcast.25, bf16[4096,64]{1,0:T(8,128)(2,1)} %bitcast.26), custom_call_target="tpu_custom_call" | custom-call | tf_op jit(solution)/shard_map/join_couplings/pallas_call | solution.py:122
  50.2 2.4 %all-to-all-done.2 = bf16[8,12,16,128]{3,2,1,0:T(8,128)(2,1)S(1)} async-done(((bf16[8,12,16,128]{3,2,1,0:T(8,128)(2,1)}), bf16[8,12,16,128]{3,2,1,0:T(8,128)(2,1)S(1)}, u32[]{:S(2)}, u32[]{:S(2)}) %all-to-all-start.2) | async-done | bytes 393248 | tf_op jit(solution)/shard_map/all_to_all | solution.py:515
  52.7 2.1 %far_field.2.refs_1_ = bf16[4,16,128]{2,1,0:T(8,128)(2,1)S(1)} custom-call(s32[16,16]{1,0:T(8,128)} %get-tuple-element.46.refs_0_, s32[4,16]{1,0:T(4,128)} %get-tuple-element.47.refs_1_, bf16[96,16,128]{2,1,0:T(8,128)(2,1)S(1)} %bitcast.19, bf16[5,256,1024]{2,1,0:T(8,128)(2,1)S(1)} %join_couplings.1.refs_3_, bf16[4,256,64]{2,1,0:T(8,128)(2,1)S(1)} %bitcast.14), custom_call_target="tpu_custom_call" | custom-call | tf_op jit(solution)/shard_map/far_field/pallas_call | solution.py:122
  54.7 2.7 %collective-permute-start.7 = (bf16[4,16,128]{2,1,0:T(8,128)(2,1)S(1)}, bf16[4,16,128]{2,1,0:T(8,128)(2,1)S(1)}, u32[]{:S(2)}, u32[]{:S(2)}) collective-permute-start(bf16[4,16,128]{2,1,0:T(8,128)(2,1)S(1)} %far_field.2.refs_1_), channel_id=1, source_target_pairs={{0,3},{1,0},{2,1},{3,2},{4,7},{5,4},{6,5},{7,6},{8,11},{9,8},{10,9... | collective-permute-start | bytes 49160 | tf_op jit(solution)/shard_map/ppermute | solution.py:482
  60.7 2.0 %collective-permute-done.6.refs_3_ = bf16[4,16,128]{2,1,0:T(8,128)(2,1)S(1)} collective-permute-done((bf16[4,16,128]{2,1,0:T(8,128)(2,1)S(1)}, bf16[4,16,128]{2,1,0:T(8,128)(2,1)S(1)}, u32[]{:S(2)}, u32[]{:S(2)}) %collective-permute-start.6) | collective-permute-done | bytes 16416 | tf_op jit(solution)/shard_map/ppermute | solution.py:482
  62.9 2.4 %second_coefficients.1 = (bf16[16,32,256]{2,1,0:T(8,128)(2,1)}, bf16[4,32,256]{2,1,0:T(8,128)(2,1)S(1)}, bf16[4,32,256]{2,1,0:T(8,128)(2,1)S(1)}, bf16[8,5,16,128]{3,2,1,0:T(8,128)(2,1)}) custom-call(s32[1]{0:T(128)} %bitcast.refs_0_, bf16[4,16,128]{2,1,0:T(8,128)(2,1)S(1)} %far_field.2.refs_1_, bf16[4,16,128]{2,1,0:T(8,128)(2,1)S(1)} %collective-permute-done.5.refs_2_, ...), custom_call_target="tpu_custom_call" | custom-call | tf_op jit(solution)/shard_map/second_coefficients/pallas_call | solution.py:122
  65.3 7.0 %all-to-all-start.3 = ((bf16[8,5,16,128]{3,2,1,0:T(8,128)(2,1)}), bf16[8,5,16,128]{3,2,1,0:T(8,128)(2,1)S(1)}, u32[]{:S(2)}, u32[]{:S(2)}) async-start(bf16[8,5,16,128]{3,2,1,0:T(8,128)(2,1)} %get-tuple-element.70), calls=%async_computation.3 | async-start | bytes 327680 | tf_op jit(solution)/shard_map/all_to_all | solution.py:505
  72.3 1.9 %collective-permute-start.11 = (bf16[4,32,256]{2,1,0:T(8,128)(2,1)S(1)}, bf16[4,32,256]{2,1,0:T(8,128)(2,1)S(1)}, u32[]{:S(2)}, u32[]{:S(2)}) collective-permute-start(bf16[4,32,256]{2,1,0:T(8,128)(2,1)S(1)} %get-tuple-element.71), channel_id=1, source_target_pairs={{0,4},{4,8},{8,12},{12,16},{16,20},{20,24},{24,28},{28,32},{32,36}... | collective-permute-start | bytes 196616 | tf_op jit(solution)/shard_map/ppermute | solution.py:495
  74.2 5.8 %collective-permute-start.12 = (bf16[4,32,256]{2,1,0:T(8,128)(2,1)S(1)}, bf16[4,32,256]{2,1,0:T(8,128)(2,1)}, u32[]{:S(2)}, u32[]{:S(2)}) collective-permute-start(bf16[4,32,256]{2,1,0:T(8,128)(2,1)S(1)} %get-tuple-element.72), channel_id=1, source_target_pairs={{4,0},{8,4},{12,8},{16,12},{20,16},{24,20},{28,24},{32,28},{36,32}... | collective-permute-start | bytes 196616 | tf_op jit(solution)/shard_map/ppermute | solution.py:496
  83.4 7.7 %all-to-all-start.4 = ((bf16[8,12,16,128]{3,2,1,0:T(8,128)(2,1)}), bf16[8,12,16,128]{3,2,1,0:T(8,128)(2,1)S(1)}, u32[]{:S(2)}, u32[]{:S(2)}) async-start(bf16[8,12,16,128]{3,2,1,0:T(8,128)(2,1)} %choose_rows.3), calls=%async_computation.4 | async-start | bytes 786432 | tf_op jit(solution)/shard_map/all_to_all | solution.py:515
  91.1 5.5 %near_field.1 = (f32[16,32,64]{2,1,0:T(8,128)}, bf16[32,16,64]{2,1,0:T(8,128)(2,1)}) custom-call(s32[1]{0:T(128)} %bitcast.refs_0_, s32[1]{0:T(128)} %bitcast.1.refs_0_.refs_1_, s32[16,9]{1,0:T(8,128)} %refs_2_.3, bf16[16,32,256]{2,1,0:T(8,128)(2,1)} %get-tuple-element.69.refs_3_, bf16[4,32,256]{2,1,0:T(8,128)(2,1)} %copy-done.2, ...), custom_call_target="tpu_custom_call" | custom-call | tf_op jit(solution)/shard_map/near_field/pallas_call | solution.py:122
  96.6 3.4 %all-to-all-done.4 = bf16[8,12,16,128]{3,2,1,0:T(8,128)(2,1)S(1)} async-done(((bf16[8,12,16,128]{3,2,1,0:T(8,128)(2,1)}), bf16[8,12,16,128]{3,2,1,0:T(8,128)(2,1)S(1)}, u32[]{:S(2)}, u32[]{:S(2)}) %all-to-all-start.4) | async-done | bytes 393248 | tf_op jit(solution)/shard_map/all_to_all | solution.py:515
  100.1 2.1 %far_field.3.refs_1_ = bf16[4,16,128]{2,1,0:T(8,128)(2,1)S(1)} custom-call(s32[16,16]{1,0:T(8,128)} %get-tuple-element.46.refs_0_, s32[4,16]{1,0:T(4,128)} %get-tuple-element.47.refs_1_, bf16[96,16,128]{2,1,0:T(8,128)(2,1)S(1)} %bitcast.20, bf16[5,256,1024]{2,1,0:T(8,128)(2,1)S(1)} %join_couplings.1.refs_3_, bf16[4,256,64]{2,1,0:T(8,128)(2,1)S(1)} %bitcast.16), custom_call_target="tpu_custom_call" | custom-call | tf_op jit(solution)/shard_map/far_field/pallas_call | solution.py:122
  106.0 2.1 %collective-permute-done.14.refs_3_ = bf16[4,16,128]{2,1,0:T(8,128)(2,1)S(1)} collective-permute-done((bf16[4,16,128]{2,1,0:T(8,128)(2,1)S(1)}, bf16[4,16,128]{2,1,0:T(8,128)(2,1)S(1)}, u32[]{:S(2)}, u32[]{:S(2)}) %collective-permute-start.14) | collective-permute-done | bytes 16416 | tf_op jit(solution)/shard_map/ppermute | solution.py:482
  109.1 1.9 %output.1 = bf16[32,16,64]{2,1,0:T(8,128)(2,1)} custom-call(s32[1]{0:T(128)} %bitcast.refs_0_, bf16[4,16,128]{2,1,0:T(8,128)(2,1)S(1)} %far_field.3.refs_1_, bf16[4,16,128]{2,1,0:T(8,128)(2,1)S(1)} %collective-permute-done.13.refs_2_, bf16[4,16,128]{2,1,0:T(8,128)(2,1)S(1)} %collective-permute-done.14.refs_3_, ...), custom_call_target="tpu_custom_call" | custom-call | tf_op jit(solution)/shard_map/output/pallas_call | solution.py:122
  (37 shorter events, 20.3 us)
Async XLA Ops:
  2.5 8.5 %collective-permute-start = (bf16[336,128]{1,0:T(8,128)(2,1)S(1)}, bf16[336,128]{1,0:T(8,128)(2,1)S(1)}, u32[]{:S(2)}, u32[]{:S(2)}) collective-permute-start(bf16[336,128]{1,0:T(8,128)(2,1)S(1)} %get-tuple-element.49), channel_id=1, source_target_pairs={{0,1},{1,2},{2,3},{3,0},{4,5},{5,6},{6,7},{7,4},{8,9},{9,10},{10,1... | collective-permute-start | bytes 258056 | tf_op jit(solution)/shard_map/ppermute | solution.py:482
  4.0 6.9 %collective-permute-start.1 = (bf16[336,128]{1,0:T(8,128)(2,1)S(1)}, bf16[336,128]{1,0:T(8,128)(2,1)S(1)}, u32[]{:S(2)}, u32[]{:S(2)}) collective-permute-start(bf16[336,128]{1,0:T(8,128)(2,1)S(1)} %get-tuple-element.50), channel_id=1, source_target_pairs={{0,2},{1,3},{2,0},{3,1},{4,6},{5,7},{6,4},{7,5},{8,10},{9,11},{10,... | collective-permute-start | bytes 258056 | tf_op jit(solution)/shard_map/ppermute | solution.py:482
  6.8 4.5 %collective-permute-start.2 = (bf16[336,128]{1,0:T(8,128)(2,1)S(1)}, bf16[336,128]{1,0:T(8,128)(2,1)S(1)}, u32[]{:S(2)}, u32[]{:S(2)}) collective-permute-start(bf16[336,128]{1,0:T(8,128)(2,1)S(1)} %get-tuple-element.51), channel_id=1, source_target_pairs={{0,3},{1,0},{2,1},{3,2},{4,7},{5,4},{6,5},{7,6},{8,11},{9,8},{10,9... | collective-permute-start | bytes 258056 | tf_op jit(solution)/shard_map/ppermute | solution.py:482
  12.2 15.4 %all-to-all-start = ((bf16[8,5,16,128]{3,2,1,0:T(8,128)(2,1)}), bf16[8,5,16,128]{3,2,1,0:T(8,128)(2,1)S(1)}, u32[]{:S(2)}, u32[]{:S(2)}) async-start(bf16[8,5,16,128]{3,2,1,0:T(8,128)(2,1)} %get-tuple-element.57), calls=%async_computation | async-start | bytes 327680 | tf_op jit(solution)/shard_map/all_to_all | solution.py:505
  19.8 11.0 %collective-permute-start.3 = (bf16[4,32,256]{2,1,0:T(8,128)(2,1)S(1)}, bf16[4,32,256]{2,1,0:T(8,128)(2,1)S(1)}, u32[]{:S(2)}, u32[]{:S(2)}) collective-permute-start(bf16[4,32,256]{2,1,0:T(8,128)(2,1)S(1)} %get-tuple-element.62), channel_id=1, source_target_pairs={{0,4},{4,8},{8,12},{12,16},{16,20},{20,24},{24,28},{28,32},{32,36}... | collective-permute-start | bytes 196616 | tf_op jit(solution)/shard_map/ppermute | solution.py:495
  21.7 9.1 %collective-permute-start.4 = (bf16[4,32,256]{2,1,0:T(8,128)(2,1)S(1)}, bf16[4,32,256]{2,1,0:T(8,128)(2,1)S(1)}, u32[]{:S(2)}, u32[]{:S(2)}) collective-permute-start(bf16[4,32,256]{2,1,0:T(8,128)(2,1)S(1)} %get-tuple-element.63), channel_id=1, source_target_pairs={{4,0},{8,4},{12,8},{16,12},{20,16},{24,20},{28,24},{32,28},{36,32}... | collective-permute-start | bytes 196616 | tf_op jit(solution)/shard_map/ppermute | solution.py:496
  27.5 8.4 %all-to-all-start.1 = ((s32[8,1,128]{2,1,0:T(1,128)}), s32[8,1,128]{2,1,0:T(1,128)S(1)}, u32[]{:S(2)}, u32[]{:S(2)}) async-start(s32[8,1,128]{2,1,0:T(1,128)} %bitcast.5), calls=%async_computation.1 | async-start | bytes 8192 | tf_op jit(solution)/shard_map/all_to_all | solution.py:545
  37.5 15.2 %copy-start = (bf16[16,64,64]{2,1,0:T(8,128)(2,1)S(1)}, bf16[16,64,64]{2,1,0:T(8,128)(2,1)}, u32[]{:S(2)}) copy-start(bf16[16,64,64]{2,1,0:T(8,128)(2,1)} %param.12) | copy-start | bytes 393220
  37.5 15.2 %all-to-all-start.2 = ((bf16[8,12,16,128]{3,2,1,0:T(8,128)(2,1)}), bf16[8,12,16,128]{3,2,1,0:T(8,128)(2,1)S(1)}, u32[]{:S(2)}, u32[]{:S(2)}) async-start(bf16[8,12,16,128]{3,2,1,0:T(8,128)(2,1)} %choose_rows.2), calls=%async_computation.2 | async-start | bytes 786432 | tf_op jit(solution)/shard_map/all_to_all | solution.py:515
  43.7 14.1 %collective-permute-start.10 = (bf16[768,128]{1,0:T(8,128)(2,1)}, bf16[768,128]{1,0:T(8,128)(2,1)S(1)}, u32[]{:S(2)}, u32[]{:S(2)}) collective-permute-start(bf16[768,128]{1,0:T(8,128)(2,1)} %near_field_sent.1.refs_1_), channel_id=1, source_target_pairs={{0,3},{1,0},{2,1},{3,2},{4,7},{5,4},{6,5},{7,6},{8,11},{9,8},{10,9... | collective-permute-start | bytes 589832 | tf_op jit(solution)/shard_map/ppermute | solution.py:482
  46.4 12.1 %collective-permute-start.9 = (bf16[768,128]{1,0:T(8,128)(2,1)}, bf16[768,128]{1,0:T(8,128)(2,1)}, u32[]{:S(2)}, u32[]{:S(2)}) collective-permute-start(bf16[768,128]{1,0:T(8,128)(2,1)} %near_field_sent.1.refs_1_), channel_id=1, source_target_pairs={{0,2},{1,3},{2,0},{3,1},{4,6},{5,7},{6,4},{7,5},{8,10},{9,11},{10,... | collective-permute-start | bytes 589832 | tf_op jit(solution)/shard_map/ppermute | solution.py:482
  46.7 12.5 %collective-permute-start.8 = (bf16[768,128]{1,0:T(8,128)(2,1)}, bf16[768,128]{1,0:T(8,128)(2,1)}, u32[]{:S(2)}, u32[]{:S(2)}) collective-permute-start(bf16[768,128]{1,0:T(8,128)(2,1)} %near_field_sent.1.refs_1_), channel_id=1, source_target_pairs={{0,1},{1,2},{2,3},{3,0},{4,5},{5,6},{6,7},{7,4},{8,9},{9,10},{10,1... | collective-permute-start | bytes 589832 | tf_op jit(solution)/shard_map/ppermute | solution.py:482
  54.7 6.0 %collective-permute-start.7 = (bf16[4,16,128]{2,1,0:T(8,128)(2,1)S(1)}, bf16[4,16,128]{2,1,0:T(8,128)(2,1)S(1)}, u32[]{:S(2)}, u32[]{:S(2)}) collective-permute-start(bf16[4,16,128]{2,1,0:T(8,128)(2,1)S(1)} %far_field.2.refs_1_), channel_id=1, source_target_pairs={{0,3},{1,0},{2,1},{3,2},{4,7},{5,4},{6,5},{7,6},{8,11},{9,8},{10,9... | collective-permute-start | bytes 49160 | tf_op jit(solution)/shard_map/ppermute | solution.py:482
  57.5 5.2 %collective-permute-start.6 = (bf16[4,16,128]{2,1,0:T(8,128)(2,1)S(1)}, bf16[4,16,128]{2,1,0:T(8,128)(2,1)S(1)}, u32[]{:S(2)}, u32[]{:S(2)}) collective-permute-start(bf16[4,16,128]{2,1,0:T(8,128)(2,1)S(1)} %far_field.2.refs_1_), channel_id=1, source_target_pairs={{0,2},{1,3},{2,0},{3,1},{4,6},{5,7},{6,4},{7,5},{8,10},{9,11},{10,... | collective-permute-start | bytes 49160 | tf_op jit(solution)/shard_map/ppermute | solution.py:482
  57.8 5.1 %collective-permute-start.5 = (bf16[4,16,128]{2,1,0:T(8,128)(2,1)S(1)}, bf16[4,16,128]{2,1,0:T(8,128)(2,1)S(1)}, u32[]{:S(2)}, u32[]{:S(2)}) collective-permute-start(bf16[4,16,128]{2,1,0:T(8,128)(2,1)S(1)} %far_field.2.refs_1_), channel_id=1, source_target_pairs={{0,1},{1,2},{2,3},{3,0},{4,5},{5,6},{6,7},{7,4},{8,9},{9,10},{10,1... | collective-permute-start | bytes 49160 | tf_op jit(solution)/shard_map/ppermute | solution.py:482
  65.3 16.6 %all-to-all-start.3 = ((bf16[8,5,16,128]{3,2,1,0:T(8,128)(2,1)}), bf16[8,5,16,128]{3,2,1,0:T(8,128)(2,1)S(1)}, u32[]{:S(2)}, u32[]{:S(2)}) async-start(bf16[8,5,16,128]{3,2,1,0:T(8,128)(2,1)} %get-tuple-element.70), calls=%async_computation.3 | async-start | bytes 327680 | tf_op jit(solution)/shard_map/all_to_all | solution.py:505
  72.3 7.7 %collective-permute-start.11 = (bf16[4,32,256]{2,1,0:T(8,128)(2,1)S(1)}, bf16[4,32,256]{2,1,0:T(8,128)(2,1)S(1)}, u32[]{:S(2)}, u32[]{:S(2)}) collective-permute-start(bf16[4,32,256]{2,1,0:T(8,128)(2,1)S(1)} %get-tuple-element.71), channel_id=1, source_target_pairs={{0,4},{4,8},{8,12},{12,16},{16,20},{20,24},{24,28},{28,32},{32,36}... | collective-permute-start | bytes 196616 | tf_op jit(solution)/shard_map/ppermute | solution.py:495
  74.2 7.6 %collective-permute-start.12 = (bf16[4,32,256]{2,1,0:T(8,128)(2,1)S(1)}, bf16[4,32,256]{2,1,0:T(8,128)(2,1)}, u32[]{:S(2)}, u32[]{:S(2)}) collective-permute-start(bf16[4,32,256]{2,1,0:T(8,128)(2,1)S(1)} %get-tuple-element.72), channel_id=1, source_target_pairs={{4,0},{8,4},{12,8},{16,12},{20,16},{24,20},{28,24},{32,28},{36,32}... | collective-permute-start | bytes 196616 | tf_op jit(solution)/shard_map/ppermute | solution.py:496
  80.0 0.6 copy-start.2
  83.4 16.7 %all-to-all-start.4 = ((bf16[8,12,16,128]{3,2,1,0:T(8,128)(2,1)}), bf16[8,12,16,128]{3,2,1,0:T(8,128)(2,1)S(1)}, u32[]{:S(2)}, u32[]{:S(2)}) async-start(bf16[8,12,16,128]{3,2,1,0:T(8,128)(2,1)} %choose_rows.3), calls=%async_computation.4 | async-start | bytes 786432 | tf_op jit(solution)/shard_map/all_to_all | solution.py:515
  91.1 18.0 %copy-start.1 = (bf16[16,64,64]{2,1,0:T(8,128)(2,1)S(1)}, bf16[16,64,64]{2,1,0:T(8,128)(2,1)}, u32[]{:S(2)}) copy-start(bf16[16,64,64]{2,1,0:T(8,128)(2,1)} %refs_6_.1) | copy-start | bytes 393220
  102.1 3.8 %collective-permute-start.15 = (bf16[4,16,128]{2,1,0:T(8,128)(2,1)S(1)}, bf16[4,16,128]{2,1,0:T(8,128)(2,1)S(1)}, u32[]{:S(2)}, u32[]{:S(2)}) collective-permute-start(bf16[4,16,128]{2,1,0:T(8,128)(2,1)S(1)} %far_field.3.refs_1_), channel_id=1, source_target_pairs={{0,3},{1,0},{2,1},{3,2},{4,7},{5,4},{6,5},{7,6},{8,11},{9,8},{10,9... | collective-permute-start | bytes 49160 | tf_op jit(solution)/shard_map/ppermute | solution.py:482
  102.8 5.3 %collective-permute-start.14 = (bf16[4,16,128]{2,1,0:T(8,128)(2,1)S(1)}, bf16[4,16,128]{2,1,0:T(8,128)(2,1)S(1)}, u32[]{:S(2)}, u32[]{:S(2)}) collective-permute-start(bf16[4,16,128]{2,1,0:T(8,128)(2,1)S(1)} %far_field.3.refs_1_), channel_id=1, source_target_pairs={{0,2},{1,3},{2,0},{3,1},{4,6},{5,7},{6,4},{7,5},{8,10},{9,11},{10,... | collective-permute-start | bytes 49160 | tf_op jit(solution)/shard_map/ppermute | solution.py:482
  104.2 4.9 %collective-permute-start.13 = (bf16[4,16,128]{2,1,0:T(8,128)(2,1)S(1)}, bf16[4,16,128]{2,1,0:T(8,128)(2,1)S(1)}, u32[]{:S(2)}, u32[]{:S(2)}) collective-permute-start(bf16[4,16,128]{2,1,0:T(8,128)(2,1)S(1)} %far_field.3.refs_1_), channel_id=1, source_target_pairs={{0,1},{1,2},{2,3},{3,0},{4,5},{5,6},{6,7},{7,4},{8,9},{9,10},{10,1... | collective-permute-start | bytes 49160 | tf_op jit(solution)/shard_map/ppermute | solution.py:482

commit v7 on v6

--- a/solution.py
+++ b/solution.py
@@ -26,7 +26,7 @@
 OUT_TILES = LEAF_OUT + PLANES
 GOT_ROWS = 4 * PLANE * OUT_TILES
 PACKED = LEAVES // 2 * PROBES
-SENT = PACKED + LEAVES // 2 * RANK
+PACKED_BASIS = LEAVES // 2 * RANK
 BF16, F32 = jnp.bfloat16, jnp.float32
 
 NT = (((1,), (1,)), ((), ()))
@@ -195,7 +195,7 @@
 
 
 def partial_kernel(
-    sub_ref, x_ref, basis_ref, transfer_ref, out0_ref, out1_ref, out2_ref, out3_ref, sums_ref
+    sub_ref, x_ref, basis_ref, transfer_ref, out0_ref, out1_ref, out2_ref, out3_ref, packed_ref, sums_ref
 ):
     out_refs = [out0_ref, out1_ref, out2_ref, out3_ref]
     x = jnp.transpose(x_ref[...].astype(F32), (1, 0, 2)).astype(BF16)
@@ -203,6 +203,10 @@
         pair = jnp.concatenate([x[2 * j], x[2 * j + 1]], axis=1)
         for out_ref in out_refs:
             out_ref[pl.ds(j * PROBES, PROBES), :] = pair
+        q, n = j // 2, j % 2 * 2 * RANK
+        pair = [basis_ref[q, n : n + RANK, :], basis_ref[q, n + RANK : n + 2 * RANK, :]]
+        packed_ref[pl.ds(j * RANK, RANK), :] = jnp.concatenate(pair, axis=1)
+    packed_ref.send()
     parents = []
     sums = []
     for q in range(PARENTS):
@@ -252,17 +256,33 @@
             high_ref[i - (LEAVES - REACH)] = x
 
 
-def join_kernel(sub_ref, got0_ref, got1_ref, got2_ref, got3_ref, near_ref, basis_ref, slots_ref):
-    in_order(sub_ref, [got0_ref, got1_ref, got2_ref, got3_ref], slots_ref, SENT)
-
-    def whole(i, start, size):
+def join_kernel(
+    sub_ref,
+    near0_ref,
+    near1_ref,
+    near2_ref,
+    near3_ref,
+    basis0_ref,
+    basis1_ref,
+    basis2_ref,
+    basis3_ref,
+    near_ref,
+    basis_ref,
+    near_slots_ref,
+    basis_slots_ref,
+):
+    basis_refs = [basis0_ref, basis1_ref, basis2_ref, basis3_ref]
+    in_order(sub_ref, basis_refs, basis_slots_ref, PACKED_BASIS)
+    in_order(sub_ref, [near0_ref, near1_ref, near2_ref, near3_ref], near_slots_ref, PACKED)
+
+    def whole(slots_ref, i, size):
         half = slice((i % 2) * ROWS, (i % 2 + 1) * ROWS)
-        rows = pl.ds(start + (i // 2) * size, size)
+        rows = pl.ds((i // 2) * size, size)
         return jnp.concatenate([slots_ref[s, rows, half] for s in range(SUBS)], axis=1)
 
     for i in range(LEAVES):
-        near_ref[i // 4, pl.ds(i % 4 * PROBES, PROBES), :] = whole(i, 0, PROBES)
-        basis_ref[i // 4, pl.ds(i % 4 * RANK, RANK), :] = whole(i, PACKED, RANK)
+        near_ref[i // 4, pl.ds(i % 4 * PROBES, PROBES), :] = whole(near_slots_ref, i, PROBES)
+        basis_ref[i // 4, pl.ds(i % 4 * RANK, RANK), :] = whole(basis_slots_ref, i, RANK)
 
 
 def weights_kernel(_, couplings_ref, coarse_ref, out_ref):
@@ -428,16 +448,13 @@
 
 
 def near_sent_kernel(
-    first_ref, list_ref, x_ref, low_ref, high_ref, blocks_ref, basis_ref, out_ref, wide_ref
+    first_ref, list_ref, x_ref, low_ref, high_ref, blocks_ref, out_ref, wide_ref
 ):
     parts = near_parts(first_ref, list_ref, x_ref, low_ref, high_ref, blocks_ref, wide_ref)
     for q, four in enumerate(parts):
         for j in range(2):
             pair = jnp.concatenate(four[2 * j : 2 * j + 2], axis=1).astype(BF16)
             out_ref[pl.ds((2 * q + j) * PROBES, PROBES), :] = pair
-    for j in range(LEAVES // 2):
-        pair = jnp.concatenate([basis_ref[2 * j], basis_ref[2 * j + 1]], axis=1)
-        out_ref[pl.ds(PACKED + j * RANK, RANK), :] = pair
 
 
 def near_kernel(
@@ -504,7 +521,7 @@
     def along(tiles):
         return lax.all_to_all(tiles, "leaf", 0, 0, axis_index_groups=along_z, tiled=True)
 
-    def within(column, asked):
+    def within(column, asked, edges=()):
         (chosen,) = call(
             choose_kernel,
             "choose_rows",
@@ -512,13 +529,14 @@
             of_kind("smem", asked) + of_kind("vmem", column),
             [pltpu.VMEM((PLANES * LEAVES, OWN, LANES), F32)],
         )
+        chosen, edges = lax.optimization_barrier((chosen, edges))
         got = lax.all_to_all(chosen, "leaf", 0, 0, axis_index_groups=in_plane, tiled=True)
-        return got.reshape((PLANE * OUT_TILES,) + tile)
-
-    packed = call(
+        return got.reshape((PLANE * OUT_TILES,) + tile), edges
+
+    *packed, packed_basis = call(
         partial_kernel,
         "partial_sums",
-        [((PACKED + TILES * 16, LANES), BF16)] * SUBS,
+        [((PACKED + TILES * 16, LANES), BF16)] * SUBS + [((PACKED_BASIS, LANES), BF16, 1)],
         of_kind("smem", sub) + of_kind("hbm", probes, four_bases, four_transfers),
         [pltpu.VMEM((TILES, PROBES, 4 * RANK), F32)],
     )
@@ -541,17 +559,18 @@
         of_kind("smem", sub) + of_kind("vmem", *pieces),
         [pltpu.VMEM((SUBS, PACKED, LANES), BF16)],
     )
-    column, wanted = lax.optimization_barrier((along(tiles), wanted))
+    bases = over_sub([packed_basis] * SUBS)
+    column, wanted, bases = lax.optimization_barrier((along(tiles), wanted, bases))
     asked = lax.all_to_all(wanted, "leaf", 0, 0, axis_index_groups=in_plane, tiled=True)
     (sent,) = call(
         near_sent_kernel,
         "near_field_sent",
-        [((SENT, LANES), BF16, 1)],
-        near_args(x0, *halos(low, high), "vmem") + of_kind("hbm", leaf_cluster_basis),
+        [((PACKED, LANES), BF16, 1)],
+        near_args(x0, *halos(low, high), "vmem"),
         wide_scratch,
     )
     column, sent, later = lax.optimization_barrier((column, sent, sub))
-    got = within(column, asked)
+    got, _ = within(column, asked)
     (weights,) = call(
         weights_kernel,
         "join_couplings",
@@ -576,8 +595,11 @@
         join_kernel,
         "join_near_basis",
         [((PARENTS, 4 * PROBES, UNKNOWNS), BF16), ((PARENTS, 4 * RANK, UNKNOWNS), BF16)],
-        of_kind("smem", sub) + of_kind("hbm", pieces[0]) + of_kind("any", *pieces[1:]),
-        [pltpu.VMEM((SUBS, SENT, LANES), BF16)],
+        of_kind("smem", sub)
+        + of_kind("hbm", pieces[0])
+        + of_kind("any", *pieces[1:])
+        + of_kind("hbm", *bases),
+        [pltpu.VMEM((SUBS, PACKED, LANES), BF16), pltpu.VMEM((SUBS, PACKED_BASIS, LANES), BF16)],
     )
     x1, low, high, tiles = call(
         second_kernel,
@@ -588,8 +610,7 @@
         + of_kind("vmem", near1, basis, four_transfers),
         [field_scratch, pltpu.VMEM((4, PROBES, UNKNOWNS), F32)],
     )
-    column, edges = lax.optimization_barrier((along(tiles), halos(low, high)))
-    got = within(column, asked)
+    got, edges = within(along(tiles), asked, halos(low, high))
     near2, first = call(
         near_kernel,
         "near_field",

time: 112 us -> 117 us (1.045)
  starting transfers between devices: 63.7 us -> 67.6 us
  local copies, waits for them, and re-layouts: 0.63 us -> 1.93 us
    ppermute x12 -> x15, starting transfers between devices: 16.4 us -> 20.7 us  [over_sub(): lax.ppermute(pieces[k], 'sub', [(i, (i + k) % SUBS) for i in range(SUBS)])]
    all_to_all x2, starting transfers between devices: 13.9 us -> 12.3 us  [within(): lax.all_to_all(chosen, 'leaf', 0, 0, axis_index_groups=in_plane, tiled=True)]
    all_to_all x2, starting transfers between devices: 14.7 us -> 16 us  [along(): lax.all_to_all(tiles, 'leaf', 0, 0, axis_index_groups=along_z, tiled=True)]
    unnamed x6 -> x12, local copies, waits for them, and re-layouts: 0.63 us -> 1.93 us
    ppermute x12 -> x15, waiting for transfers between devices: 6.87 us -> 7.83 us  [over_sub(): lax.ppermute(pieces[k], 'sub', [(i, (i + k) % SUBS) for i in range(SUBS)])]
  transfers between devices with their start and end apart: 21 -> 24, of which waited for: 10 -> 10; matrix products, arithmetic and copies ran while one was open for 0% -> 0% of each run, Pallas kernels for 18% -> 18%
where the time goes in v7:
time: 117 us; the launch traced here: 116 us
  starting transfers between devices  67.6 us (58%)
  Pallas kernels  31.9 us (27%)
  waiting for transfers between devices  13.4 us (11%)
  local copies, waits for them, and re-layouts  1.93 us (2%)
    pallas_call x13, Pallas kernels, call(): pl.pallas_call(body, name=name, out_shape=[pltpu.HBM(out[0], out[1]) if l...  31.9 us
    ppermute x15, starting transfers between devices, over_sub(): lax.ppermute(pieces[k], 'sub', [(i, (i + k) % SUBS) for i in range(SUBS)])  20.7 us
    all_to_all x2, starting transfers between devices, along(): lax.all_to_all(tiles, 'leaf', 0, 0, axis_index_groups=along_z, tiled=True)  16 us
    all_to_all x2, starting transfers between devices, within(): lax.all_to_all(chosen, 'leaf', 0, 0, axis_index_groups=in_plane, tiled=True)  12.3 us
    ppermute x2, starting transfers between devices, halos(): lax.ppermute(low, 'leaf', [(i + 1, i) for i in range(groups - 1)])  11.5 us
    ppermute x15, waiting for transfers between devices, over_sub(): lax.ppermute(pieces[k], 'sub', [(i, (i + k) % SUBS) for i in range(SUBS)])  7.83 us
    all_to_all x2, waiting for transfers between devices, within(): lax.all_to_all(chosen, 'leaf', 0, 0, axis_index_groups=in_plane, tiled=True)  4.95 us
    ppermute x2, starting transfers between devices, halos(): lax.ppermute(high, 'leaf', [(i, i + 1) for i in range(groups - 1)])  3.82 us
  transfers between devices with their start and end apart: 24, of which 10 were waited for; matrix products, arithmetic and copies ran while one was open for 0% of the time, Pallas kernels for 18%

profile of v7, /device:TPU:96, one launch (start us, length us, event | category | flops | bytes accessed | tf_op | source)
XLA Modules:
  0.0 115.9 jit_solution(12892742225041509987)
XLA Ops:
  4.0 2.7 %collective-permute-start.1 = (bf16[336,128]{1,0:T(8,128)(2,1)S(1)}, bf16[336,128]{1,0:T(8,128)(2,1)S(1)}, u32[]{:S(2)}, u32[]{:S(2)}) collective-permute-start(bf16[336,128]{1,0:T(8,128)(2,1)S(1)} %get-tuple-element.55), channel_id=1, source_target_pairs={{0,2},{1,3},{2,0},{3,1},{4,6},{5,7},{6,4},{7,5},{8,10},{9,11},{10,... | collective-permute-start | bytes 258056 | tf_op jit(solution)/shard_map/ppermute | solution.py:499
  8.2 2.8 %index_tables.1 = (s32[8,128]{1,0:T(8,128)}, s32[16,16]{1,0:T(8,128)}, s32[4,16]{1,0:T(4,128)}) custom-call(s32[1]{0:T(128)} %bitcast.1.refs_0_.refs_1_, s32[16,16]{1,0:T(8,128)} %refs_1_.4, s32[4,16]{1,0:T(4,128)} %refs_2_.2), custom_call_target="tpu_custom_call" | custom-call | tf_op jit(solution)/shard_map/index_tables/pallas_call | solution.py:122
  12.2 7.7 %all-to-all-start = ((bf16[8,5,16,128]{3,2,1,0:T(8,128)(2,1)}), bf16[8,5,16,128]{3,2,1,0:T(8,128)(2,1)S(1)}, u32[]{:S(2)}, u32[]{:S(2)}) async-start(bf16[8,5,16,128]{3,2,1,0:T(8,128)(2,1)} %get-tuple-element.62), calls=%async_computation | async-start | bytes 327680 | tf_op jit(solution)/shard_map/all_to_all | solution.py:522
  19.8 2.6 %collective-permute-start.5 = (bf16[512,128]{1,0:T(8,128)(2,1)}, bf16[512,128]{1,0:T(8,128)(2,1)S(1)}, u32[]{:S(2)}, u32[]{:S(2)}) collective-permute-start(bf16[512,128]{1,0:T(8,128)(2,1)} %get-tuple-element.73.refs_5_), channel_id=1, source_target_pairs={{0,3},{1,0},{2,1},{3,2},{4,7},{5,4},{6,5},{7,6},{8,11},{9,8},{10,9... | collective-permute-start | bytes 393224 | tf_op jit(solution)/shard_map/ppermute | solution.py:499
  23.5 1.9 %collective-permute-start.6 = (bf16[4,32,256]{2,1,0:T(8,128)(2,1)S(1)}, bf16[4,32,256]{2,1,0:T(8,128)(2,1)S(1)}, u32[]{:S(2)}, u32[]{:S(2)}) collective-permute-start(bf16[4,32,256]{2,1,0:T(8,128)(2,1)S(1)} %get-tuple-element.68), channel_id=1, source_target_pairs={{0,4},{4,8},{8,12},{12,16},{16,20},{20,24},{24,28},{28,32},{32,36}... | collective-permute-start | bytes 196616 | tf_op jit(solution)/shard_map/ppermute | solution.py:512
  25.4 5.8 %collective-permute-start.7 = (bf16[4,32,256]{2,1,0:T(8,128)(2,1)S(1)}, bf16[4,32,256]{2,1,0:T(8,128)(2,1)S(1)}, u32[]{:S(2)}, u32[]{:S(2)}) collective-permute-start(bf16[4,32,256]{2,1,0:T(8,128)(2,1)S(1)} %get-tuple-element.69), channel_id=1, source_target_pairs={{4,0},{8,4},{12,8},{16,12},{20,16},{24,20},{28,24},{32,28},{36,32}... | collective-permute-start | bytes 196616 | tf_op jit(solution)/shard_map/ppermute | solution.py:513
  32.5 3.3 %all-to-all-start.1 = ((s32[8,1,128]{2,1,0:T(1,128)}), s32[8,1,128]{2,1,0:T(1,128)S(1)}, u32[]{:S(2)}, u32[]{:S(2)}) async-start(s32[8,1,128]{2,1,0:T(1,128)} %bitcast.5), calls=%async_computation.1 | async-start | bytes 8192 | tf_op jit(solution)/shard_map/all_to_all | solution.py:564
  35.8 4.9 %near_field_sent.1.refs_1_ = bf16[256,128]{1,0:T(8,128)(2,1)} custom-call(s32[1]{0:T(128)} %bitcast.1.refs_0_.refs_1_, s32[16,9]{1,0:T(8,128)} %refs_2_.3, bf16[16,32,256]{2,1,0:T(8,128)(2,1)} %get-tuple-element.67.refs_2_, bf16[4,32,256]{2,1,0:T(8,128)(2,1)S(1)} %collective-permute-done.6.refs_3_, bf16[4,32,256]{2,1,0:T(8,128)(2,1)S(1)} %collective-permute-done.7.refs_4_, ...), custom_call_target="tpu_custom_call" | custom-call | tf_op jit(solution)/shard_map/near_field_sent/pallas_call | solution.py:122
  42.5 4.7 %all-to-all-start.2 = ((bf16[8,12,16,128]{3,2,1,0:T(8,128)(2,1)}), bf16[8,12,16,128]{3,2,1,0:T(8,128)(2,1)S(1)}, u32[]{:S(2)}, u32[]{:S(2)}) async-start(bf16[8,12,16,128]{3,2,1,0:T(8,128)(2,1)} %choose_rows.2), calls=%async_computation.2 | async-start | bytes 786432 | tf_op jit(solution)/shard_map/all_to_all | solution.py:533
  47.2 2.6 %collective-permute-start.13 = (bf16[256,128]{1,0:T(8,128)(2,1)}, bf16[256,128]{1,0:T(8,128)(2,1)S(1)}, u32[]{:S(2)}, u32[]{:S(2)}) collective-permute-start(bf16[256,128]{1,0:T(8,128)(2,1)} %near_field_sent.1.refs_1_), channel_id=1, source_target_pairs={{0,3},{1,0},{2,1},{3,2},{4,7},{5,4},{6,5},{7,6},{8,11},{9,8},{10,9... | collective-permute-start | bytes 196616 | tf_op jit(solution)/shard_map/ppermute | solution.py:499
  49.8 2.0 %collective-permute-start.12 = (bf16[256,128]{1,0:T(8,128)(2,1)}, bf16[256,128]{1,0:T(8,128)(2,1)S(1)}, u32[]{:S(2)}, u32[]{:S(2)}) collective-permute-start(bf16[256,128]{1,0:T(8,128)(2,1)} %near_field_sent.1.refs_1_), channel_id=1, source_target_pairs={{0,2},{1,3},{2,0},{3,1},{4,6},{5,7},{6,4},{7,5},{8,10},{9,11},{10,... | collective-permute-start | bytes 196616 | tf_op jit(solution)/shard_map/ppermute | solution.py:499
  51.8 2.9 %join_couplings.1.refs_3_ = bf16[5,256,1024]{2,1,0:T(8,128)(2,1)S(1)} custom-call(s32[1]{0:T(128)} %bitcast.refs_0_, bf16[16384,64]{1,0:T(8,128)(2,1)} %bitcast.25, bf16[4096,64]{1,0:T(8,128)(2,1)} %bitcast.26), custom_call_target="tpu_custom_call" | custom-call | tf_op jit(solution)/shard_map/join_couplings/pallas_call | solution.py:122
  56.2 2.1 %far_field.2.refs_1_ = bf16[4,16,128]{2,1,0:T(8,128)(2,1)S(1)} custom-call(s32[16,16]{1,0:T(8,128)} %get-tuple-element.51.refs_0_, s32[4,16]{1,0:T(4,128)} %get-tuple-element.52.refs_1_, bf16[96,16,128]{2,1,0:T(8,128)(2,1)S(1)} %bitcast.17, bf16[5,256,1024]{2,1,0:T(8,128)(2,1)S(1)} %join_couplings.1.refs_3_, bf16[4,256,64]{2,1,0:T(8,128)(2,1)S(1)} %bitcast.14), custom_call_target="tpu_custom_call" | custom-call | tf_op jit(solution)/shard_map/far_field/pallas_call | solution.py:122
  58.2 2.7 %collective-permute-start.10 = (bf16[4,16,128]{2,1,0:T(8,128)(2,1)S(1)}, bf16[4,16,128]{2,1,0:T(8,128)(2,1)S(1)}, u32[]{:S(2)}, u32[]{:S(2)}) collective-permute-start(bf16[4,16,128]{2,1,0:T(8,128)(2,1)S(1)} %far_field.2.refs_1_), channel_id=1, source_target_pairs={{0,3},{1,0},{2,1},{3,2},{4,7},{5,4},{6,5},{7,6},{8,11},{9,8},{10,9... | collective-permute-start | bytes 49160 | tf_op jit(solution)/shard_map/ppermute | solution.py:499
  60.9 2.0 %collective-permute-start.9 = (bf16[4,16,128]{2,1,0:T(8,128)(2,1)S(1)}, bf16[4,16,128]{2,1,0:T(8,128)(2,1)S(1)}, u32[]{:S(2)}, u32[]{:S(2)}) collective-permute-start(bf16[4,16,128]{2,1,0:T(8,128)(2,1)S(1)} %far_field.2.refs_1_), channel_id=1, source_target_pairs={{0,2},{1,3},{2,0},{3,1},{4,6},{5,7},{6,4},{7,5},{8,10},{9,11},{10,... | collective-permute-start | bytes 49160 | tf_op jit(solution)/shard_map/ppermute | solution.py:499
  67.8 2.4 %second_coefficients.1 = (bf16[16,32,256]{2,1,0:T(8,128)(2,1)}, bf16[4,32,256]{2,1,0:T(8,128)(2,1)S(1)}, bf16[4,32,256]{2,1,0:T(8,128)(2,1)S(1)}, bf16[8,5,16,128]{3,2,1,0:T(8,128)(2,1)}) custom-call(s32[1]{0:T(128)} %bitcast.refs_0_, bf16[4,16,128]{2,1,0:T(8,128)(2,1)S(1)} %far_field.2.refs_1_, bf16[4,16,128]{2,1,0:T(8,128)(2,1)S(1)} %collective-permute-done.8.refs_2_, ...), custom_call_target="tpu_custom_call" | custom-call | tf_op jit(solution)/shard_map/second_coefficients/pallas_call | solution.py:122
  70.2 8.3 %all-to-all-start.3 = ((bf16[8,5,16,128]{3,2,1,0:T(8,128)(2,1)}), bf16[8,5,16,128]{3,2,1,0:T(8,128)(2,1)S(1)}, u32[]{:S(2)}, u32[]{:S(2)}) async-start(bf16[8,5,16,128]{3,2,1,0:T(8,128)(2,1)} %get-tuple-element.80), calls=%async_computation.3 | async-start | bytes 327680 | tf_op jit(solution)/shard_map/all_to_all | solution.py:522
  78.6 1.9 %collective-permute-start.14 = (bf16[4,32,256]{2,1,0:T(8,128)(2,1)S(1)}, bf16[4,32,256]{2,1,0:T(8,128)(2,1)S(1)}, u32[]{:S(2)}, u32[]{:S(2)}) collective-permute-start(bf16[4,32,256]{2,1,0:T(8,128)(2,1)S(1)} %get-tuple-element.81), channel_id=1, source_target_pairs={{0,4},{4,8},{8,12},{12,16},{16,20},{20,24},{24,28},{28,32},{32,36}... | collective-permute-start | bytes 196616 | tf_op jit(solution)/shard_map/ppermute | solution.py:512
  80.5 5.8 %collective-permute-start.15 = (bf16[4,32,256]{2,1,0:T(8,128)(2,1)S(1)}, bf16[4,32,256]{2,1,0:T(8,128)(2,1)S(1)}, u32[]{:S(2)}, u32[]{:S(2)}) collective-permute-start(bf16[4,32,256]{2,1,0:T(8,128)(2,1)S(1)} %get-tuple-element.82), channel_id=1, source_target_pairs={{4,0},{8,4},{12,8},{16,12},{20,16},{24,20},{28,24},{32,28},{36,32}... | collective-permute-start | bytes 196616 | tf_op jit(solution)/shard_map/ppermute | solution.py:513
  88.8 7.6 %all-to-all-start.4 = ((bf16[8,12,16,128]{3,2,1,0:T(8,128)(2,1)}), bf16[8,12,16,128]{3,2,1,0:T(8,128)(2,1)S(1)}, u32[]{:S(2)}, u32[]{:S(2)}) async-start(bf16[8,12,16,128]{3,2,1,0:T(8,128)(2,1)} %choose_rows.3), calls=%async_computation.4 | async-start | bytes 786432 | tf_op jit(solution)/shard_map/all_to_all | solution.py:533
  96.4 5.5 %near_field.1 = (f32[16,32,64]{2,1,0:T(8,128)}, bf16[32,16,64]{2,1,0:T(8,128)(2,1)}) custom-call(s32[1]{0:T(128)} %bitcast.refs_0_, s32[1]{0:T(128)} %bitcast.1.refs_0_.refs_1_, s32[16,9]{1,0:T(8,128)} %refs_2_.3, bf16[16,32,256]{2,1,0:T(8,128)(2,1)} %get-tuple-element.79.refs_3_, bf16[4,32,256]{2,1,0:T(8,128)(2,1)} %copy-done.4, ...), custom_call_target="tpu_custom_call" | custom-call | tf_op jit(solution)/shard_map/near_field/pallas_call | solution.py:122
  101.9 3.4 %all-to-all-done.4 = bf16[8,12,16,128]{3,2,1,0:T(8,128)(2,1)S(1)} async-done(((bf16[8,12,16,128]{3,2,1,0:T(8,128)(2,1)}), bf16[8,12,16,128]{3,2,1,0:T(8,128)(2,1)S(1)}, u32[]{:S(2)}, u32[]{:S(2)}) %all-to-all-start.4) | async-done | bytes 393248 | tf_op jit(solution)/shard_map/all_to_all | solution.py:533
  105.3 2.1 %far_field.3.refs_1_ = bf16[4,16,128]{2,1,0:T(8,128)(2,1)S(1)} custom-call(s32[16,16]{1,0:T(8,128)} %get-tuple-element.51.refs_0_, s32[4,16]{1,0:T(4,128)} %get-tuple-element.52.refs_1_, bf16[96,16,128]{2,1,0:T(8,128)(2,1)S(1)} %bitcast.18, bf16[5,256,1024]{2,1,0:T(8,128)(2,1)S(1)} %join_couplings.1.refs_3_, bf16[4,256,64]{2,1,0:T(8,128)(2,1)S(1)} %bitcast.16), custom_call_target="tpu_custom_call" | custom-call | tf_op jit(solution)/shard_map/far_field/pallas_call | solution.py:122
  113.9 1.9 %output.1 = bf16[32,16,64]{2,1,0:T(8,128)(2,1)} custom-call(s32[1]{0:T(128)} %bitcast.refs_0_, bf16[4,16,128]{2,1,0:T(8,128)(2,1)S(1)} %far_field.3.refs_1_, bf16[4,16,128]{2,1,0:T(8,128)(2,1)S(1)} %collective-permute-done.16.refs_2_, bf16[4,16,128]{2,1,0:T(8,128)(2,1)S(1)} %collective-permute-done.17.refs_3_, ...), custom_call_target="tpu_custom_call" | custom-call | tf_op jit(solution)/shard_map/output/pallas_call | solution.py:122
  (49 shorter events, 25.5 us)
Async XLA Ops:
  2.5 8.5 %collective-permute-start = (bf16[336,128]{1,0:T(8,128)(2,1)S(1)}, bf16[336,128]{1,0:T(8,128)(2,1)S(1)}, u32[]{:S(2)}, u32[]{:S(2)}) collective-permute-start(bf16[336,128]{1,0:T(8,128)(2,1)S(1)} %get-tuple-element.54), channel_id=1, source_target_pairs={{0,1},{1,2},{2,3},{3,0},{4,5},{5,6},{6,7},{7,4},{8,9},{9,10},{10,1... | collective-permute-start | bytes 258056 | tf_op jit(solution)/shard_map/ppermute | solution.py:499
  4.0 6.9 %collective-permute-start.1 = (bf16[336,128]{1,0:T(8,128)(2,1)S(1)}, bf16[336,128]{1,0:T(8,128)(2,1)S(1)}, u32[]{:S(2)}, u32[]{:S(2)}) collective-permute-start(bf16[336,128]{1,0:T(8,128)(2,1)S(1)} %get-tuple-element.55), channel_id=1, source_target_pairs={{0,2},{1,3},{2,0},{3,1},{4,6},{5,7},{6,4},{7,5},{8,10},{9,11},{10,... | collective-permute-start | bytes 258056 | tf_op jit(solution)/shard_map/ppermute | solution.py:499
  6.8 4.5 %collective-permute-start.2 = (bf16[336,128]{1,0:T(8,128)(2,1)S(1)}, bf16[336,128]{1,0:T(8,128)(2,1)S(1)}, u32[]{:S(2)}, u32[]{:S(2)}) collective-permute-start(bf16[336,128]{1,0:T(8,128)(2,1)S(1)} %get-tuple-element.56), channel_id=1, source_target_pairs={{0,3},{1,0},{2,1},{3,2},{4,7},{5,4},{6,5},{7,6},{8,11},{9,8},{10,9... | collective-permute-start | bytes 258056 | tf_op jit(solution)/shard_map/ppermute | solution.py:499
  12.2 20.3 %all-to-all-start = ((bf16[8,5,16,128]{3,2,1,0:T(8,128)(2,1)}), bf16[8,5,16,128]{3,2,1,0:T(8,128)(2,1)S(1)}, u32[]{:S(2)}, u32[]{:S(2)}) async-start(bf16[8,5,16,128]{3,2,1,0:T(8,128)(2,1)} %get-tuple-element.62), calls=%async_computation | async-start | bytes 327680 | tf_op jit(solution)/shard_map/all_to_all | solution.py:522
  19.8 11.3 %collective-permute-start.5 = (bf16[512,128]{1,0:T(8,128)(2,1)}, bf16[512,128]{1,0:T(8,128)(2,1)S(1)}, u32[]{:S(2)}, u32[]{:S(2)}) collective-permute-start(bf16[512,128]{1,0:T(8,128)(2,1)} %get-tuple-element.73.refs_5_), channel_id=1, source_target_pairs={{0,3},{1,0},{2,1},{3,2},{4,7},{5,4},{6,5},{7,6},{8,11},{9,8},{10,9... | collective-permute-start | bytes 393224 | tf_op jit(solution)/shard_map/ppermute | solution.py:499
  22.5 8.7 %collective-permute-start.4 = (bf16[512,128]{1,0:T(8,128)(2,1)}, bf16[512,128]{1,0:T(8,128)(2,1)S(1)}, u32[]{:S(2)}, u32[]{:S(2)}) collective-permute-start(bf16[512,128]{1,0:T(8,128)(2,1)} %get-tuple-element.73.refs_5_), channel_id=1, source_target_pairs={{0,2},{1,3},{2,0},{3,1},{4,6},{5,7},{6,4},{7,5},{8,10},{9,11},{10,... | collective-permute-start | bytes 393224 | tf_op jit(solution)/shard_map/ppermute | solution.py:499
  22.8 9.6 %collective-permute-start.3 = (bf16[512,128]{1,0:T(8,128)(2,1)}, bf16[512,128]{1,0:T(8,128)(2,1)}, u32[]{:S(2)}, u32[]{:S(2)}) collective-permute-start(bf16[512,128]{1,0:T(8,128)(2,1)} %get-tuple-element.73.refs_5_), channel_id=1, source_target_pairs={{0,1},{1,2},{2,3},{3,0},{4,5},{5,6},{6,7},{7,4},{8,9},{9,10},{10,1... | collective-permute-start | bytes 393224 | tf_op jit(solution)/shard_map/ppermute | solution.py:499
  23.5 12.3 %collective-permute-start.6 = (bf16[4,32,256]{2,1,0:T(8,128)(2,1)S(1)}, bf16[4,32,256]{2,1,0:T(8,128)(2,1)S(1)}, u32[]{:S(2)}, u32[]{:S(2)}) collective-permute-start(bf16[4,32,256]{2,1,0:T(8,128)(2,1)S(1)} %get-tuple-element.68), channel_id=1, source_target_pairs={{0,4},{4,8},{8,12},{12,16},{16,20},{20,24},{24,28},{28,32},{32,36}... | collective-permute-start | bytes 196616 | tf_op jit(solution)/shard_map/ppermute | solution.py:512
  25.4 10.4 %collective-permute-start.7 = (bf16[4,32,256]{2,1,0:T(8,128)(2,1)S(1)}, bf16[4,32,256]{2,1,0:T(8,128)(2,1)S(1)}, u32[]{:S(2)}, u32[]{:S(2)}) collective-permute-start(bf16[4,32,256]{2,1,0:T(8,128)(2,1)S(1)} %get-tuple-element.69), channel_id=1, source_target_pairs={{4,0},{8,4},{12,8},{16,12},{20,16},{24,20},{28,24},{32,28},{36,32}... | collective-permute-start | bytes 196616 | tf_op jit(solution)/shard_map/ppermute | solution.py:513
  32.5 8.5 %all-to-all-start.1 = ((s32[8,1,128]{2,1,0:T(1,128)}), s32[8,1,128]{2,1,0:T(1,128)S(1)}, u32[]{:S(2)}, u32[]{:S(2)}) async-start(s32[8,1,128]{2,1,0:T(1,128)} %bitcast.5), calls=%async_computation.1 | async-start | bytes 8192 | tf_op jit(solution)/shard_map/all_to_all | solution.py:564
  42.5 13.6 %all-to-all-start.2 = ((bf16[8,12,16,128]{3,2,1,0:T(8,128)(2,1)}), bf16[8,12,16,128]{3,2,1,0:T(8,128)(2,1)S(1)}, u32[]{:S(2)}, u32[]{:S(2)}) async-start(bf16[8,12,16,128]{3,2,1,0:T(8,128)(2,1)} %choose_rows.2), calls=%async_computation.2 | async-start | bytes 786432 | tf_op jit(solution)/shard_map/all_to_all | solution.py:533
  47.2 15.7 %collective-permute-start.13 = (bf16[256,128]{1,0:T(8,128)(2,1)}, bf16[256,128]{1,0:T(8,128)(2,1)S(1)}, u32[]{:S(2)}, u32[]{:S(2)}) collective-permute-start(bf16[256,128]{1,0:T(8,128)(2,1)} %near_field_sent.1.refs_1_), channel_id=1, source_target_pairs={{0,3},{1,0},{2,1},{3,2},{4,7},{5,4},{6,5},{7,6},{8,11},{9,8},{10,9... | collective-permute-start | bytes 196616 | tf_op jit(solution)/shard_map/ppermute | solution.py:499
  49.8 13.1 %collective-permute-start.12 = (bf16[256,128]{1,0:T(8,128)(2,1)}, bf16[256,128]{1,0:T(8,128)(2,1)S(1)}, u32[]{:S(2)}, u32[]{:S(2)}) collective-permute-start(bf16[256,128]{1,0:T(8,128)(2,1)} %near_field_sent.1.refs_1_), channel_id=1, source_target_pairs={{0,2},{1,3},{2,0},{3,1},{4,6},{5,7},{6,4},{7,5},{8,10},{9,11},{10,... | collective-permute-start | bytes 196616 | tf_op jit(solution)/shard_map/ppermute | solution.py:499
  51.8 11.1 %collective-permute-start.11 = (bf16[256,128]{1,0:T(8,128)(2,1)}, bf16[256,128]{1,0:T(8,128)(2,1)S(1)}, u32[]{:S(2)}, u32[]{:S(2)}) collective-permute-start(bf16[256,128]{1,0:T(8,128)(2,1)} %near_field_sent.1.refs_1_), channel_id=1, source_target_pairs={{0,1},{1,2},{2,3},{3,0},{4,5},{5,6},{6,7},{7,4},{8,9},{9,10},{10,1... | collective-permute-start | bytes 196616 | tf_op jit(solution)/shard_map/ppermute | solution.py:499
  58.2 6.4 %collective-permute-start.10 = (bf16[4,16,128]{2,1,0:T(8,128)(2,1)S(1)}, bf16[4,16,128]{2,1,0:T(8,128)(2,1)S(1)}, u32[]{:S(2)}, u32[]{:S(2)}) collective-permute-start(bf16[4,16,128]{2,1,0:T(8,128)(2,1)S(1)} %far_field.2.refs_1_), channel_id=1, source_target_pairs={{0,3},{1,0},{2,1},{3,2},{4,7},{5,4},{6,5},{7,6},{8,11},{9,8},{10,9... | collective-permute-start | bytes 49160 | tf_op jit(solution)/shard_map/ppermute | solution.py:499
  60.9 5.2 %collective-permute-start.9 = (bf16[4,16,128]{2,1,0:T(8,128)(2,1)S(1)}, bf16[4,16,128]{2,1,0:T(8,128)(2,1)S(1)}, u32[]{:S(2)}, u32[]{:S(2)}) collective-permute-start(bf16[4,16,128]{2,1,0:T(8,128)(2,1)S(1)} %far_field.2.refs_1_), channel_id=1, source_target_pairs={{0,2},{1,3},{2,0},{3,1},{4,6},{5,7},{6,4},{7,5},{8,10},{9,11},{10,... | collective-permute-start | bytes 49160 | tf_op jit(solution)/shard_map/ppermute | solution.py:499
  62.9 5.0 %collective-permute-start.8 = (bf16[4,16,128]{2,1,0:T(8,128)(2,1)S(1)}, bf16[4,16,128]{2,1,0:T(8,128)(2,1)S(1)}, u32[]{:S(2)}, u32[]{:S(2)}) collective-permute-start(bf16[4,16,128]{2,1,0:T(8,128)(2,1)S(1)} %far_field.2.refs_1_), channel_id=1, source_target_pairs={{0,1},{1,2},{2,3},{3,0},{4,5},{5,6},{6,7},{7,4},{8,9},{9,10},{10,1... | collective-permute-start | bytes 49160 | tf_op jit(solution)/shard_map/ppermute | solution.py:499
  70.2 16.0 %all-to-all-start.3 = ((bf16[8,5,16,128]{3,2,1,0:T(8,128)(2,1)}), bf16[8,5,16,128]{3,2,1,0:T(8,128)(2,1)S(1)}, u32[]{:S(2)}, u32[]{:S(2)}) async-start(bf16[8,5,16,128]{3,2,1,0:T(8,128)(2,1)} %get-tuple-element.80), calls=%async_computation.3 | async-start | bytes 327680 | tf_op jit(solution)/shard_map/all_to_all | solution.py:522
  78.6 9.2 %collective-permute-start.14 = (bf16[4,32,256]{2,1,0:T(8,128)(2,1)S(1)}, bf16[4,32,256]{2,1,0:T(8,128)(2,1)S(1)}, u32[]{:S(2)}, u32[]{:S(2)}) collective-permute-start(bf16[4,32,256]{2,1,0:T(8,128)(2,1)S(1)} %get-tuple-element.81), channel_id=1, source_target_pairs={{0,4},{4,8},{8,12},{12,16},{16,20},{20,24},{24,28},{28,32},{32,36}... | collective-permute-start | bytes 196616 | tf_op jit(solution)/shard_map/ppermute | solution.py:512
  80.5 7.6 %collective-permute-start.15 = (bf16[4,32,256]{2,1,0:T(8,128)(2,1)S(1)}, bf16[4,32,256]{2,1,0:T(8,128)(2,1)S(1)}, u32[]{:S(2)}, u32[]{:S(2)}) collective-permute-start(bf16[4,32,256]{2,1,0:T(8,128)(2,1)S(1)} %get-tuple-element.82), channel_id=1, source_target_pairs={{4,0},{8,4},{12,8},{16,12},{20,16},{24,20},{28,24},{32,28},{36,32}... | collective-permute-start | bytes 196616 | tf_op jit(solution)/shard_map/ppermute | solution.py:513
  88.8 16.5 %all-to-all-start.4 = ((bf16[8,12,16,128]{3,2,1,0:T(8,128)(2,1)}), bf16[8,12,16,128]{3,2,1,0:T(8,128)(2,1)S(1)}, u32[]{:S(2)}, u32[]{:S(2)}) async-start(bf16[8,12,16,128]{3,2,1,0:T(8,128)(2,1)} %choose_rows.3), calls=%async_computation.4 | async-start | bytes 786432 | tf_op jit(solution)/shard_map/all_to_all | solution.py:533
  107.4 3.8 %collective-permute-start.18 = (bf16[4,16,128]{2,1,0:T(8,128)(2,1)S(1)}, bf16[4,16,128]{2,1,0:T(8,128)(2,1)S(1)}, u32[]{:S(2)}, u32[]{:S(2)}) collective-permute-start(bf16[4,16,128]{2,1,0:T(8,128)(2,1)S(1)} %far_field.3.refs_1_), channel_id=1, source_target_pairs={{0,3},{1,0},{2,1},{3,2},{4,7},{5,4},{6,5},{7,6},{8,11},{9,8},{10,9... | collective-permute-start | bytes 49160 | tf_op jit(solution)/shard_map/ppermute | solution.py:499
  107.5 5.2 %collective-permute-start.17 = (bf16[4,16,128]{2,1,0:T(8,128)(2,1)S(1)}, bf16[4,16,128]{2,1,0:T(8,128)(2,1)S(1)}, u32[]{:S(2)}, u32[]{:S(2)}) collective-permute-start(bf16[4,16,128]{2,1,0:T(8,128)(2,1)S(1)} %far_field.3.refs_1_), channel_id=1, source_target_pairs={{0,2},{1,3},{2,0},{3,1},{4,6},{5,7},{6,4},{7,5},{8,10},{9,11},{10,... | collective-permute-start | bytes 49160 | tf_op jit(solution)/shard_map/ppermute | solution.py:499
  108.5 5.4 %collective-permute-start.16 = (bf16[4,16,128]{2,1,0:T(8,128)(2,1)S(1)}, bf16[4,16,128]{2,1,0:T(8,128)(2,1)S(1)}, u32[]{:S(2)}, u32[]{:S(2)}) collective-permute-start(bf16[4,16,128]{2,1,0:T(8,128)(2,1)S(1)} %far_field.3.refs_1_), channel_id=1, source_target_pairs={{0,1},{1,2},{2,3},{3,0},{4,5},{5,6},{6,7},{7,4},{8,9},{9,10},{10,1... | collective-permute-start | bytes 49160 | tf_op jit(solution)/shard_map/ppermute | solution.py:499
  (6 other events, 33.7 us)

commit v8 on v6

--- a/solution.py
+++ b/solution.py
@@ -504,7 +504,7 @@
     def along(tiles):
         return lax.all_to_all(tiles, "leaf", 0, 0, axis_index_groups=along_z, tiled=True)
 
-    def within(column, asked):
+    def within(column, asked, edges=()):
         (chosen,) = call(
             choose_kernel,
             "choose_rows",
@@ -512,8 +512,9 @@
             of_kind("smem", asked) + of_kind("vmem", column),
             [pltpu.VMEM((PLANES * LEAVES, OWN, LANES), F32)],
         )
+        chosen, edges = lax.optimization_barrier((chosen, edges))
         got = lax.all_to_all(chosen, "leaf", 0, 0, axis_index_groups=in_plane, tiled=True)
-        return got.reshape((PLANE * OUT_TILES,) + tile)
+        return got.reshape((PLANE * OUT_TILES,) + tile), edges
 
     packed = call(
         partial_kernel,
@@ -551,7 +552,7 @@
         wide_scratch,
     )
     column, sent, later = lax.optimization_barrier((column, sent, sub))
-    got = within(column, asked)
+    got, _ = within(column, asked)
     (weights,) = call(
         weights_kernel,
         "join_couplings",
@@ -588,8 +589,7 @@
         + of_kind("vmem", near1, basis, four_transfers),
         [field_scratch, pltpu.VMEM((4, PROBES, UNKNOWNS), F32)],
     )
-    column, edges = lax.optimization_barrier((along(tiles), halos(low, high)))
-    got = within(column, asked)
+    got, edges = within(along(tiles), asked, halos(low, high))
     near2, first = call(
         near_kernel,
         "near_field",

time: 112 us -> 111 us (level)
  transfers between devices with their start and end apart: 21 -> 21, of which waited for: 10 -> 10; matrix products, arithmetic and copies ran while one was open for 0% -> 0% of each run, Pallas kernels for 18% -> 19%
where the time goes in v8:
time: 111 us; the launch traced here: 110 us
  starting transfers between devices  63.6 us (57%)
  Pallas kernels  31.7 us (29%)
  waiting for transfers between devices  13.1 us (12%)
    pallas_call x13, Pallas kernels, call(): pl.pallas_call(body, name=name, out_shape=[pltpu.HBM(out[0], out[1]) if l...  31.7 us
    ppermute x12, starting transfers between devices, over_sub(): lax.ppermute(pieces[k], 'sub', [(i, (i + k) % SUBS) for i in range(SUBS)])  16.4 us
    all_to_all x2, starting transfers between devices, along(): lax.all_to_all(tiles, 'leaf', 0, 0, axis_index_groups=along_z, tiled=True)  14.7 us
    all_to_all x2, starting transfers between devices, within(): lax.all_to_all(chosen, 'leaf', 0, 0, axis_index_groups=in_plane, tiled=True)  13.8 us
    ppermute x2, starting transfers between devices, halos(): lax.ppermute(low, 'leaf', [(i + 1, i) for i in range(groups - 1)])  11.5 us
    ppermute x12, waiting for transfers between devices, over_sub(): lax.ppermute(pieces[k], 'sub', [(i, (i + k) % SUBS) for i in range(SUBS)])  6.85 us
    all_to_all x2, waiting for transfers between devices, within(): lax.all_to_all(chosen, 'leaf', 0, 0, axis_index_groups=in_plane, tiled=True)  5.87 us
    ppermute x2, starting transfers between devices, halos(): lax.ppermute(high, 'leaf', [(i, i + 1) for i in range(groups - 1)])  3.82 us
  transfers between devices with their start and end apart: 21, of which 10 were waited for; matrix products, arithmetic and copies ran while one was open for 0% of the time, Pallas kernels for 19%

profile of v8, /device:TPU:96, one launch (start us, length us, event | category | flops | bytes accessed | tf_op | source)
XLA Modules:
  0.0 110.1 jit_solution(2964057928822140096)
XLA Ops:
  4.0 2.7 %collective-permute-start.1 = (bf16[336,128]{1,0:T(8,128)(2,1)S(1)}, bf16[336,128]{1,0:T(8,128)(2,1)S(1)}, u32[]{:S(2)}, u32[]{:S(2)}) collective-permute-start(bf16[336,128]{1,0:T(8,128)(2,1)S(1)} %get-tuple-element.50), channel_id=1, source_target_pairs={{0,2},{1,3},{2,0},{3,1},{4,6},{5,7},{6,4},{7,5},{8,10},{9,11},{10,... | collective-permute-start | bytes 258056 | tf_op jit(solution)/shard_map/ppermute | solution.py:482
  8.2 2.7 %index_tables.1 = (s32[8,128]{1,0:T(8,128)}, s32[16,16]{1,0:T(8,128)}, s32[4,16]{1,0:T(4,128)}) custom-call(s32[1]{0:T(128)} %bitcast.1.refs_0_.refs_1_, s32[16,16]{1,0:T(8,128)} %refs_1_.4, s32[4,16]{1,0:T(4,128)} %refs_2_.2), custom_call_target="tpu_custom_call" | custom-call | tf_op jit(solution)/shard_map/index_tables/pallas_call | solution.py:122
  12.1 7.7 %all-to-all-start = ((bf16[8,5,16,128]{3,2,1,0:T(8,128)(2,1)}), bf16[8,5,16,128]{3,2,1,0:T(8,128)(2,1)S(1)}, u32[]{:S(2)}, u32[]{:S(2)}) async-start(bf16[8,5,16,128]{3,2,1,0:T(8,128)(2,1)} %get-tuple-element.57), calls=%async_computation | async-start | bytes 327680 | tf_op jit(solution)/shard_map/all_to_all | solution.py:505
  19.8 1.9 %collective-permute-start.3 = (bf16[4,32,256]{2,1,0:T(8,128)(2,1)S(1)}, bf16[4,32,256]{2,1,0:T(8,128)(2,1)S(1)}, u32[]{:S(2)}, u32[]{:S(2)}) collective-permute-start(bf16[4,32,256]{2,1,0:T(8,128)(2,1)S(1)} %get-tuple-element.62), channel_id=1, source_target_pairs={{0,4},{4,8},{8,12},{12,16},{16,20},{20,24},{24,28},{28,32},{32,36}... | collective-permute-start | bytes 196616 | tf_op jit(solution)/shard_map/ppermute | solution.py:495
  21.7 5.8 %collective-permute-start.4 = (bf16[4,32,256]{2,1,0:T(8,128)(2,1)S(1)}, bf16[4,32,256]{2,1,0:T(8,128)(2,1)S(1)}, u32[]{:S(2)}, u32[]{:S(2)}) collective-permute-start(bf16[4,32,256]{2,1,0:T(8,128)(2,1)S(1)} %get-tuple-element.63), channel_id=1, source_target_pairs={{4,0},{8,4},{12,8},{16,12},{20,16},{24,20},{28,24},{32,28},{36,32}... | collective-permute-start | bytes 196616 | tf_op jit(solution)/shard_map/ppermute | solution.py:496
  27.5 3.3 %all-to-all-start.1 = ((s32[8,1,128]{2,1,0:T(1,128)}), s32[8,1,128]{2,1,0:T(1,128)S(1)}, u32[]{:S(2)}, u32[]{:S(2)}) async-start(s32[8,1,128]{2,1,0:T(1,128)} %bitcast.5), calls=%async_computation.1 | async-start | bytes 8192 | tf_op jit(solution)/shard_map/all_to_all | solution.py:546
  30.9 5.0 %near_field_sent.1.refs_1_ = bf16[768,128]{1,0:T(8,128)(2,1)} custom-call(s32[1]{0:T(128)} %bitcast.1.refs_0_.refs_1_, s32[16,9]{1,0:T(8,128)} %refs_2_.3, bf16[16,32,256]{2,1,0:T(8,128)(2,1)} %get-tuple-element.61.refs_2_, bf16[4,32,256]{2,1,0:T(8,128)(2,1)S(1)} %collective-permute-done.3.refs_3_, bf16[4,32,256]{2,1,0:T(8,128)(2,1)S(1)} %collective-permute-done.4.refs_4_, ...), custom_call_target="tpu_custom_call" | custom-call | tf_op jit(solution)/shard_map/near_field_sent/pallas_call | solution.py:122
  37.5 6.2 %all-to-all-start.2 = ((bf16[8,12,16,128]{3,2,1,0:T(8,128)(2,1)}), bf16[8,12,16,128]{3,2,1,0:T(8,128)(2,1)S(1)}, u32[]{:S(2)}, u32[]{:S(2)}) async-start(bf16[8,12,16,128]{3,2,1,0:T(8,128)(2,1)} %choose_rows.2), calls=%async_computation.2 | async-start | bytes 786432 | tf_op jit(solution)/shard_map/all_to_all | solution.py:516
  43.7 2.6 %collective-permute-start.10 = (bf16[768,128]{1,0:T(8,128)(2,1)}, bf16[768,128]{1,0:T(8,128)(2,1)S(1)}, u32[]{:S(2)}, u32[]{:S(2)}) collective-permute-start(bf16[768,128]{1,0:T(8,128)(2,1)} %near_field_sent.1.refs_1_), channel_id=1, source_target_pairs={{0,3},{1,0},{2,1},{3,2},{4,7},{5,4},{6,5},{7,6},{8,11},{9,8},{10,9... | collective-permute-start | bytes 589832 | tf_op jit(solution)/shard_map/ppermute | solution.py:482
  47.4 2.9 %join_couplings.1.refs_3_ = bf16[5,256,1024]{2,1,0:T(8,128)(2,1)S(1)} custom-call(s32[1]{0:T(128)} %bitcast.refs_0_, bf16[16384,64]{1,0:T(8,128)(2,1)} %bitcast.25, bf16[4096,64]{1,0:T(8,128)(2,1)} %bitcast.26), custom_call_target="tpu_custom_call" | custom-call | tf_op jit(solution)/shard_map/join_couplings/pallas_call | solution.py:122
  50.2 2.4 %all-to-all-done.2 = bf16[8,12,16,128]{3,2,1,0:T(8,128)(2,1)S(1)} async-done(((bf16[8,12,16,128]{3,2,1,0:T(8,128)(2,1)}), bf16[8,12,16,128]{3,2,1,0:T(8,128)(2,1)S(1)}, u32[]{:S(2)}, u32[]{:S(2)}) %all-to-all-start.2) | async-done | bytes 393248 | tf_op jit(solution)/shard_map/all_to_all | solution.py:516
  52.7 2.0 %far_field.2.refs_1_ = bf16[4,16,128]{2,1,0:T(8,128)(2,1)S(1)} custom-call(s32[16,16]{1,0:T(8,128)} %get-tuple-element.46.refs_0_, s32[4,16]{1,0:T(4,128)} %get-tuple-element.47.refs_1_, bf16[96,16,128]{2,1,0:T(8,128)(2,1)S(1)} %bitcast.19, bf16[5,256,1024]{2,1,0:T(8,128)(2,1)S(1)} %join_couplings.1.refs_3_, bf16[4,256,64]{2,1,0:T(8,128)(2,1)S(1)} %bitcast.14), custom_call_target="tpu_custom_call" | custom-call | tf_op jit(solution)/shard_map/far_field/pallas_call | solution.py:122
  54.7 2.7 %collective-permute-start.7 = (bf16[4,16,128]{2,1,0:T(8,128)(2,1)S(1)}, bf16[4,16,128]{2,1,0:T(8,128)(2,1)S(1)}, u32[]{:S(2)}, u32[]{:S(2)}) collective-permute-start(bf16[4,16,128]{2,1,0:T(8,128)(2,1)S(1)} %far_field.2.refs_1_), channel_id=1, source_target_pairs={{0,3},{1,0},{2,1},{3,2},{4,7},{5,4},{6,5},{7,6},{8,11},{9,8},{10,9... | collective-permute-start | bytes 49160 | tf_op jit(solution)/shard_map/ppermute | solution.py:482
  60.7 2.0 %collective-permute-done.6.refs_3_ = bf16[4,16,128]{2,1,0:T(8,128)(2,1)S(1)} collective-permute-done((bf16[4,16,128]{2,1,0:T(8,128)(2,1)S(1)}, bf16[4,16,128]{2,1,0:T(8,128)(2,1)S(1)}, u32[]{:S(2)}, u32[]{:S(2)}) %collective-permute-start.6) | collective-permute-done | bytes 16416 | tf_op jit(solution)/shard_map/ppermute | solution.py:482
  62.9 2.4 %second_coefficients.1 = (bf16[16,32,256]{2,1,0:T(8,128)(2,1)}, bf16[4,32,256]{2,1,0:T(8,128)(2,1)S(1)}, bf16[4,32,256]{2,1,0:T(8,128)(2,1)S(1)}, bf16[8,5,16,128]{3,2,1,0:T(8,128)(2,1)}) custom-call(s32[1]{0:T(128)} %bitcast.refs_0_, bf16[4,16,128]{2,1,0:T(8,128)(2,1)S(1)} %far_field.2.refs_1_, bf16[4,16,128]{2,1,0:T(8,128)(2,1)S(1)} %collective-permute-done.5.refs_2_, ...), custom_call_target="tpu_custom_call" | custom-call | tf_op jit(solution)/shard_map/second_coefficients/pallas_call | solution.py:122
  65.3 7.0 %all-to-all-start.3 = ((bf16[8,5,16,128]{3,2,1,0:T(8,128)(2,1)}), bf16[8,5,16,128]{3,2,1,0:T(8,128)(2,1)S(1)}, u32[]{:S(2)}, u32[]{:S(2)}) async-start(bf16[8,5,16,128]{3,2,1,0:T(8,128)(2,1)} %get-tuple-element.70), calls=%async_computation.3 | async-start | bytes 327680 | tf_op jit(solution)/shard_map/all_to_all | solution.py:505
  72.3 1.9 %collective-permute-start.11 = (bf16[4,32,256]{2,1,0:T(8,128)(2,1)S(1)}, bf16[4,32,256]{2,1,0:T(8,128)(2,1)S(1)}, u32[]{:S(2)}, u32[]{:S(2)}) collective-permute-start(bf16[4,32,256]{2,1,0:T(8,128)(2,1)S(1)} %get-tuple-element.71), channel_id=1, source_target_pairs={{0,4},{4,8},{8,12},{12,16},{16,20},{20,24},{24,28},{28,32},{32,36}... | collective-permute-start | bytes 196616 | tf_op jit(solution)/shard_map/ppermute | solution.py:495
  74.2 5.8 %collective-permute-start.12 = (bf16[4,32,256]{2,1,0:T(8,128)(2,1)S(1)}, bf16[4,32,256]{2,1,0:T(8,128)(2,1)S(1)}, u32[]{:S(2)}, u32[]{:S(2)}) collective-permute-start(bf16[4,32,256]{2,1,0:T(8,128)(2,1)S(1)} %get-tuple-element.72), channel_id=1, source_target_pairs={{4,0},{8,4},{12,8},{16,12},{20,16},{24,20},{28,24},{32,28},{36,32}... | collective-permute-start | bytes 196616 | tf_op jit(solution)/shard_map/ppermute | solution.py:496
  82.5 7.6 %all-to-all-start.4 = ((bf16[8,12,16,128]{3,2,1,0:T(8,128)(2,1)}), bf16[8,12,16,128]{3,2,1,0:T(8,128)(2,1)S(1)}, u32[]{:S(2)}, u32[]{:S(2)}) async-start(bf16[8,12,16,128]{3,2,1,0:T(8,128)(2,1)} %choose_rows.3), calls=%async_computation.4 | async-start | bytes 786432 | tf_op jit(solution)/shard_map/all_to_all | solution.py:516
  90.1 5.5 %near_field.1 = (f32[16,32,64]{2,1,0:T(8,128)}, bf16[32,16,64]{2,1,0:T(8,128)(2,1)}) custom-call(s32[1]{0:T(128)} %bitcast.refs_0_, s32[1]{0:T(128)} %bitcast.1.refs_0_.refs_1_, s32[16,9]{1,0:T(8,128)} %refs_2_.3, bf16[16,32,256]{2,1,0:T(8,128)(2,1)} %get-tuple-element.69.refs_3_, bf16[4,32,256]{2,1,0:T(8,128)(2,1)} %copy-done.2, ...), custom_call_target="tpu_custom_call" | custom-call | tf_op jit(solution)/shard_map/near_field/pallas_call | solution.py:122
  95.6 3.4 %all-to-all-done.4 = bf16[8,12,16,128]{3,2,1,0:T(8,128)(2,1)S(1)} async-done(((bf16[8,12,16,128]{3,2,1,0:T(8,128)(2,1)}), bf16[8,12,16,128]{3,2,1,0:T(8,128)(2,1)S(1)}, u32[]{:S(2)}, u32[]{:S(2)}) %all-to-all-start.4) | async-done | bytes 393248 | tf_op jit(solution)/shard_map/all_to_all | solution.py:516
  99.0 2.0 %far_field.3.refs_1_ = bf16[4,16,128]{2,1,0:T(8,128)(2,1)S(1)} custom-call(s32[16,16]{1,0:T(8,128)} %get-tuple-element.46.refs_0_, s32[4,16]{1,0:T(4,128)} %get-tuple-element.47.refs_1_, bf16[96,16,128]{2,1,0:T(8,128)(2,1)S(1)} %bitcast.20, bf16[5,256,1024]{2,1,0:T(8,128)(2,1)S(1)} %join_couplings.1.refs_3_, bf16[4,256,64]{2,1,0:T(8,128)(2,1)S(1)} %bitcast.16), custom_call_target="tpu_custom_call" | custom-call | tf_op jit(solution)/shard_map/far_field/pallas_call | solution.py:122
  104.9 2.1 %collective-permute-done.14.refs_3_ = bf16[4,16,128]{2,1,0:T(8,128)(2,1)S(1)} collective-permute-done((bf16[4,16,128]{2,1,0:T(8,128)(2,1)S(1)}, bf16[4,16,128]{2,1,0:T(8,128)(2,1)S(1)}, u32[]{:S(2)}, u32[]{:S(2)}) %collective-permute-start.14) | collective-permute-done | bytes 16416 | tf_op jit(solution)/shard_map/ppermute | solution.py:482
  108.1 1.9 %output.1 = bf16[32,16,64]{2,1,0:T(8,128)(2,1)} custom-call(s32[1]{0:T(128)} %bitcast.refs_0_, bf16[4,16,128]{2,1,0:T(8,128)(2,1)S(1)} %far_field.3.refs_1_, bf16[4,16,128]{2,1,0:T(8,128)(2,1)S(1)} %collective-permute-done.13.refs_2_, bf16[4,16,128]{2,1,0:T(8,128)(2,1)S(1)} %collective-permute-done.14.refs_3_, ...), custom_call_target="tpu_custom_call" | custom-call | tf_op jit(solution)/shard_map/output/pallas_call | solution.py:122
  (39 shorter events, 19.4 us)
Async XLA Ops:
  2.5 8.5 %collective-permute-start = (bf16[336,128]{1,0:T(8,128)(2,1)S(1)}, bf16[336,128]{1,0:T(8,128)(2,1)S(1)}, u32[]{:S(2)}, u32[]{:S(2)}) collective-permute-start(bf16[336,128]{1,0:T(8,128)(2,1)S(1)} %get-tuple-element.49), channel_id=1, source_target_pairs={{0,1},{1,2},{2,3},{3,0},{4,5},{5,6},{6,7},{7,4},{8,9},{9,10},{10,1... | collective-permute-start | bytes 258056 | tf_op jit(solution)/shard_map/ppermute | solution.py:482
  4.0 6.9 %collective-permute-start.1 = (bf16[336,128]{1,0:T(8,128)(2,1)S(1)}, bf16[336,128]{1,0:T(8,128)(2,1)S(1)}, u32[]{:S(2)}, u32[]{:S(2)}) collective-permute-start(bf16[336,128]{1,0:T(8,128)(2,1)S(1)} %get-tuple-element.50), channel_id=1, source_target_pairs={{0,2},{1,3},{2,0},{3,1},{4,6},{5,7},{6,4},{7,5},{8,10},{9,11},{10,... | collective-permute-start | bytes 258056 | tf_op jit(solution)/shard_map/ppermute | solution.py:482
  6.8 4.5 %collective-permute-start.2 = (bf16[336,128]{1,0:T(8,128)(2,1)S(1)}, bf16[336,128]{1,0:T(8,128)(2,1)S(1)}, u32[]{:S(2)}, u32[]{:S(2)}) collective-permute-start(bf16[336,128]{1,0:T(8,128)(2,1)S(1)} %get-tuple-element.51), channel_id=1, source_target_pairs={{0,3},{1,0},{2,1},{3,2},{4,7},{5,4},{6,5},{7,6},{8,11},{9,8},{10,9... | collective-permute-start | bytes 258056 | tf_op jit(solution)/shard_map/ppermute | solution.py:482
  12.1 15.4 %all-to-all-start = ((bf16[8,5,16,128]{3,2,1,0:T(8,128)(2,1)}), bf16[8,5,16,128]{3,2,1,0:T(8,128)(2,1)S(1)}, u32[]{:S(2)}, u32[]{:S(2)}) async-start(bf16[8,5,16,128]{3,2,1,0:T(8,128)(2,1)} %get-tuple-element.57), calls=%async_computation | async-start | bytes 327680 | tf_op jit(solution)/shard_map/all_to_all | solution.py:505
  19.8 11.0 %collective-permute-start.3 = (bf16[4,32,256]{2,1,0:T(8,128)(2,1)S(1)}, bf16[4,32,256]{2,1,0:T(8,128)(2,1)S(1)}, u32[]{:S(2)}, u32[]{:S(2)}) collective-permute-start(bf16[4,32,256]{2,1,0:T(8,128)(2,1)S(1)} %get-tuple-element.62), channel_id=1, source_target_pairs={{0,4},{4,8},{8,12},{12,16},{16,20},{20,24},{24,28},{28,32},{32,36}... | collective-permute-start | bytes 196616 | tf_op jit(solution)/shard_map/ppermute | solution.py:495
  21.7 9.1 %collective-permute-start.4 = (bf16[4,32,256]{2,1,0:T(8,128)(2,1)S(1)}, bf16[4,32,256]{2,1,0:T(8,128)(2,1)S(1)}, u32[]{:S(2)}, u32[]{:S(2)}) collective-permute-start(bf16[4,32,256]{2,1,0:T(8,128)(2,1)S(1)} %get-tuple-element.63), channel_id=1, source_target_pairs={{4,0},{8,4},{12,8},{16,12},{20,16},{24,20},{28,24},{32,28},{36,32}... | collective-permute-start | bytes 196616 | tf_op jit(solution)/shard_map/ppermute | solution.py:496
  27.5 8.4 %all-to-all-start.1 = ((s32[8,1,128]{2,1,0:T(1,128)}), s32[8,1,128]{2,1,0:T(1,128)S(1)}, u32[]{:S(2)}, u32[]{:S(2)}) async-start(s32[8,1,128]{2,1,0:T(1,128)} %bitcast.5), calls=%async_computation.1 | async-start | bytes 8192 | tf_op jit(solution)/shard_map/all_to_all | solution.py:546
  37.5 15.2 %copy-start = (bf16[16,64,64]{2,1,0:T(8,128)(2,1)S(1)}, bf16[16,64,64]{2,1,0:T(8,128)(2,1)}, u32[]{:S(2)}) copy-start(bf16[16,64,64]{2,1,0:T(8,128)(2,1)} %param.12) | copy-start | bytes 393220
  37.5 15.2 %all-to-all-start.2 = ((bf16[8,12,16,128]{3,2,1,0:T(8,128)(2,1)}), bf16[8,12,16,128]{3,2,1,0:T(8,128)(2,1)S(1)}, u32[]{:S(2)}, u32[]{:S(2)}) async-start(bf16[8,12,16,128]{3,2,1,0:T(8,128)(2,1)} %choose_rows.2), calls=%async_computation.2 | async-start | bytes 786432 | tf_op jit(solution)/shard_map/all_to_all | solution.py:516
  43.7 14.1 %collective-permute-start.10 = (bf16[768,128]{1,0:T(8,128)(2,1)}, bf16[768,128]{1,0:T(8,128)(2,1)S(1)}, u32[]{:S(2)}, u32[]{:S(2)}) collective-permute-start(bf16[768,128]{1,0:T(8,128)(2,1)} %near_field_sent.1.refs_1_), channel_id=1, source_target_pairs={{0,3},{1,0},{2,1},{3,2},{4,7},{5,4},{6,5},{7,6},{8,11},{9,8},{10,9... | collective-permute-start | bytes 589832 | tf_op jit(solution)/shard_map/ppermute | solution.py:482
  46.4 12.1 %collective-permute-start.9 = (bf16[768,128]{1,0:T(8,128)(2,1)}, bf16[768,128]{1,0:T(8,128)(2,1)}, u32[]{:S(2)}, u32[]{:S(2)}) collective-permute-start(bf16[768,128]{1,0:T(8,128)(2,1)} %near_field_sent.1.refs_1_), channel_id=1, source_target_pairs={{0,2},{1,3},{2,0},{3,1},{4,6},{5,7},{6,4},{7,5},{8,10},{9,11},{10,... | collective-permute-start | bytes 589832 | tf_op jit(solution)/shard_map/ppermute | solution.py:482
  46.7 12.5 %collective-permute-start.8 = (bf16[768,128]{1,0:T(8,128)(2,1)}, bf16[768,128]{1,0:T(8,128)(2,1)}, u32[]{:S(2)}, u32[]{:S(2)}) collective-permute-start(bf16[768,128]{1,0:T(8,128)(2,1)} %near_field_sent.1.refs_1_), channel_id=1, source_target_pairs={{0,1},{1,2},{2,3},{3,0},{4,5},{5,6},{6,7},{7,4},{8,9},{9,10},{10,1... | collective-permute-start | bytes 589832 | tf_op jit(solution)/shard_map/ppermute | solution.py:482
  54.7 6.0 %collective-permute-start.7 = (bf16[4,16,128]{2,1,0:T(8,128)(2,1)S(1)}, bf16[4,16,128]{2,1,0:T(8,128)(2,1)S(1)}, u32[]{:S(2)}, u32[]{:S(2)}) collective-permute-start(bf16[4,16,128]{2,1,0:T(8,128)(2,1)S(1)} %far_field.2.refs_1_), channel_id=1, source_target_pairs={{0,3},{1,0},{2,1},{3,2},{4,7},{5,4},{6,5},{7,6},{8,11},{9,8},{10,9... | collective-permute-start | bytes 49160 | tf_op jit(solution)/shard_map/ppermute | solution.py:482
  57.4 5.2 %collective-permute-start.6 = (bf16[4,16,128]{2,1,0:T(8,128)(2,1)S(1)}, bf16[4,16,128]{2,1,0:T(8,128)(2,1)S(1)}, u32[]{:S(2)}, u32[]{:S(2)}) collective-permute-start(bf16[4,16,128]{2,1,0:T(8,128)(2,1)S(1)} %far_field.2.refs_1_), channel_id=1, source_target_pairs={{0,2},{1,3},{2,0},{3,1},{4,6},{5,7},{6,4},{7,5},{8,10},{9,11},{10,... | collective-permute-start | bytes 49160 | tf_op jit(solution)/shard_map/ppermute | solution.py:482
  57.8 5.0 %collective-permute-start.5 = (bf16[4,16,128]{2,1,0:T(8,128)(2,1)S(1)}, bf16[4,16,128]{2,1,0:T(8,128)(2,1)S(1)}, u32[]{:S(2)}, u32[]{:S(2)}) collective-permute-start(bf16[4,16,128]{2,1,0:T(8,128)(2,1)S(1)} %far_field.2.refs_1_), channel_id=1, source_target_pairs={{0,1},{1,2},{2,3},{3,0},{4,5},{5,6},{6,7},{7,4},{8,9},{9,10},{10,1... | collective-permute-start | bytes 49160 | tf_op jit(solution)/shard_map/ppermute | solution.py:482
  65.3 14.7 %all-to-all-start.3 = ((bf16[8,5,16,128]{3,2,1,0:T(8,128)(2,1)}), bf16[8,5,16,128]{3,2,1,0:T(8,128)(2,1)S(1)}, u32[]{:S(2)}, u32[]{:S(2)}) async-start(bf16[8,5,16,128]{3,2,1,0:T(8,128)(2,1)} %get-tuple-element.70), calls=%async_computation.3 | async-start | bytes 327680 | tf_op jit(solution)/shard_map/all_to_all | solution.py:505
  72.3 9.2 %collective-permute-start.11 = (bf16[4,32,256]{2,1,0:T(8,128)(2,1)S(1)}, bf16[4,32,256]{2,1,0:T(8,128)(2,1)S(1)}, u32[]{:S(2)}, u32[]{:S(2)}) collective-permute-start(bf16[4,32,256]{2,1,0:T(8,128)(2,1)S(1)} %get-tuple-element.71), channel_id=1, source_target_pairs={{0,4},{4,8},{8,12},{12,16},{16,20},{20,24},{24,28},{28,32},{32,36}... | collective-permute-start | bytes 196616 | tf_op jit(solution)/shard_map/ppermute | solution.py:495
  74.2 7.6 %collective-permute-start.12 = (bf16[4,32,256]{2,1,0:T(8,128)(2,1)S(1)}, bf16[4,32,256]{2,1,0:T(8,128)(2,1)S(1)}, u32[]{:S(2)}, u32[]{:S(2)}) collective-permute-start(bf16[4,32,256]{2,1,0:T(8,128)(2,1)S(1)} %get-tuple-element.72), channel_id=1, source_target_pairs={{4,0},{8,4},{12,8},{16,12},{20,16},{24,20},{28,24},{32,28},{36,32}... | collective-permute-start | bytes 196616 | tf_op jit(solution)/shard_map/ppermute | solution.py:496
  81.5 0.6 copy-start.2
  82.5 16.5 %all-to-all-start.4 = ((bf16[8,12,16,128]{3,2,1,0:T(8,128)(2,1)}), bf16[8,12,16,128]{3,2,1,0:T(8,128)(2,1)S(1)}, u32[]{:S(2)}, u32[]{:S(2)}) async-start(bf16[8,12,16,128]{3,2,1,0:T(8,128)(2,1)} %choose_rows.3), calls=%async_computation.4 | async-start | bytes 786432 | tf_op jit(solution)/shard_map/all_to_all | solution.py:516
  90.1 18.0 %copy-start.1 = (bf16[16,64,64]{2,1,0:T(8,128)(2,1)S(1)}, bf16[16,64,64]{2,1,0:T(8,128)(2,1)}, u32[]{:S(2)}) copy-start(bf16[16,64,64]{2,1,0:T(8,128)(2,1)} %refs_6_.1) | copy-start | bytes 393220
  101.1 3.8 %collective-permute-start.15 = (bf16[4,16,128]{2,1,0:T(8,128)(2,1)S(1)}, bf16[4,16,128]{2,1,0:T(8,128)(2,1)S(1)}, u32[]{:S(2)}, u32[]{:S(2)}) collective-permute-start(bf16[4,16,128]{2,1,0:T(8,128)(2,1)S(1)} %far_field.3.refs_1_), channel_id=1, source_target_pairs={{0,3},{1,0},{2,1},{3,2},{4,7},{5,4},{6,5},{7,6},{8,11},{9,8},{10,9... | collective-permute-start | bytes 49160 | tf_op jit(solution)/shard_map/ppermute | solution.py:482
  101.7 5.3 %collective-permute-start.14 = (bf16[4,16,128]{2,1,0:T(8,128)(2,1)S(1)}, bf16[4,16,128]{2,1,0:T(8,128)(2,1)S(1)}, u32[]{:S(2)}, u32[]{:S(2)}) collective-permute-start(bf16[4,16,128]{2,1,0:T(8,128)(2,1)S(1)} %far_field.3.refs_1_), channel_id=1, source_target_pairs={{0,2},{1,3},{2,0},{3,1},{4,6},{5,7},{6,4},{7,5},{8,10},{9,11},{10,... | collective-permute-start | bytes 49160 | tf_op jit(solution)/shard_map/ppermute | solution.py:482
  103.1 4.9 %collective-permute-start.13 = (bf16[4,16,128]{2,1,0:T(8,128)(2,1)S(1)}, bf16[4,16,128]{2,1,0:T(8,128)(2,1)S(1)}, u32[]{:S(2)}, u32[]{:S(2)}) collective-permute-start(bf16[4,16,128]{2,1,0:T(8,128)(2,1)S(1)} %far_field.3.refs_1_), channel_id=1, source_target_pairs={{0,1},{1,2},{2,3},{3,0},{4,5},{5,6},{6,7},{7,4},{8,9},{9,10},{10,1... | collective-permute-start | bytes 49160 | tf_op jit(solution)/shard_map/ppermute | solution.py:482
  (1 other events, 0.6 us)
